TPU v7x, 512 devices: a whole 4x8x8 slice. The times are simulated.
512 devices in a mesh: rep: 4 (over z_lo), ctx: 128 (over y, x, z_hi, core).
Axes of the slice: x: 4, y: 8, z: 8 (z_hi: 2, z_lo: 4; z = z_hi * 4 + z_lo), core: 2. Of those that a mesh axis runs over, the one named last changes fastest.
Arguments:
- inputs: bfloat16 [4, 16384, 256], P('rep', 'ctx'), may hold values from -6 to 6
- out_grad: bfloat16 [4, 16384, 256], P('rep', 'ctx'), may hold values from -6 to 6
- out_gate: bfloat16 [4, 16384, 256], P('rep', 'ctx'), may hold values from -6 to 6
- filter_param: float32 [16384, 256], P('ctx'), may hold values from -6 to 6
- skip_gain: float32 [256], replicated, may hold values from -4 to 4
Outputs:
- input_grad: bfloat16 [4, 16384, 256], P('rep', 'ctx')
- filter_grad: float32 [16384, 256], P('ctx', 'rep')
All inputs are finite; a program needn't handle non-finite values.
Results may differ from a plain program's by a relative error of at most 0.001.
Values sent between devices are 32-bit elements; how exact they have to be, the bound alone decides.
No kernel may reach another device: no remote copies, remote signals or barrier semaphores. Data moves between devices by JAX's collectives and lax.ppermute only.
A program may use at most 64 MiB of HBM per device.

v0:
```python
import math

import jax
import jax.numpy as jnp
from jax import lax
from jax.sharding import PartitionSpec as P

highest = lax.Precision.HIGHEST


def local_transform(real_part, imag_part, sign):
    length = real_part.shape[1]
    columns = real_part.shape[2]
    counter = jnp.arange(length, dtype=jnp.int32)
    angles = (
        2.0 * math.pi / length * (counter[:, None] * counter[None, :] % length).astype(jnp.float32)
    )
    stacked = jnp.concatenate([real_part, imag_part], axis=2)
    cosine_sum = jnp.einsum("ki,jiw->jkw", jnp.cos(angles), stacked, precision=highest)
    sine_sum = jnp.einsum("ki,jiw->jkw", jnp.sin(angles), stacked, precision=highest)
    out_real = cosine_sum[:, :, :columns] - sign * sine_sum[:, :, columns:]
    out_imag = cosine_sum[:, :, columns:] + sign * sine_sum[:, :, :columns]
    return (out_real, out_imag)


def spectrum_forward(signal):
    members = lax.axis_size("ctx")
    length = signal.shape[0]
    columns = signal.shape[1]
    stride = length // members
    device = lax.axis_index("ctx")
    padded = 2 * members * length
    blocks = lax.all_to_all(
        signal.reshape(members, stride, columns), "ctx", split_axis=0, concat_axis=0, tiled=True
    )
    target = jnp.arange(2 * members, dtype=jnp.int32)
    source = jnp.arange(members, dtype=jnp.int32)
    angles = (
        2.0
        * math.pi
        / (2 * members)
        * (target[:, None] * source[None, :] % (2 * members)).astype(jnp.float32)
    )
    flattened = blocks.reshape(members, stride * columns)
    first_real = jnp.dot(jnp.cos(angles), flattened, precision=highest).reshape(
        2 * members, stride, columns
    )
    first_imag = -jnp.dot(jnp.sin(angles), flattened, precision=highest).reshape(
        2 * members, stride, columns
    )
    offsets = device * stride + jnp.arange(stride, dtype=jnp.int32)
    rotation = (
        -2.0 * math.pi / padded * (target[:, None] * offsets[None, :] % padded).astype(jnp.float32)
    )
    twist_real = jnp.cos(rotation)[:, :, None]
    twist_imag = jnp.sin(rotation)[:, :, None]
    turned_real = first_real * twist_real - first_imag * twist_imag
    turned_imag = first_real * twist_imag + first_imag * twist_real
    spread_real, spread_imag = (
        lax.all_to_all(turned_real, "ctx", split_axis=0, concat_axis=1, tiled=True),
        lax.all_to_all(turned_imag, "ctx", split_axis=0, concat_axis=1, tiled=True),
    )
    return local_transform(spread_real, spread_imag, -1.0)


def spectrum_inverse(real_part, imag_part):
    members = lax.axis_size("ctx")
    length = real_part.shape[1]
    columns = real_part.shape[2]
    stride = length // members
    device = lax.axis_index("ctx")
    padded = 2 * members * length
    back_real, back_imag = local_transform(real_part, imag_part, 1.0)
    target = 2 * device + jnp.arange(2, dtype=jnp.int32)
    offsets = jnp.arange(length, dtype=jnp.int32)
    rotation = (
        2.0 * math.pi / padded * (target[:, None] * offsets[None, :] % padded).astype(jnp.float32)
    )
    twist_real = jnp.cos(rotation)[:, :, None]
    twist_imag = jnp.sin(rotation)[:, :, None]
    turned_real = back_real * twist_real - back_imag * twist_imag
    turned_imag = back_real * twist_imag + back_imag * twist_real
    spread_real, spread_imag = (
        lax.all_to_all(turned_real, "ctx", split_axis=1, concat_axis=0, tiled=True),
        lax.all_to_all(turned_imag, "ctx", split_axis=1, concat_axis=0, tiled=True),
    )
    freqs = jnp.arange(2 * members, dtype=jnp.int32)
    source = jnp.arange(members, dtype=jnp.int32)
    angles = (
        2.0
        * math.pi
        / (2 * members)
        * (source[:, None] * freqs[None, :] % (2 * members)).astype(jnp.float32)
    )
    flat_real = spread_real.reshape(2 * members, stride * columns)
    flat_imag = spread_imag.reshape(2 * members, stride * columns)
    values = jnp.dot(jnp.cos(angles), flat_real, precision=highest) - jnp.dot(
        jnp.sin(angles), flat_imag, precision=highest
    )
    values = values * (1.0 / padded)
    returned = lax.all_to_all(
        values.reshape(members, stride, columns), "ctx", split_axis=0, concat_axis=1, tiled=True
    )
    return returned.reshape(length, columns)


def local(inputs, out_grad, out_gate, filter_param, skip_gain):
    signal = inputs[0].astype(jnp.float32)
    gated_grad = out_grad[0].astype(jnp.float32) * out_gate[0].astype(jnp.float32)
    members = lax.axis_size("ctx")
    length = signal.shape[0]
    channels = signal.shape[1]
    norm_scale = 1.0 / math.sqrt(members * length)
    filt = filter_param * norm_scale
    spec_real, spec_imag = spectrum_forward(jnp.concatenate([gated_grad, signal, filt], axis=1))
    filter_real = spec_real[:, :, 2 * channels :]
    filter_imag = spec_imag[:, :, 2 * channels :]
    gated_real = spec_real[:, :, :channels]
    gated_imag = spec_imag[:, :, :channels]
    input_real = spec_real[:, :, channels : 2 * channels]
    input_imag = spec_imag[:, :, channels : 2 * channels]
    back_real = gated_real * filter_real + gated_imag * filter_imag
    back_imag = gated_imag * filter_real - gated_real * filter_imag
    cross_real = gated_real * input_real + gated_imag * input_imag
    cross_imag = gated_imag * input_real - gated_real * input_imag
    restored = spectrum_inverse(
        jnp.concatenate([back_real, cross_real], axis=2),
        jnp.concatenate([back_imag, cross_imag], axis=2),
    )
    filter_part = lax.psum_scatter(restored[:, channels:], "rep", scatter_dimension=1, tiled=True)
    input_part = restored[:, :channels] + skip_gain[None, :] * gated_grad
    return (input_part.astype(jnp.bfloat16)[None], filter_part * norm_scale)


def solution(mesh):
    return jax.shard_map(
        local,
        mesh=mesh,
        in_specs=(
            P("rep", "ctx", None),
            P("rep", "ctx", None),
            P("rep", "ctx", None),
            P("ctx", None),
            P(),
        ),
        out_specs=(P("rep", "ctx", None), P("ctx", "rep")),
        check_vma=False,
    )
```

profile of v0, /device:TPU:1, one launch (start us, length us, event | category | flops | bytes accessed | tf_op | source)
XLA Modules:
  0.0 249.3 jit_solution(15134741077692145696)
XLA Ops:
  7.2 0.9 bitcast_convert_fusion
  8.0 0.9 broadcast_multiply_fusion
  8.9 0.9 multiply_bitcast_fusion
  9.9 1.0 reshape.140
  10.9 20.8 %all-to-all-start = ((f32[128,1,768]{2,1,0:T(1,128)}), f32[128,1,768]{2,1,0:T(1,128)S(1)}, u32[]{:S(2)}, u32[]{:S(2)}) async-start(f32[128,1,768]{2,1,0:T(1,128)} %reshape.140), calls=%async_computation | async-start | bytes 786432 | tf_op jit(solution)/shard_map/all_to_all | solution.py:33
  31.7 0.1 fusion.56
  31.8 20.0 %all-to-all-done = f32[128,1,768]{2,1,0:T(1,128)S(1)} async-done(((f32[128,1,768]{2,1,0:T(1,128)}), f32[128,1,768]{2,1,0:T(1,128)S(1)}, u32[]{:S(2)}, u32[]{:S(2)}) %all-to-all-start) | async-done | bytes 393248 | tf_op jit(solution)/shard_map/all_to_all | solution.py:33
  51.8 1.3 convolution_negate_fusion
  53.1 1.4 subtract_bitcast_fusion
  54.5 1.7 copy.21
  56.2 7.2 %all-to-all-start.1 = ((f32[256,1,768]{2,1,0:T(1,128)}), f32[256,1,768]{2,1,0:T(1,128)S(1)}, u32[]{:S(2)}, u32[]{:S(2)}) async-start(f32[256,1,768]{2,1,0:T(1,128)} %copy.21), calls=%async_computation.1 | async-start | bytes 1572864 | tf_op jit(solution)/shard_map/all_to_all | solution.py:60
  63.4 1.7 copy.23
  65.1 26.4 %all-to-all-done.1 = f32[256,1,768]{2,1,0:T(1,128)S(1)} async-done(((f32[256,1,768]{2,1,0:T(1,128)}), f32[256,1,768]{2,1,0:T(1,128)S(1)}, u32[]{:S(2)}, u32[]{:S(2)}) %all-to-all-start.1) | async-done | bytes 786464 | tf_op jit(solution)/shard_map/all_to_all | solution.py:60
  91.5 7.3 %all-to-all-start.2 = ((f32[256,1,768]{2,1,0:T(1,128)}), f32[256,1,768]{2,1,0:T(1,128)S(1)}, u32[]{:S(2)}, u32[]{:S(2)}) async-start(f32[256,1,768]{2,1,0:T(1,128)} %copy.23), calls=%async_computation.2 | async-start | bytes 1572864 | tf_op jit(solution)/shard_map/all_to_all | solution.py:61
  98.8 0.1 fusion.55
  99.0 0.7 copy.22
  99.7 27.2 %all-to-all-done.2 = f32[256,1,768]{2,1,0:T(1,128)S(1)} async-done(((f32[256,1,768]{2,1,0:T(1,128)}), f32[256,1,768]{2,1,0:T(1,128)S(1)}, u32[]{:S(2)}, u32[]{:S(2)}) %all-to-all-start.2) | async-done | bytes 786464 | tf_op jit(solution)/shard_map/all_to_all | solution.py:61
  126.9 0.7 copy.24
  127.6 1.7 convolution_bitcast_fusion.1
  129.3 1.7 convolution_bitcast_fusion
  131.0 0.2 fusion.3
  131.2 0.1 multiply_add_fusion.2
  131.3 1.2 convolution_bitcast_fusion.3
  132.5 1.2 convolution_bitcast_fusion.2
  133.8 0.2 multiply_add_fusion
  133.9 1.0 copy.25
  134.9 7.3 %all-to-all-start.3 = ((f32[2,128,512]{2,0,1:T(2,128)}), f32[2,128,512]{2,0,1:T(2,128)S(1)}, u32[]{:S(2)}, u32[]{:S(2)}) async-start(f32[2,128,512]{2,0,1:T(2,128)} %copy.25), calls=%async_computation.3 | async-start | bytes 1048576 | tf_op jit(solution)/shard_map/all_to_all | solution.py:84
  142.2 1.0 copy.26
  143.2 21.7 %all-to-all-done.3 = f32[2,128,512]{2,0,1:T(2,128)S(1)} async-done(((f32[2,128,512]{2,0,1:T(2,128)}), f32[2,128,512]{2,0,1:T(2,128)S(1)}, u32[]{:S(2)}, u32[]{:S(2)}) %all-to-all-start.3) | async-done | bytes 524320 | tf_op jit(solution)/shard_map/all_to_all | solution.py:84
  165.0 7.3 %all-to-all-start.4 = ((f32[2,128,512]{2,0,1:T(2,128)}), f32[2,128,512]{2,0,1:T(2,128)S(1)}, u32[]{:S(2)}, u32[]{:S(2)}) async-start(f32[2,128,512]{2,0,1:T(2,128)} %copy.26), calls=%async_computation.4 | async-start | bytes 1048576 | tf_op jit(solution)/shard_map/all_to_all | solution.py:85
  172.2 0.3 reduce-scatter.4.cloned.1.call-start
  172.5 0.4 reshape.142
  172.9 1.0 fusion.21
  173.8 21.1 %all-to-all-done.4 = f32[2,128,512]{2,0,1:T(2,128)S(1)} async-done(((f32[2,128,512]{2,0,1:T(2,128)}), f32[2,128,512]{2,0,1:T(2,128)S(1)}, u32[]{:S(2)}, u32[]{:S(2)}) %all-to-all-start.4) | async-done | bytes 524320 | tf_op jit(solution)/shard_map/all_to_all | solution.py:85
  195.0 0.4 reshape.143
  195.3 0.0 copy-start
  195.3 0.0 copy-start.1
  195.4 0.0 copy-start.2
  195.4 1.0 fusion.1
  196.3 0.3 copy.27
  196.6 24.2 %all_to_all.80 = f32[128,1,512]{2,1,0:T(1,128)S(1)} all-to-all(f32[128,1,512]{2,1,0:T(1,128)S(1)} %copy.27), channel_id=1, replica_groups=mesh['rep'=4,'ctx'=128] {'ctx'}, dimensions={0} | all-to-all | bytes 524288 | tf_op jit(solution)/shard_map/all_to_all | solution.py:101
  220.8 0.0 copy-done
  220.8 0.7 fusion.94
  221.5 0.7 copy.29
  222.2 0.0 reduce-scatter.4.cloned.1.call-update
  222.3 18.6 %reduce-scatter.4.cloned.1.call-done = f32[64,128]{1,0:T(8,128)} async-done(((f32[256,128]{1,0:T(8,128)}), f32[64,128]{1,0:T(8,128)}) %reduce-scatter.4.cloned.1.call-update) | async-done | bytes 32784
  240.9 0.8 copy.30
  241.7 0.7 copy.28
  (6 shorter events, 0.1 us)
Async XLA Ops:
  10.9 40.9 %all-to-all-start = ((f32[128,1,768]{2,1,0:T(1,128)}), f32[128,1,768]{2,1,0:T(1,128)S(1)}, u32[]{:S(2)}, u32[]{:S(2)}) async-start(f32[128,1,768]{2,1,0:T(1,128)} %reshape.140), calls=%async_computation | async-start | bytes 786432 | tf_op jit(solution)/shard_map/all_to_all | solution.py:33
  56.2 35.3 %all-to-all-start.1 = ((f32[256,1,768]{2,1,0:T(1,128)}), f32[256,1,768]{2,1,0:T(1,128)S(1)}, u32[]{:S(2)}, u32[]{:S(2)}) async-start(f32[256,1,768]{2,1,0:T(1,128)} %copy.21), calls=%async_computation.1 | async-start | bytes 1572864 | tf_op jit(solution)/shard_map/all_to_all | solution.py:60
  91.5 35.4 %all-to-all-start.2 = ((f32[256,1,768]{2,1,0:T(1,128)}), f32[256,1,768]{2,1,0:T(1,128)S(1)}, u32[]{:S(2)}, u32[]{:S(2)}) async-start(f32[256,1,768]{2,1,0:T(1,128)} %copy.23), calls=%async_computation.2 | async-start | bytes 1572864 | tf_op jit(solution)/shard_map/all_to_all | solution.py:61
  134.9 30.0 %all-to-all-start.3 = ((f32[2,128,512]{2,0,1:T(2,128)}), f32[2,128,512]{2,0,1:T(2,128)S(1)}, u32[]{:S(2)}, u32[]{:S(2)}) async-start(f32[2,128,512]{2,0,1:T(2,128)} %copy.25), calls=%async_computation.3 | async-start | bytes 1048576 | tf_op jit(solution)/shard_map/all_to_all | solution.py:84
  165.0 30.0 %all-to-all-start.4 = ((f32[2,128,512]{2,0,1:T(2,128)}), f32[2,128,512]{2,0,1:T(2,128)S(1)}, u32[]{:S(2)}, u32[]{:S(2)}) async-start(f32[2,128,512]{2,0,1:T(2,128)} %copy.26), calls=%async_computation.4 | async-start | bytes 1048576 | tf_op jit(solution)/shard_map/all_to_all | solution.py:85
  172.2 68.6 %reduce-scatter.4.cloned.1.call-start = ((), (), s32[]{:S(2)}) async-start(), calls=%async_computation.7 | async-start | bytes 163840
  195.3 25.5 %copy-start = (bf16[1,128,256]{2,1,0:T(8,128)(2,1)S(1)}, bf16[1,128,256]{2,1,0:T(8,128)(2,1)}, u32[]{:S(2)}) copy-start(bf16[1,128,256]{2,1,0:T(8,128)(2,1)} %param.7) | copy-start | bytes 196612
  195.3 25.5 %copy-start.1 = (bf16[1,128,256]{2,1,0:T(8,128)(2,1)S(1)}, bf16[1,128,256]{2,1,0:T(8,128)(2,1)}, u32[]{:S(2)}) copy-start(bf16[1,128,256]{2,1,0:T(8,128)(2,1)} %param.6) | copy-start | bytes 196612
  195.4 25.5 %copy-start.2 = (f32[256]{0:T(256)S(1)}, f32[256]{0:T(256)}, u32[]{:S(2)}) copy-start(f32[256]{0:T(256)} %param.9) | copy-start | bytes 3076
Sparse Core Ops, SparseCore 0:
  222.4 18.4 reduce-scatter.3
where the time goes:
time: 251 us; the launch traced here: 249 us
  waiting for transfers between devices  135 us (54%)
  starting transfers between devices  50.3 us (20%)
  blocking collectives  24.2 us (10%)
  between operations  14.3 us (6%)
  local copies, waits for them, and re-layouts  11.2 us (4%)
  matrix products  10.4 us (4%)
  other arithmetic  3.96 us (2%)
    all_to_all x1, waiting for transfers between devices, spectrum_forward(): lax.all_to_all(turned_imag, 'ctx', split_axis=0, concat_axis=1, tiled=True)  27.2 us
    all_to_all x1, waiting for transfers between devices, spectrum_forward(): lax.all_to_all(turned_real, 'ctx', split_axis=0, concat_axis=1, tiled=True)  26.4 us
    all_to_all x1, blocking collectives, spectrum_inverse(): lax.all_to_all(values.reshape(members, stride, columns), 'ctx', split_axi...  24.2 us
    all_to_all x1, waiting for transfers between devices, spectrum_inverse(): lax.all_to_all(turned_real, 'ctx', split_axis=1, concat_axis=0, tiled=True)  21.7 us
    all_to_all x1, waiting for transfers between devices, spectrum_inverse(): lax.all_to_all(turned_imag, 'ctx', split_axis=1, concat_axis=0, tiled=True)  21.1 us
    all_to_all x1, starting transfers between devices, spectrum_forward(): lax.all_to_all(signal.reshape(members, stride, columns), 'ctx', split_axi...  20.8 us
    all_to_all x1, waiting for transfers between devices, spectrum_forward(): lax.all_to_all(signal.reshape(members, stride, columns), 'ctx', split_axi...  20 us
    unnamed x2, waiting for transfers between devices  18.6 us
  transfers between devices with their start and end apart: 6, of which 6 were waited for; matrix products, arithmetic and copies ran while one was open for 2% of the time, Pallas kernels for 0%

commit v1 on v0

v1 whole, which is shorter than its diff:
```python
import math

import jax
import jax.numpy as jnp
import numpy as np
from jax import lax
from jax.experimental import pallas as pl
from jax.experimental.pallas import tpu as pltpu
from jax.sharding import PartitionSpec as P

highest = lax.Precision.HIGHEST


def tables(members, stride):
    padded = 2 * members * stride
    t1 = np.arange(members)
    t2 = np.arange(stride)
    odd = 2 * np.arange(members) + 1
    outer = 2.0 * np.pi / (4 * members) * (odd[:, None] * t1[None, :] % (4 * members))
    twist = 2.0 * np.pi / (2 * padded) * (odd[:, None] * t2[None, :] % (2 * padded))
    inner = 2.0 * np.pi / stride * (t2[:, None] * t2[None, :] % stride)
    first = np.concatenate([np.cos(outer), -np.sin(outer)], axis=0)
    second = np.block([[np.cos(inner), -np.sin(inner)], [np.sin(inner), np.cos(inner)]])
    scale = 2.0 / padded / math.sqrt(members * stride)
    return [
        np.asarray(table, np.float32)
        for table in (first, np.cos(twist), np.sin(twist), second, second.T, first.T * scale)
    ]


def pack_kernel(inputs_ref, grad_ref, gate_ref, filter_ref, out_ref):
    half = inputs_ref.shape[1] // 2
    gated = grad_ref[...].astype(jnp.float32) * gate_ref[...].astype(jnp.float32)
    signals = (gated, inputs_ref[...].astype(jnp.float32), filter_ref[...])
    for index, signal in enumerate(signals):
        for part in range(2):
            block = signal[:, part * half : (part + 1) * half]
            out_ref[pl.ds(2 * index + part, half, stride=6), :] = block.T


def spectra_kernel(
    signal_ref, first_ref, cos_ref, sin_ref, second_ref, back_ref, last_ref, out_ref
):
    stride = signal_ref.shape[1]
    members = signal_ref.shape[0] // 6
    signals = [signal_ref[pl.ds(row, members, stride=6), :] for row in range(6)]
    partial = jnp.dot(first_ref[...], jnp.concatenate(signals, axis=1), precision=highest)
    cosine = cos_ref[...]
    sine = sin_ref[...]
    turned = []
    for row in range(6):
        real = partial[:members, row * stride : (row + 1) * stride]
        imag = partial[members:, row * stride : (row + 1) * stride]
        turned.append(
            jnp.concatenate([real * cosine + imag * sine, imag * cosine - real * sine], axis=1)
        )
    spectrum = jnp.dot(jnp.concatenate(turned, axis=0), second_ref[...], precision=highest)
    parts = [spectrum[row * members : (row + 1) * members] for row in range(6)]
    products = []
    for one, other in ((0, 4), (1, 5), (0, 2), (1, 3)):
        real, imag = parts[one][:, :stride], parts[one][:, stride:]
        other_real, other_imag = parts[other][:, :stride], parts[other][:, stride:]
        products.append(
            jnp.concatenate(
                [real * other_real + imag * other_imag, imag * other_real - real * other_imag],
                axis=1,
            )
        )
    restored = jnp.dot(jnp.concatenate(products, axis=0), back_ref[...], precision=highest)
    columns = []
    for row in range(4):
        real = restored[row * members : (row + 1) * members, :stride]
        imag = restored[row * members : (row + 1) * members, stride:]
        columns.append(
            jnp.concatenate([real * cosine - imag * sine, imag * cosine + real * sine], axis=0)
        )
    values = jnp.dot(last_ref[...], jnp.concatenate(columns, axis=1), precision=highest)
    for row in range(4):
        out_ref[pl.ds(row, members, stride=4), :] = values[:, row * stride : (row + 1) * stride]


def pick_kernel(returned_ref, out_ref):
    members = returned_ref.shape[0] // 4
    for part in range(2):
        out_ref[part * members : (part + 1) * members, :] = returned_ref[
            pl.ds(2 + part, members, stride=4), :
        ]


def input_kernel(returned_ref, grad_ref, gate_ref, skip_ref, out_ref):
    members = returned_ref.shape[0] // 4
    gated = grad_ref[...].astype(jnp.float32) * gate_ref[...].astype(jnp.float32)
    skipped = gated * skip_ref[...]
    for part in range(2):
        columns = slice(part * members, (part + 1) * members)
        block = returned_ref[pl.ds(part, members, stride=4), :]
        out_ref[:, columns] = (block.T + skipped[:, columns]).astype(jnp.bfloat16)


def filter_kernel(pieces_ref, out_ref):
    count = out_ref.shape[1]
    total = pieces_ref[:count, :]
    for piece in range(1, pieces_ref.shape[0] // count):
        total = total + pieces_ref[piece * count : (piece + 1) * count, :]
    out_ref[...] = total.T


def local(inputs, out_grad, out_gate, filter_param, skip_gain):
    members = lax.axis_size("ctx")
    seqs = lax.axis_size("rep")
    stride, channels = filter_param.shape
    f32 = jnp.float32
    packed = pl.pallas_call(
        pack_kernel, out_shape=jax.ShapeDtypeStruct((members * 6, stride), f32)
    )(inputs[0], out_grad[0], out_gate[0], filter_param)
    spread = lax.all_to_all(packed, "ctx", split_axis=0, concat_axis=0, tiled=True)
    values = pl.pallas_call(
        spectra_kernel, out_shape=jax.ShapeDtypeStruct((members * 4, stride), f32)
    )(spread, *tables(members, stride))
    returned = lax.all_to_all(values, "ctx", split_axis=0, concat_axis=0, tiled=True)
    picked = pl.pallas_call(
        pick_kernel, out_shape=jax.ShapeDtypeStruct((channels, stride), f32)
    )(returned)
    pieces = lax.all_to_all(picked, "rep", split_axis=0, concat_axis=0, tiled=True)
    input_part = pl.pallas_call(
        input_kernel, out_shape=jax.ShapeDtypeStruct((stride, channels), jnp.bfloat16)
    )(returned, out_grad[0], out_gate[0], skip_gain[None, :])
    filter_part = pl.pallas_call(
        filter_kernel, out_shape=jax.ShapeDtypeStruct((stride, channels // seqs), f32)
    )(pieces)
    return (input_part[None], filter_part)


def solution(mesh):
    return jax.shard_map(
        local,
        mesh=mesh,
        in_specs=(
            P("rep", "ctx", None),
            P("rep", "ctx", None),
            P("rep", "ctx", None),
            P("ctx", None),
            P(),
        ),
        out_specs=(P("rep", "ctx", None), P("ctx", "rep")),
        check_vma=False,
    )
```

time: 251 us -> 94.9 us (0.38)
  waiting for transfers between devices: 135 us -> 3.05 us
  starting transfers between devices: 50.3 us -> 4.28 us
  blocking collectives: 24.2 us -> 69.1 us
  between operations: 14.3 us -> 0.64 us
  Pallas kernels: 0 us -> 12.4 us
  matrix products: 10.4 us -> 0 us
  local copies, waits for them, and re-layouts: 11.2 us -> 4.03 us
  other arithmetic: 3.96 us -> 0 us
    all_to_all x5 -> x1, waiting for transfers between devices: 116 us -> 3.05 us  [local(): lax.all_to_all(picked, 'rep', split_axis=0, concat_axis=0, tiled=True)]
    all_to_all x5 -> x1, starting transfers between devices: 50 us -> 4.28 us  [local(): lax.all_to_all(picked, 'rep', split_axis=0, concat_axis=0, tiled=True)]
    all_to_all x1 -> x2, blocking collectives: 24.2 us -> 69.1 us  [the longest x1 43.2 us: local(): lax.all_to_all(packed, 'ctx', split_axis=0, concat_axis=0, tiled=True)]
    unnamed x2 -> x0, waiting for transfers between devices: 18.6 us -> none
    pallas_call x0 -> x5, Pallas kernels: none -> 12.4 us  [the longest x1 5.44 us: local(): pl.pallas_call(spectra_kernel, out_shape=jax.ShapeDtypeStruct((members *...]
    dot_general x8 -> x0, matrix products: 10.4 us -> none  [the longest x2 2.92 us: local_transform(): jnp.einsum('ki,jiw->jkw', jnp.sin(angles), stacked, precision=highest)]
    sub x2 -> x0, local copies, waits for them, and re-layouts: 2.72 us -> none  [the longest x1 1.73 us: spectrum_forward(): turned_real = first_real * twist_real - first_imag * twist_imag]
    add x2 -> x0, local copies, waits for them, and re-layouts: 2.69 us -> none  [the longest x1 1.69 us: spectrum_forward(): turned_imag = first_real * twist_imag + first_imag * twist_real]
  transfers between devices with their start and end apart: 6 -> 1, of which waited for: 6 -> 1; matrix products, arithmetic and copies ran while one was open for 2% -> 0% of each run, Pallas kernels for 0% -> 2%
where the time goes in v1:
time: 94.9 us; the launch traced here: 93.4 us
  blocking collectives  69.1 us (73%)
  Pallas kernels  12.4 us (13%)
  starting transfers between devices  4.28 us (5%)
  local copies, waits for them, and re-layouts  4.03 us (4%)
  waiting for transfers between devices  3.05 us (3%)
    all_to_all x1, blocking collectives, local(): lax.all_to_all(packed, 'ctx', split_axis=0, concat_axis=0, tiled=True)  43.2 us
    all_to_all x1, blocking collectives, local(): lax.all_to_all(values, 'ctx', split_axis=0, concat_axis=0, tiled=True)  25.8 us
    pallas_call x1, Pallas kernels, local(): pl.pallas_call(spectra_kernel, out_shape=jax.ShapeDtypeStruct((members *...  5.44 us
    all_to_all x1, starting transfers between devices, local(): lax.all_to_all(picked, 'rep', split_axis=0, concat_axis=0, tiled=True)  4.28 us
    all_to_all x1, waiting for transfers between devices, local(): lax.all_to_all(picked, 'rep', split_axis=0, concat_axis=0, tiled=True)  3.05 us
    unnamed x3, local copies, waits for them, and re-layouts  2.18 us
    pallas_call x1, Pallas kernels, local(): pl.pallas_call(pack_kernel, out_shape=jax.ShapeDtypeStruct((members * 6,...  1.94 us
  transfers between devices with their start and end apart: 1, of which 1 were waited for; matrix products, arithmetic and copies ran while one was open for 0% of the time, Pallas kernels for 2%

profile of v1, /device:TPU:1, one launch (start us, length us, event | category | flops | bytes accessed | tf_op | source)
XLA Modules:
  0.0 93.4 jit_solution(12027633751862142984)
XLA Ops:
  0.6 1.9 %shard_map.122 = f32[768,128]{1,0:T(8,128)} custom-call(bf16[128,256]{1,0:T(8,128)(2,1)} %bitcast.19, bf16[128,256]{1,0:T(8,128)(2,1)} %bitcast.14, bf16[128,256]{1,0:T(8,128)(2,1)} %bitcast.16, f32[128,256]{1,0:T(8,128)} %filter_ref.1), custom_call_target="tpu_custom_call" | custom-call | tf_op jit(solution)/shard_map/pallas_call | solution.py:113
  2.6 1.0 %all_to_all.21 = f32[128,6,128]{2,1,0:T(8,128)S(1)} reshape(f32[768,128]{1,0:T(8,128)} %shard_map.122) | data formatting | bytes 786432 | tf_op jit(solution)/shard_map/all_to_all | solution.py:116
  3.6 43.2 %all_to_all.33 = f32[128,6,128]{2,1,0:T(8,128)S(1)} all-to-all(f32[128,6,128]{2,1,0:T(8,128)S(1)} %all_to_all.21), channel_id=1, replica_groups=mesh['rep'=4,'ctx'=128] {'ctx'}, dimensions={0} | all-to-all | bytes 786432 | tf_op jit(solution)/shard_map/all_to_all | solution.py:116
  46.9 0.8 all_to_all.23.signal_ref
  47.7 5.4 %shard_map.123 = f32[512,128]{1,0:T(8,128)} custom-call(f32[768,128]{1,0:T(8,128)} %all_to_all.23.signal_ref, f32[256,128]{1,0:T(8,128)} %constant.12.clone.first_ref, f32[128,128]{1,0:T(8,128)} %constant.13.clone.cos_ref, f32[128,128]{1,0:T(8,128)} %constant.14.clone.sin_ref, f32[256,256]{1,0:T(8,128)} %constant.15.clone.second_ref, ...), custom_call_target="tpu_custom_call" | custom-call | tf_op jit(solution)/shard_map/pallas_call | solution.py:117
  53.1 25.8 %all_to_all.34 = f32[128,4,128]{2,1,0:T(4,128)} all-to-all(f32[128,4,128]{2,1,0:T(4,128)} %bitcast.11), channel_id=1, replica_groups=mesh['rep'=4,'ctx'=128] {'ctx'}, dimensions={0} | all-to-all | bytes 524288 | tf_op jit(solution)/shard_map/all_to_all | solution.py:120
  78.9 1.6 %shard_map.125 = f32[256,128]{1,0:T(8,128)} custom-call(f32[512,128]{1,0:T(8,128)} %bitcast.9), custom_call_target="tpu_custom_call" | custom-call | tf_op jit(solution)/shard_map/pallas_call | solution.py:121
  80.6 4.3 %all-to-all-start.2 = ((f32[4,64,128]{2,1,0:T(8,128)}), f32[4,64,128]{2,1,0:T(8,128)S(1)}, u32[]{:S(2)}, u32[]{:S(2)}) async-start(f32[4,64,128]{2,1,0:T(8,128)} %bitcast.12), calls=%async_computation.2 | async-start | bytes 262144 | tf_op jit(solution)/shard_map/all_to_all | solution.py:124
  84.9 1.7 %shard_map.124 = bf16[128,256]{1,0:T(8,128)(2,1)} custom-call(f32[512,128]{1,0:T(8,128)} %bitcast.10, bf16[128,256]{1,0:T(8,128)(2,1)} %bitcast.15, bf16[128,256]{1,0:T(8,128)(2,1)} %bitcast.17, f32[1,256]{1,0:T(1,128)} %bitcast.20), custom_call_target="tpu_custom_call" | custom-call | tf_op jit(solution)/shard_map/pallas_call | solution.py:125
  86.6 3.0 %all-to-all-done.2 = f32[4,64,128]{2,1,0:T(8,128)S(1)} async-done(((f32[4,64,128]{2,1,0:T(8,128)}), f32[4,64,128]{2,1,0:T(8,128)S(1)}, u32[]{:S(2)}, u32[]{:S(2)}) %all-to-all-start.2) | async-done | bytes 131104 | tf_op jit(solution)/shard_map/all_to_all | solution.py:124
  89.6 0.0 copy-start
  89.6 0.6 copy-done
  90.3 1.6 %shard_map.126 = f32[128,64]{1,0:T(8,128)} custom-call(f32[256,128]{1,0:T(8,128)} %bitcast.13), custom_call_target="tpu_custom_call" | custom-call | tf_op jit(solution)/shard_map/pallas_call | solution.py:128
  91.9 1.5 %copy.14 = f32[128,64]{0,1:T(8,128)} copy(f32[128,64]{1,0:T(8,128)} %shard_map.126) | data formatting | bytes 65536
Async XLA Ops:
  80.6 9.1 %all-to-all-start.2 = ((f32[4,64,128]{2,1,0:T(8,128)}), f32[4,64,128]{2,1,0:T(8,128)S(1)}, u32[]{:S(2)}, u32[]{:S(2)}) async-start(f32[4,64,128]{2,1,0:T(8,128)} %bitcast.12), calls=%async_computation.2 | async-start | bytes 262144 | tf_op jit(solution)/shard_map/all_to_all | solution.py:124
  89.6 0.6 copy-start

commit v2 on v1

v2 whole, which is shorter than its diff:
```python
import math

import jax
import jax.numpy as jnp
import numpy as np
from jax import lax
from jax.experimental import pallas as pl
from jax.experimental.pallas import tpu as pltpu
from jax.sharding import PartitionSpec as P


def halves(values):
    high = values.astype(jnp.bfloat16)
    return high, (values - high.astype(jnp.float32)).astype(jnp.bfloat16)


def product(left, right):
    def dot(one, other):
        return jnp.dot(one, other, preferred_element_type=jnp.float32)

    total = dot(left[0], right[0])
    if right[1] is not None:
        total = total + dot(left[0], right[1])
    return total + dot(left[1], right[0])


def tables(members, stride):
    padded = 2 * members * stride
    t1 = np.arange(members)
    t2 = np.arange(stride)
    odd = 2 * np.arange(members) + 1
    outer = 2.0 * np.pi / (4 * members) * (odd[:, None] * t1[None, :] % (4 * members))
    twist = 2.0 * np.pi / (2 * padded) * (odd[:, None] * t2[None, :] % (2 * padded))
    inner = 2.0 * np.pi / stride * (t2[:, None] * t2[None, :] % stride)
    first = np.concatenate([np.cos(outer), -np.sin(outer)], axis=0)
    second = np.block([[np.cos(inner), -np.sin(inner)], [np.sin(inner), np.cos(inner)]])
    scale = 2.0 / padded / math.sqrt(members * stride)
    result = [np.asarray(np.cos(twist), np.float32), np.asarray(np.sin(twist), np.float32)]
    for table in (first, second, second.T, first.T * scale):
        high = table.astype(jnp.bfloat16)
        result += [high, (table - high.astype(np.float64)).astype(jnp.bfloat16)]
    return result


def pack_kernel(inputs_ref, grad_ref, gate_ref, filter_ref, out_ref):
    half = inputs_ref.shape[1] // 2
    gated = grad_ref[...].astype(jnp.float32) * gate_ref[...].astype(jnp.float32)
    signals = (gated, inputs_ref[...].astype(jnp.float32), filter_ref[...])
    for index, signal in enumerate(signals):
        for part in range(2):
            block = signal[:, part * half : (part + 1) * half]
            out_ref[pl.ds(2 * index + part, half, stride=6), :] = block.T


def spectra_kernel(signal_ref, cos_ref, sin_ref, *refs):
    first, second, back, last = [(refs[at][...], refs[at + 1][...]) for at in (0, 2, 4, 6)]
    out_ref = refs[8]
    stride = signal_ref.shape[1]
    members = signal_ref.shape[0] // 6
    signals = [signal_ref[pl.ds(row, members, stride=6), :] for row in range(6)]
    cosine = cos_ref[...]
    sine = sin_ref[...]
    partial = []
    for row in range(0, 6, 2):
        pair = jnp.concatenate(signals[row : row + 2], axis=1)
        sides = (pair.astype(jnp.bfloat16), None) if row == 2 else halves(pair)
        both = product(first, sides)
        partial += [both[:, :stride], both[:, stride:]]
    turned = []
    for value in partial:
        real, imag = value[:members], value[members:]
        turned.append(
            jnp.concatenate([real * cosine + imag * sine, imag * cosine - real * sine], axis=1)
        )
    parts = [product(halves(value), second) for value in turned]
    columns = []
    for one, other in ((0, 4), (1, 5), (0, 2), (1, 3)):
        real, imag = parts[one][:, :stride], parts[one][:, stride:]
        other_real, other_imag = parts[other][:, :stride], parts[other][:, stride:]
        value = jnp.concatenate(
            [real * other_real + imag * other_imag, imag * other_real - real * other_imag], axis=1
        )
        restored = product(halves(value), back)
        real, imag = restored[:, :stride], restored[:, stride:]
        columns.append(
            jnp.concatenate([real * cosine - imag * sine, imag * cosine + real * sine], axis=0)
        )
    for row in range(0, 4, 2):
        values = product(last, halves(jnp.concatenate(columns[row : row + 2], axis=1)))
        for part in range(2):
            out_ref[pl.ds(row + part, members, stride=4), :] = values[
                :, part * stride : (part + 1) * stride
            ]


def pick_kernel(returned_ref, out_ref):
    members = returned_ref.shape[0] // 4
    for part in range(2):
        out_ref[part * members : (part + 1) * members, :] = returned_ref[
            pl.ds(2 + part, members, stride=4), :
        ]


def input_kernel(returned_ref, grad_ref, gate_ref, skip_ref, out_ref):
    members = returned_ref.shape[0] // 4
    gated = grad_ref[...].astype(jnp.float32) * gate_ref[...].astype(jnp.float32)
    skipped = gated * skip_ref[...]
    for part in range(2):
        columns = slice(part * members, (part + 1) * members)
        block = returned_ref[pl.ds(part, members, stride=4), :]
        out_ref[:, columns] = (block.T + skipped[:, columns]).astype(jnp.bfloat16)


def filter_kernel(pieces_ref, out_ref):
    count = out_ref.shape[0]
    total = pieces_ref[:count, :]
    for piece in range(1, pieces_ref.shape[0] // count):
        total = total + pieces_ref[piece * count : (piece + 1) * count, :]
    out_ref[...] = total


def exchange(values, axis):
    rows, columns = values.shape
    pairs = values.reshape(rows // 2, 2, columns)
    pairs = lax.all_to_all(pairs, axis, split_axis=0, concat_axis=0, tiled=True)
    return pairs.reshape(rows, columns)


def local(inputs, out_grad, out_gate, filter_param, skip_gain):
    members = lax.axis_size("ctx")
    seqs = lax.axis_size("rep")
    stride, channels = filter_param.shape
    f32 = jnp.float32
    packed = pl.pallas_call(
        pack_kernel, out_shape=jax.ShapeDtypeStruct((members * 6, stride), f32)
    )(inputs[0], out_grad[0], out_gate[0], filter_param)
    spread = exchange(packed, "ctx")
    values = pl.pallas_call(
        spectra_kernel, out_shape=jax.ShapeDtypeStruct((members * 4, stride), f32)
    )(spread, *tables(members, stride))
    returned = exchange(values, "ctx")
    picked = pl.pallas_call(
        pick_kernel, out_shape=jax.ShapeDtypeStruct((channels, stride), f32)
    )(returned)
    pieces = exchange(picked, "rep")
    input_part = pl.pallas_call(
        input_kernel, out_shape=jax.ShapeDtypeStruct((stride, channels), jnp.bfloat16)
    )(returned, out_grad[0], out_gate[0], skip_gain[None, :])
    filter_part = pl.pallas_call(
        filter_kernel, out_shape=jax.ShapeDtypeStruct((channels // seqs, stride), f32)
    )(pieces)
    return (input_part[None], filter_part.T)


def solution(mesh):
    return jax.shard_map(
        local,
        mesh=mesh,
        in_specs=(
            P("rep", "ctx", None),
            P("rep", "ctx", None),
            P("rep", "ctx", None),
            P("ctx", None),
            P(),
        ),
        out_specs=(P("rep", "ctx", None), P("ctx", "rep")),
        check_vma=False,
    )
```

time: 94.9 us -> 86.9 us (0.916)
  local copies, waits for them, and re-layouts: 4.03 us -> 0.65 us
  blocking collectives: 69.1 us -> 66.6 us
  Pallas kernels: 12.4 us -> 10.3 us
    all_to_all x2, blocking collectives: 69.1 us -> 66.6 us  [exchange(): pairs = lax.all_to_all(pairs, axis, split_axis=0, concat_axis=0, tiled=True)]
    pallas_call x1, Pallas kernels: 5.44 us -> 3.45 us  [local(): pl.pallas_call(spectra_kernel, out_shape=jax.ShapeDtypeStruct((members *...]
    all_to_all x2 -> x0, local copies, waits for them, and re-layouts: 1.85 us -> none  [local(): lax.all_to_all(packed, 'ctx', split_axis=0, concat_axis=0, tiled=True)]
    unnamed x3 -> x2, local copies, waits for them, and re-layouts: 2.18 us -> 0.65 us
where the time goes in v2:
time: 86.9 us; the launch traced here: 85.5 us
  blocking collectives  66.6 us (77%)
  Pallas kernels  10.3 us (12%)
  starting transfers between devices  4.27 us (5%)
  waiting for transfers between devices  3.05 us (4%)
    all_to_all x2, blocking collectives, exchange(): pairs = lax.all_to_all(pairs, axis, split_axis=0, concat_axis=0, tiled=True)  66.6 us
    all_to_all x1, starting transfers between devices, exchange(): pairs = lax.all_to_all(pairs, axis, split_axis=0, concat_axis=0, tiled=True)  4.27 us
    pallas_call x1, Pallas kernels, local(): pl.pallas_call(spectra_kernel, out_shape=jax.ShapeDtypeStruct((members *...  3.45 us
    all_to_all x1, waiting for transfers between devices, exchange(): pairs = lax.all_to_all(pairs, axis, split_axis=0, concat_axis=0, tiled=True)  3.05 us
    pallas_call x1, Pallas kernels, local(): pl.pallas_call(pack_kernel, out_shape=jax.ShapeDtypeStruct((members * 6,...  1.93 us
  transfers between devices with their start and end apart: 1, of which 1 were waited for; matrix products, arithmetic and copies ran while one was open for 0% of the time, Pallas kernels for 2%

profile of v2, /device:TPU:1, one launch (start us, length us, event | category | flops | bytes accessed | tf_op | source)
XLA Modules:
  0.0 85.5 jit_solution(536491261065658885)
XLA Ops:
  0.6 1.9 %shard_map.158 = f32[768,128]{1,0:T(8,128)} custom-call(bf16[128,256]{1,0:T(8,128)(2,1)} %bitcast.24, bf16[128,256]{1,0:T(8,128)(2,1)} %bitcast.19, bf16[128,256]{1,0:T(8,128)(2,1)} %bitcast.21, f32[128,256]{1,0:T(8,128)} %filter_ref.1), custom_call_target="tpu_custom_call" | custom-call | tf_op jit(solution)/shard_map/pallas_call | solution.py:134
  2.6 41.0 %all_to_all.15 = f32[384,2,128]{2,1,0:T(2,128)} all-to-all(f32[384,2,128]{2,1,0:T(2,128)} %bitcast.15), channel_id=1, replica_groups=mesh['rep'=4,'ctx'=128] {'ctx'}, dimensions={0} | all-to-all | bytes 786432 | tf_op jit(solution)/shard_map/all_to_all | solution.py:125
  43.6 3.5 %shard_map.159 = f32[512,128]{1,0:T(8,128)} custom-call(f32[768,128]{1,0:T(8,128)} %bitcast.14, f32[128,128]{1,0:T(8,128)} %constant.20.clone.cos_ref, f32[128,128]{1,0:T(8,128)} %constant.21.clone.sin_ref, bf16[256,128]{1,0:T(8,128)(2,1)} %constant.22.clone.refs_0_, bf16[256,128]{1,0:T(8,128)(2,1)} %constant.23.clone.refs_1_, ...), custom_call_target="tpu_custom_call" | custom-call | tf_op jit(solution)/shard_map/pallas_call | solution.py:138
  47.0 25.6 %all_to_all.16 = f32[256,2,128]{2,1,0:T(2,128)} all-to-all(f32[256,2,128]{2,1,0:T(2,128)} %bitcast.16), channel_id=1, replica_groups=mesh['rep'=4,'ctx'=128] {'ctx'}, dimensions={0} | all-to-all | bytes 524288 | tf_op jit(solution)/shard_map/all_to_all | solution.py:125
  72.6 1.6 %shard_map.161 = f32[256,128]{1,0:T(8,128)} custom-call(f32[512,128]{1,0:T(8,128)} %bitcast.12), custom_call_target="tpu_custom_call" | custom-call | tf_op jit(solution)/shard_map/pallas_call | solution.py:142
  74.3 4.3 %all-to-all-start.2 = ((f32[128,2,128]{2,1,0:T(2,128)}), f32[128,2,128]{2,1,0:T(2,128)S(1)}, u32[]{:S(2)}, u32[]{:S(2)}) async-start(f32[128,2,128]{2,1,0:T(2,128)} %bitcast.17), calls=%async_computation.2 | async-start | bytes 262144 | tf_op jit(solution)/shard_map/all_to_all | solution.py:125
  78.5 1.7 %shard_map.160 = bf16[128,256]{1,0:T(8,128)(2,1)} custom-call(f32[512,128]{1,0:T(8,128)} %bitcast.13, bf16[128,256]{1,0:T(8,128)(2,1)} %bitcast.20, bf16[128,256]{1,0:T(8,128)(2,1)} %bitcast.22, f32[1,256]{1,0:T(1,128)} %bitcast.26), custom_call_target="tpu_custom_call" | custom-call | tf_op jit(solution)/shard_map/pallas_call | solution.py:146
  80.3 3.0 %all-to-all-done.2 = f32[128,2,128]{2,1,0:T(2,128)S(1)} async-done(((f32[128,2,128]{2,1,0:T(2,128)}), f32[128,2,128]{2,1,0:T(2,128)S(1)}, u32[]{:S(2)}, u32[]{:S(2)}) %all-to-all-start.2) | async-done | bytes 131104 | tf_op jit(solution)/shard_map/all_to_all | solution.py:125
  83.3 0.0 copy-start
  83.3 0.6 copy-done
  84.0 1.5 %shard_map.162 = f32[64,128]{1,0:T(8,128)} custom-call(f32[256,128]{1,0:T(8,128)} %bitcast.18), custom_call_target="tpu_custom_call" | custom-call | tf_op jit(solution)/shard_map/pallas_call | solution.py:149
Async XLA Ops:
  74.3 9.0 %all-to-all-start.2 = ((f32[128,2,128]{2,1,0:T(2,128)}), f32[128,2,128]{2,1,0:T(2,128)S(1)}, u32[]{:S(2)}, u32[]{:S(2)}) async-start(f32[128,2,128]{2,1,0:T(2,128)} %bitcast.17), calls=%async_computation.2 | async-start | bytes 262144 | tf_op jit(solution)/shard_map/all_to_all | solution.py:125
  83.3 0.6 copy-start

commit v3 on v2

--- a/solution.py
+++ b/solution.py
@@ -131,24 +131,26 @@
     seqs = lax.axis_size("rep")
     stride, channels = filter_param.shape
     f32 = jnp.float32
-    packed = pl.pallas_call(
-        pack_kernel, out_shape=jax.ShapeDtypeStruct((members * 6, stride), f32)
-    )(inputs[0], out_grad[0], out_gate[0], filter_param)
+    def near(values):
+        return pltpu.with_memory_space_constraint(values, pltpu.VMEM)
+
+    packed = pl.pallas_call(pack_kernel, out_shape=pltpu.VMEM((members * 6, stride), f32))(
+        inputs[0], out_grad[0], out_gate[0], filter_param
+    )
     spread = exchange(packed, "ctx")
-    values = pl.pallas_call(
-        spectra_kernel, out_shape=jax.ShapeDtypeStruct((members * 4, stride), f32)
-    )(spread, *tables(members, stride))
-    returned = exchange(values, "ctx")
-    picked = pl.pallas_call(
-        pick_kernel, out_shape=jax.ShapeDtypeStruct((channels, stride), f32)
-    )(returned)
+    constants = [near(jnp.asarray(table)) for table in tables(members, stride)]
+    values = pl.pallas_call(spectra_kernel, out_shape=pltpu.VMEM((members * 4, stride), f32))(
+        near(spread), *constants
+    )
+    returned = near(exchange(values, "ctx"))
+    picked = pl.pallas_call(pick_kernel, out_shape=pltpu.VMEM((channels, stride), f32))(returned)
     pieces = exchange(picked, "rep")
     input_part = pl.pallas_call(
         input_kernel, out_shape=jax.ShapeDtypeStruct((stride, channels), jnp.bfloat16)
-    )(returned, out_grad[0], out_gate[0], skip_gain[None, :])
+    )(returned, near(out_grad[0]), near(out_gate[0]), near(skip_gain[None, :]))
     filter_part = pl.pallas_call(
         filter_kernel, out_shape=jax.ShapeDtypeStruct((channels // seqs, stride), f32)
-    )(pieces)
+    )(near(pieces))
     return (input_part[None], filter_part.T)
 
 

time: 86.9 us -> 80.2 us (0.923)
  Pallas kernels: 10.3 us -> 4.61 us
  blocking collectives: 66.6 us -> 64.9 us
    pallas_call x3, Pallas kernels: 7.01 us -> 3.26 us  [the longest x1 1.4 us: local(): pl.pallas_call(spectra_kernel, out_shape=pltpu.VMEM((members * 4, stride)...]
    all_to_all x2, blocking collectives: 66.6 us -> 64.9 us  [exchange(): pairs = lax.all_to_all(pairs, axis, split_axis=0, concat_axis=0, tiled=True)]
    pallas_call x1, Pallas kernels: 1.72 us -> 0.73 us  [local(): pl.pallas_call(input_kernel, out_shape=jax.ShapeDtypeStruct((stride, chan...]
    pallas_call x1, Pallas kernels: 1.53 us -> 0.62 us  [local(): pl.pallas_call(filter_kernel, out_shape=jax.ShapeDtypeStruct((channels //...]
  transfers between devices with their start and end apart: 1 -> 1, of which waited for: 1 -> 1; matrix products, arithmetic and copies ran while one was open for 0% -> 0% of each run, Pallas kernels for 2% -> 1%
where the time goes in v3:
time: 80.2 us; the launch traced here: 78.8 us
  blocking collectives  64.9 us (81%)
  Pallas kernels  4.61 us (6%)
  starting transfers between devices  4.4 us (5%)
  waiting for transfers between devices  3.36 us (4%)
    all_to_all x2, blocking collectives, exchange(): pairs = lax.all_to_all(pairs, axis, split_axis=0, concat_axis=0, tiled=True)  64.9 us
    all_to_all x1, starting transfers between devices, exchange(): pairs = lax.all_to_all(pairs, axis, split_axis=0, concat_axis=0, tiled=True)  4.4 us
    all_to_all x1, waiting for transfers between devices, exchange(): pairs = lax.all_to_all(pairs, axis, split_axis=0, concat_axis=0, tiled=True)  3.36 us
  transfers between devices with their start and end apart: 1, of which 1 were waited for; matrix products, arithmetic and copies ran while one was open for 0% of the time, Pallas kernels for 1%

profile of v3, /device:TPU:1, one launch (start us, length us, event | category | flops | bytes accessed | tf_op | source)
XLA Modules:
  0.0 78.8 jit_solution(2292171698991362737)
XLA Ops:
  0.6 0.0 copy-start.10
  0.6 0.0 copy-start.11
  0.7 1.2 %shard_map.158 = f32[768,128]{1,0:T(8,128)S(1)} custom-call(bf16[128,256]{1,0:T(8,128)(2,1)} %bitcast.24, bf16[128,256]{1,0:T(8,128)(2,1)} %bitcast.18, bf16[128,256]{1,0:T(8,128)(2,1)} %bitcast.20, f32[128,256]{1,0:T(8,128)} %filter_ref.1), custom_call_target="tpu_custom_call" | custom-call | tf_op jit(solution)/shard_map/pallas_call | solution.py:137
  1.9 0.0 copy-start.2
  1.9 0.0 copy-start.3
  1.9 0.0 copy-start.4
  1.9 0.0 copy-start.5
  1.9 0.0 copy-start.6
  1.9 0.0 copy-start.7
  1.9 0.0 copy-start.8
  1.9 0.0 copy-start.9
  2.0 40.8 %all_to_all.15 = f32[384,2,128]{2,1,0:T(2,128)S(1)} all-to-all(f32[384,2,128]{2,1,0:T(2,128)S(1)} %bitcast.15), channel_id=1, replica_groups=mesh['rep'=4,'ctx'=128] {'ctx'}, dimensions={0} | all-to-all | bytes 786432 | tf_op jit(solution)/shard_map/all_to_all | solution.py:125
  42.8 0.0 copy-done.10
  42.8 0.0 copy-done.11
  42.8 0.0 copy-done.2
  42.8 0.0 copy-done.3
  42.8 0.0 copy-done.4
  42.8 0.0 copy-done.5
  42.8 0.0 copy-done.6
  42.8 0.0 copy-done.7
  42.9 0.0 copy-done.8
  42.9 0.0 copy-done.9
  42.9 1.4 %shard_map.159 = f32[512,128]{1,0:T(8,128)S(1)} custom-call(f32[768,128]{1,0:T(8,128)S(1)} %bitcast.14, f32[128,128]{1,0:T(8,128)S(1)} %copy-done.11, f32[128,128]{1,0:T(8,128)S(1)} %copy-done.10, bf16[256,128]{1,0:T(8,128)(2,1)S(1)} %copy-done.9, bf16[256,128]{1,0:T(8,128)(2,1)S(1)} %copy-done.8, bf16[256,256]{1,0:T(8,128)(2,1)S(1)} %copy-done.5, ...), custom_call_target="tpu_custom_call" | custom-call | tf_op jit(solution)/shard_map/pallas_call | solution.py:142
  44.3 24.1 %all_to_all.16 = f32[256,2,128]{2,1,0:T(2,128)S(1)} all-to-all(f32[256,2,128]{2,1,0:T(2,128)S(1)} %bitcast.16), channel_id=1, replica_groups=mesh['rep'=4,'ctx'=128] {'ctx'}, dimensions={0} | all-to-all | bytes 524288 | tf_op jit(solution)/shard_map/all_to_all | solution.py:125
  68.4 0.7 shard_map.161
  69.0 0.0 copy-start
  69.0 0.0 copy-start.1
  69.0 4.4 %all-to-all-start.2 = ((f32[128,2,128]{2,1,0:T(2,128)}), f32[128,2,128]{2,1,0:T(2,128)S(1)}, u32[]{:S(2)}, u32[]{:S(2)}) async-start(f32[128,2,128]{2,1,0:T(2,128)} %bitcast.9), calls=%async_computation.2 | async-start | bytes 262144 | tf_op jit(solution)/shard_map/all_to_all | solution.py:125
  73.4 0.0 copy-start.12
  73.4 0.0 copy-done
  73.4 0.0 copy-done.1
  73.4 0.7 copy-done.12
  74.1 0.7 shard_map.160
  74.8 3.4 %all-to-all-done.2 = f32[128,2,128]{2,1,0:T(2,128)S(1)} async-done(((f32[128,2,128]{2,1,0:T(2,128)}), f32[128,2,128]{2,1,0:T(2,128)S(1)}, u32[]{:S(2)}, u32[]{:S(2)}) %all-to-all-start.2) | async-done | bytes 131104 | tf_op jit(solution)/shard_map/all_to_all | solution.py:125
  78.2 0.6 shard_map.162
Async XLA Ops:
  0.6 42.2 %copy-start.10 = (f32[128,128]{1,0:T(8,128)S(1)}, f32[128,128]{1,0:T(8,128)}, u32[]{:S(2)}) copy-start(f32[128,128]{1,0:T(8,128)} %constant.21.clone.sin_ref) | copy-start | bytes 196612
  0.6 42.2 %copy-start.11 = (f32[128,128]{1,0:T(8,128)S(1)}, f32[128,128]{1,0:T(8,128)}, u32[]{:S(2)}) copy-start(f32[128,128]{1,0:T(8,128)} %constant.20.clone.cos_ref) | copy-start | bytes 196612
  1.9 40.9 %copy-start.2 = (bf16[256,256]{1,0:T(8,128)(2,1)S(1)}, bf16[256,256]{1,0:T(8,128)(2,1)}, u32[]{:S(2)}) copy-start(bf16[256,256]{1,0:T(8,128)(2,1)} %constant.27.clone.refs_5_) | copy-start | bytes 393220
  1.9 40.9 %copy-start.3 = (bf16[256,256]{1,0:T(8,128)(2,1)S(1)}, bf16[256,256]{1,0:T(8,128)(2,1)}, u32[]{:S(2)}) copy-start(bf16[256,256]{1,0:T(8,128)(2,1)} %constant.26.clone.refs_4_) | copy-start | bytes 393220
  1.9 40.9 %copy-start.4 = (bf16[256,256]{1,0:T(8,128)(2,1)S(1)}, bf16[256,256]{1,0:T(8,128)(2,1)}, u32[]{:S(2)}) copy-start(bf16[256,256]{1,0:T(8,128)(2,1)} %constant.25.clone.refs_3_) | copy-start | bytes 393220
  1.9 40.9 %copy-start.5 = (bf16[256,256]{1,0:T(8,128)(2,1)S(1)}, bf16[256,256]{1,0:T(8,128)(2,1)}, u32[]{:S(2)}) copy-start(bf16[256,256]{1,0:T(8,128)(2,1)} %constant.24.clone.refs_2_) | copy-start | bytes 393220
  1.9 40.9 %copy-start.6 = (bf16[128,256]{1,0:T(8,128)(2,1)S(1)}, bf16[128,256]{1,0:T(8,128)(2,1)}, u32[]{:S(2)}) copy-start(bf16[128,256]{1,0:T(8,128)(2,1)} %constant.29.clone.refs_7_) | copy-start | bytes 196612
  1.9 40.9 %copy-start.7 = (bf16[128,256]{1,0:T(8,128)(2,1)S(1)}, bf16[128,256]{1,0:T(8,128)(2,1)}, u32[]{:S(2)}) copy-start(bf16[128,256]{1,0:T(8,128)(2,1)} %constant.28.clone.refs_6_) | copy-start | bytes 196612
  1.9 40.9 %copy-start.8 = (bf16[256,128]{1,0:T(8,128)(2,1)S(1)}, bf16[256,128]{1,0:T(8,128)(2,1)}, u32[]{:S(2)}) copy-start(bf16[256,128]{1,0:T(8,128)(2,1)} %constant.23.clone.refs_1_) | copy-start | bytes 196612
  1.9 40.9 %copy-start.9 = (bf16[256,128]{1,0:T(8,128)(2,1)S(1)}, bf16[256,128]{1,0:T(8,128)(2,1)}, u32[]{:S(2)}) copy-start(bf16[256,128]{1,0:T(8,128)(2,1)} %constant.22.clone.refs_0_) | copy-start | bytes 196612
  69.0 4.4 %copy-start = (bf16[1,128,256]{2,1,0:T(8,128)(2,1)S(1)}, bf16[1,128,256]{2,1,0:T(8,128)(2,1)}, u32[]{:S(2)}) copy-start(bf16[1,128,256]{2,1,0:T(8,128)(2,1)} %param.16) | copy-start | bytes 196612
  69.0 4.4 %copy-start.1 = (bf16[1,128,256]{2,1,0:T(8,128)(2,1)S(1)}, bf16[1,128,256]{2,1,0:T(8,128)(2,1)}, u32[]{:S(2)}) copy-start(bf16[1,128,256]{2,1,0:T(8,128)(2,1)} %param.17) | copy-start | bytes 196612
  69.0 9.2 %all-to-all-start.2 = ((f32[128,2,128]{2,1,0:T(2,128)}), f32[128,2,128]{2,1,0:T(2,128)S(1)}, u32[]{:S(2)}, u32[]{:S(2)}) async-start(f32[128,2,128]{2,1,0:T(2,128)} %bitcast.9), calls=%async_computation.2 | async-start | bytes 262144 | tf_op jit(solution)/shard_map/all_to_all | solution.py:125
  73.4 0.7 copy-start.12

commit v4 on v3

--- a/solution.py
+++ b/solution.py
@@ -1,3 +1,4 @@
+import functools
 import math
 
 import jax
@@ -6,6 +7,7 @@
 from jax import lax
 from jax.experimental import pallas as pl
 from jax.experimental.pallas import tpu as pltpu
+from jax.sharding import Mesh
 from jax.sharding import PartitionSpec as P
 
 
@@ -42,14 +44,16 @@
     return result
 
 
-def pack_kernel(inputs_ref, grad_ref, gate_ref, filter_ref, out_ref):
-    half = inputs_ref.shape[1] // 2
+def pack_kernel(quarters, inputs_ref, grad_ref, gate_ref, filter_ref, out_ref):
     gated = grad_ref[...].astype(jnp.float32) * gate_ref[...].astype(jnp.float32)
     signals = (gated, inputs_ref[...].astype(jnp.float32), filter_ref[...])
+    run = filter_ref.shape[1] // (4 * quarters)
     for index, signal in enumerate(signals):
-        for part in range(2):
-            block = signal[:, part * half : (part + 1) * half]
-            out_ref[pl.ds(2 * index + part, half, stride=6), :] = block.T
+        turned = signal.T
+        for block in range(4 * quarters):
+            quarter, core, part = block // 4, block // 2 % 2, block % 2
+            row = 6 * (2 * run * quarter + core) + 2 * index + part
+            out_ref[pl.ds(row, run, stride=12), :] = turned[block * run : (block + 1) * run]
 
 
 def spectra_kernel(signal_ref, cos_ref, sin_ref, *refs):
@@ -93,78 +97,115 @@
             ]
 
 
-def pick_kernel(returned_ref, out_ref):
-    members = returned_ref.shape[0] // 4
+def pick_kernel(quarters, returned_ref, filter_ref, input_ref):
+    own = lax.axis_index("core") == 0
+    chips = returned_ref.shape[0] // 8
+    run = chips // quarters
+    for quarter in range(quarters):
+        for core in range(2):
+            for part in range(2):
+                row = (4 * quarter + 2 * core + part) * run
+                filter_ref[row : row + run, :] = returned_ref[
+                    pl.ds(8 * run * quarter + 4 * core + 2 + part, run, stride=8), :
+                ]
     for part in range(2):
-        out_ref[part * members : (part + 1) * members, :] = returned_ref[
-            pl.ds(2 + part, members, stride=4), :
-        ]
-
-
-def input_kernel(returned_ref, grad_ref, gate_ref, skip_ref, out_ref):
-    members = returned_ref.shape[0] // 4
+        input_ref[part * chips : (part + 1) * chips, :] = jnp.where(
+            own,
+            returned_ref[pl.ds(4 + part, chips, stride=8), :],
+            returned_ref[pl.ds(part, chips, stride=8), :],
+        )
+
+
+def input_kernel(quarters, returned_ref, other_ref, grad_ref, gate_ref, skip_ref, out_ref):
+    own = lax.axis_index("core") == 0
+    chips = returned_ref.shape[0] // 8
+    run = chips // quarters
+    mine = [
+        jnp.where(
+            own,
+            returned_ref[pl.ds(part, chips, stride=8), :],
+            returned_ref[pl.ds(4 + part, chips, stride=8), :],
+        )
+        for part in range(2)
+    ]
+    others = [other_ref[part * chips : (part + 1) * chips, :] for part in range(2)]
+    first = [jnp.where(own, one, other) for one, other in zip(mine, others)]
+    second = [jnp.where(own, other, one) for one, other in zip(mine, others)]
+    rows = []
+    for quarter in range(quarters):
+        for values in first + second:
+            rows.append(values[quarter * run : (quarter + 1) * run])
     gated = grad_ref[...].astype(jnp.float32) * gate_ref[...].astype(jnp.float32)
-    skipped = gated * skip_ref[...]
-    for part in range(2):
-        columns = slice(part * members, (part + 1) * members)
-        block = returned_ref[pl.ds(part, members, stride=4), :]
-        out_ref[:, columns] = (block.T + skipped[:, columns]).astype(jnp.bfloat16)
+    total = jnp.concatenate(rows, axis=0).T + gated * skip_ref[...]
+    out_ref[...] = total.astype(jnp.bfloat16)
 
 
 def filter_kernel(pieces_ref, out_ref):
     count = out_ref.shape[0]
     total = pieces_ref[:count, :]
-    for piece in range(1, pieces_ref.shape[0] // count):
-        total = total + pieces_ref[piece * count : (piece + 1) * count, :]
+    for start in range(count, pieces_ref.shape[0], count):
+        total = total + pieces_ref[start : start + count, :]
     out_ref[...] = total
 
 
 def exchange(values, axis):
     rows, columns = values.shape
-    pairs = values.reshape(rows // 2, 2, columns)
-    pairs = lax.all_to_all(pairs, axis, split_axis=0, concat_axis=0, tiled=True)
-    return pairs.reshape(rows, columns)
+    members = lax.axis_size(axis)
+    wide = values.reshape(members, 1, rows // members * columns)
+    wide = lax.all_to_all(wide, axis, split_axis=0, concat_axis=0, tiled=True)
+    return wide.reshape(rows, columns)
+
+
+def near(values):
+    return pltpu.with_memory_space_constraint(values, pltpu.VMEM)
 
 
 def local(inputs, out_grad, out_gate, filter_param, skip_gain):
-    members = lax.axis_size("ctx")
-    seqs = lax.axis_size("rep")
+    members = lax.axis_size(("chip", "core"))
+    quarters = lax.axis_size("rep")
     stride, channels = filter_param.shape
     f32 = jnp.float32
-    def near(values):
-        return pltpu.with_memory_space_constraint(values, pltpu.VMEM)
-
-    packed = pl.pallas_call(pack_kernel, out_shape=pltpu.VMEM((members * 6, stride), f32))(
-        inputs[0], out_grad[0], out_gate[0], filter_param
-    )
-    spread = exchange(packed, "ctx")
+    packed = pl.pallas_call(
+        functools.partial(pack_kernel, quarters), out_shape=pltpu.VMEM((members * 6, stride), f32)
+    )(inputs[0], out_grad[0], out_gate[0], filter_param)
+    spread = exchange(packed, ("chip", "core"))
     constants = [near(jnp.asarray(table)) for table in tables(members, stride)]
     values = pl.pallas_call(spectra_kernel, out_shape=pltpu.VMEM((members * 4, stride), f32))(
         near(spread), *constants
     )
-    returned = near(exchange(values, "ctx"))
-    picked = pl.pallas_call(pick_kernel, out_shape=pltpu.VMEM((channels, stride), f32))(returned)
-    pieces = exchange(picked, "rep")
+    returned = near(exchange(values, "chip"))
+    filter_picked, input_picked = pl.pallas_call(
+        functools.partial(pick_kernel, quarters),
+        out_shape=[pltpu.VMEM((channels, stride), f32), pltpu.VMEM((members, stride), f32)],
+    )(returned)
+    pieces = lax.all_to_all(
+        filter_picked, ("rep", "core"), split_axis=0, concat_axis=0, tiled=True
+    )
+    other = lax.ppermute(input_picked, "core", [(0, 1), (1, 0)])
     input_part = pl.pallas_call(
-        input_kernel, out_shape=jax.ShapeDtypeStruct((stride, channels), jnp.bfloat16)
-    )(returned, near(out_grad[0]), near(out_gate[0]), near(skip_gain[None, :]))
+        functools.partial(input_kernel, quarters),
+        out_shape=jax.ShapeDtypeStruct((stride, channels), jnp.bfloat16),
+    )(returned, near(other), near(out_grad[0]), near(out_gate[0]), near(skip_gain[None, :]))
     filter_part = pl.pallas_call(
-        filter_kernel, out_shape=jax.ShapeDtypeStruct((channels // seqs, stride), f32)
+        filter_kernel, out_shape=jax.ShapeDtypeStruct((channels // quarters, stride), f32)
     )(near(pieces))
     return (input_part[None], filter_part.T)
 
 
 def solution(mesh):
+    seqs, members = mesh.devices.shape
+    cores = Mesh(mesh.devices.reshape(seqs, members // 2, 2), ("rep", "chip", "core"))
+    ctx = ("chip", "core")
     return jax.shard_map(
         local,
-        mesh=mesh,
+        mesh=cores,
         in_specs=(
-            P("rep", "ctx", None),
-            P("rep", "ctx", None),
-            P("rep", "ctx", None),
-            P("ctx", None),
+            P("rep", ctx, None),
+            P("rep", ctx, None),
+            P("rep", ctx, None),
+            P(ctx, None),
             P(),
         ),
-        out_specs=(P("rep", "ctx", None), P("ctx", "rep")),
+        out_specs=(P("rep", ctx, None), P(ctx, "rep")),
         check_vma=False,
     )

time: 80.2 us -> 78.9 us (0.984); the launches traced: 78.8 us -> 78.5 us
  starting transfers between devices: 4.4 us -> 9.9 us
  blocking collectives: 64.9 us -> 60.1 us
    all_to_all x2, blocking collectives: 64.9 us -> 60.1 us  [exchange(): wide = lax.all_to_all(wide, axis, split_axis=0, concat_axis=0, tiled=True)]
    all_to_all x1, starting transfers between devices: 4.4 us -> 7.86 us  [local(): lax.all_to_all(filter_picked, ('rep', 'core'), split_axis=0, concat_axis=...]
    ppermute x0 -> x1, starting transfers between devices: none -> 2.04 us  [local(): other = lax.ppermute(input_picked, 'core', [(0, 1), (1, 0)])]
    all_to_all x1, waiting for transfers between devices: 3.36 us -> 1.79 us  [local(): lax.all_to_all(filter_picked, ('rep', 'core'), split_axis=0, concat_axis=...]
    ppermute x0 -> x1, waiting for transfers between devices: none -> 1.22 us  [local(): other = lax.ppermute(input_picked, 'core', [(0, 1), (1, 0)])]
  transfers between devices with their start and end apart: 1 -> 2, of which waited for: 1 -> 2; matrix products, arithmetic and copies ran while one was open for 0% -> 0% of each run, Pallas kernels for 1% -> 1%
where the time goes in v4:
time: 78.9 us; the launch traced here: 78.5 us
  blocking collectives  60.1 us (76%)
  starting transfers between devices  9.9 us (13%)
  Pallas kernels  4.67 us (6%)
  waiting for transfers between devices  3.01 us (4%)
  between operations  0.79 us (1%)
    all_to_all x2, blocking collectives, exchange(): wide = lax.all_to_all(wide, axis, split_axis=0, concat_axis=0, tiled=True)  60.1 us
    all_to_all x1, starting transfers between devices, local(): lax.all_to_all(filter_picked, ('rep', 'core'), split_axis=0, concat_axis=...  7.86 us
    ppermute x1, starting transfers between devices, local(): other = lax.ppermute(input_picked, 'core', [(0, 1), (1, 0)])  2.04 us
    all_to_all x1, waiting for transfers between devices, local(): lax.all_to_all(filter_picked, ('rep', 'core'), split_axis=0, concat_axis=...  1.79 us
  transfers between devices with their start and end apart: 2, of which 2 were waited for; matrix products, arithmetic and copies ran while one was open for 0% of the time, Pallas kernels for 1%

profile of v4, /device:TPU:1, one launch (start us, length us, event | category | flops | bytes accessed | tf_op | source)
XLA Modules:
  0.0 78.5 jit_solution(9912219469343700221)
XLA Ops:
  0.6 0.0 copy-start.10
  0.6 0.0 copy-start.11
  0.7 1.2 %shard_map.158 = f32[768,128]{1,0:T(8,128)S(1)} custom-call(bf16[128,256]{1,0:T(8,128)(2,1)} %bitcast.23, bf16[128,256]{1,0:T(8,128)(2,1)} %bitcast.18, bf16[128,256]{1,0:T(8,128)(2,1)} %bitcast.20, f32[128,256]{1,0:T(8,128)} %filter_ref.1), custom_call_target="tpu_custom_call" | custom-call | tf_op jit(solution)/shard_map/pallas_call | solution.py:168
  1.9 0.0 copy-start.2
  1.9 0.0 copy-start.3
  1.9 0.0 copy-start.4
  1.9 0.0 copy-start.5
  1.9 0.0 copy-start.6
  1.9 0.0 copy-start.7
  1.9 0.0 copy-start.8
  1.9 0.0 copy-start.9
  2.0 40.8 %all_to_all.21 = f32[128,1,768]{2,1,0:T(1,128)S(1)} all-to-all(f32[128,1,768]{2,1,0:T(1,128)S(1)} %bitcast.15), channel_id=1, replica_groups=mesh['rep'=4,'chip'=64,'core'=2] {'chip','core'}, dimensions={0} | all-to-all | bytes 786432 | tf_op jit(solution)/shard_map/all_to_all | solution.py:155
  42.8 0.0 copy-done.10
  42.8 0.0 copy-done.11
  42.8 0.0 copy-done.2
  42.8 0.0 copy-done.3
  42.8 0.0 copy-done.4
  42.8 0.0 copy-done.5
  42.8 0.0 copy-done.6
  42.8 0.0 copy-done.7
  42.9 0.0 copy-done.8
  42.9 0.0 copy-done.9
  42.9 1.4 %shard_map.159 = f32[512,128]{1,0:T(8,128)S(1)} custom-call(f32[768,128]{1,0:T(8,128)S(1)} %bitcast.14, f32[128,128]{1,0:T(8,128)S(1)} %copy-done.11, f32[128,128]{1,0:T(8,128)S(1)} %copy-done.10, bf16[256,128]{1,0:T(8,128)(2,1)S(1)} %copy-done.9, bf16[256,128]{1,0:T(8,128)(2,1)S(1)} %copy-done.8, bf16[256,256]{1,0:T(8,128)(2,1)S(1)} %copy-done.5, ...), custom_call_target="tpu_custom_call" | custom-call | tf_op jit(solution)/shard_map/pallas_call | solution.py:173
  44.3 19.3 %all_to_all.22 = f32[64,1,1024]{2,1,0:T(1,128)S(1)} all-to-all(f32[64,1,1024]{2,1,0:T(1,128)S(1)} %bitcast.16), channel_id=1, replica_groups=mesh['rep'=4,'chip'=64,'core'=2] {'chip'}, dimensions={0} | all-to-all | bytes 524288 | tf_op jit(solution)/shard_map/all_to_all | solution.py:155
  63.5 0.7 shard_map.160
  64.2 0.0 copy-start
  64.2 0.0 copy-start.1
  64.2 7.9 %all-to-all-start.2 = ((f32[8,32,128]{2,1,0:T(8,128)}), f32[8,32,128]{2,1,0:T(8,128)S(1)}, u32[]{:S(2)}, u32[]{:S(2)}) async-start(f32[8,32,128]{2,1,0:T(8,128)} %bitcast.9), calls=%async_computation.2 | async-start | bytes 262144 | tf_op jit(solution)/shard_map/all_to_all | solution.py:181
  72.1 0.0 copy-start.12
  72.1 2.0 %collective-permute-start = (f32[128,128]{1,0:T(8,128)S(1)}, f32[128,128]{1,0:T(8,128)S(1)}, u32[]{:S(2)}, u32[]{:S(2)}) collective-permute-start(f32[128,128]{1,0:T(8,128)S(1)} %get-tuple-element.4), channel_id=1, source_target_pairs={{0,1},{1,0},{2,3},{3,2},{4,5},{5,4},{6,7},{7,6},{8,9},{9,8},{10,11... | collective-permute-start | bytes 196616 | tf_op jit(solution)/shard_map/ppermute | solution.py:184
  74.2 1.2 %collective-permute-done.other_ref = f32[128,128]{1,0:T(8,128)S(1)} collective-permute-done((f32[128,128]{1,0:T(8,128)S(1)}, f32[128,128]{1,0:T(8,128)S(1)}, u32[]{:S(2)}, u32[]{:S(2)}) %collective-permute-start) | collective-permute-done | bytes 65568 | tf_op jit(solution)/shard_map/ppermute | solution.py:184
  75.4 0.0 copy-done
  75.4 0.0 copy-done.1
  75.4 0.0 copy-done.12
  75.4 0.7 shard_map.161
  76.1 1.8 %all-to-all-done.2 = f32[8,32,128]{2,1,0:T(8,128)S(1)} async-done(((f32[8,32,128]{2,1,0:T(8,128)}), f32[8,32,128]{2,1,0:T(8,128)S(1)}, u32[]{:S(2)}, u32[]{:S(2)}) %all-to-all-start.2) | async-done | bytes 131104 | tf_op jit(solution)/shard_map/all_to_all | solution.py:181
  77.9 0.6 shard_map.162
Async XLA Ops:
  0.6 42.2 %copy-start.10 = (f32[128,128]{1,0:T(8,128)S(1)}, f32[128,128]{1,0:T(8,128)}, u32[]{:S(2)}) copy-start(f32[128,128]{1,0:T(8,128)} %constant.21.clone.sin_ref) | copy-start | bytes 196612
  0.6 42.2 %copy-start.11 = (f32[128,128]{1,0:T(8,128)S(1)}, f32[128,128]{1,0:T(8,128)}, u32[]{:S(2)}) copy-start(f32[128,128]{1,0:T(8,128)} %constant.20.clone.cos_ref) | copy-start | bytes 196612
  1.9 40.9 %copy-start.2 = (bf16[256,256]{1,0:T(8,128)(2,1)S(1)}, bf16[256,256]{1,0:T(8,128)(2,1)}, u32[]{:S(2)}) copy-start(bf16[256,256]{1,0:T(8,128)(2,1)} %constant.27.clone.refs_5_) | copy-start | bytes 393220
  1.9 40.9 %copy-start.3 = (bf16[256,256]{1,0:T(8,128)(2,1)S(1)}, bf16[256,256]{1,0:T(8,128)(2,1)}, u32[]{:S(2)}) copy-start(bf16[256,256]{1,0:T(8,128)(2,1)} %constant.26.clone.refs_4_) | copy-start | bytes 393220
  1.9 40.9 %copy-start.4 = (bf16[256,256]{1,0:T(8,128)(2,1)S(1)}, bf16[256,256]{1,0:T(8,128)(2,1)}, u32[]{:S(2)}) copy-start(bf16[256,256]{1,0:T(8,128)(2,1)} %constant.25.clone.refs_3_) | copy-start | bytes 393220
  1.9 40.9 %copy-start.5 = (bf16[256,256]{1,0:T(8,128)(2,1)S(1)}, bf16[256,256]{1,0:T(8,128)(2,1)}, u32[]{:S(2)}) copy-start(bf16[256,256]{1,0:T(8,128)(2,1)} %constant.24.clone.refs_2_) | copy-start | bytes 393220
  1.9 40.9 %copy-start.6 = (bf16[128,256]{1,0:T(8,128)(2,1)S(1)}, bf16[128,256]{1,0:T(8,128)(2,1)}, u32[]{:S(2)}) copy-start(bf16[128,256]{1,0:T(8,128)(2,1)} %constant.29.clone.refs_7_) | copy-start | bytes 196612
  1.9 40.9 %copy-start.7 = (bf16[128,256]{1,0:T(8,128)(2,1)S(1)}, bf16[128,256]{1,0:T(8,128)(2,1)}, u32[]{:S(2)}) copy-start(bf16[128,256]{1,0:T(8,128)(2,1)} %constant.28.clone.refs_6_) | copy-start | bytes 196612
  1.9 40.9 %copy-start.8 = (bf16[256,128]{1,0:T(8,128)(2,1)S(1)}, bf16[256,128]{1,0:T(8,128)(2,1)}, u32[]{:S(2)}) copy-start(bf16[256,128]{1,0:T(8,128)(2,1)} %constant.23.clone.refs_1_) | copy-start | bytes 196612
  1.9 40.9 %copy-start.9 = (bf16[256,128]{1,0:T(8,128)(2,1)S(1)}, bf16[256,128]{1,0:T(8,128)(2,1)}, u32[]{:S(2)}) copy-start(bf16[256,128]{1,0:T(8,128)(2,1)} %constant.22.clone.refs_0_) | copy-start | bytes 196612
  64.2 11.1 %copy-start = (bf16[1,128,256]{2,1,0:T(8,128)(2,1)S(1)}, bf16[1,128,256]{2,1,0:T(8,128)(2,1)}, u32[]{:S(2)}) copy-start(bf16[1,128,256]{2,1,0:T(8,128)(2,1)} %param.16) | copy-start | bytes 196612
  64.2 11.1 %copy-start.1 = (bf16[1,128,256]{2,1,0:T(8,128)(2,1)S(1)}, bf16[1,128,256]{2,1,0:T(8,128)(2,1)}, u32[]{:S(2)}) copy-start(bf16[1,128,256]{2,1,0:T(8,128)(2,1)} %param.17) | copy-start | bytes 196612
  64.2 13.7 %all-to-all-start.2 = ((f32[8,32,128]{2,1,0:T(8,128)}), f32[8,32,128]{2,1,0:T(8,128)S(1)}, u32[]{:S(2)}, u32[]{:S(2)}) async-start(f32[8,32,128]{2,1,0:T(8,128)} %bitcast.9), calls=%async_computation.2 | async-start | bytes 262144 | tf_op jit(solution)/shard_map/all_to_all | solution.py:181
  72.1 3.3 %copy-start.12 = (f32[256]{0:T(256)S(1)}, f32[256]{0:T(256)}, u32[]{:S(2)}) copy-start(f32[256]{0:T(256)} %param.19) | copy-start | bytes 3076
  72.1 3.3 %collective-permute-start = (f32[128,128]{1,0:T(8,128)S(1)}, f32[128,128]{1,0:T(8,128)S(1)}, u32[]{:S(2)}, u32[]{:S(2)}) collective-permute-start(f32[128,128]{1,0:T(8,128)S(1)} %get-tuple-element.4), channel_id=1, source_target_pairs={{0,1},{1,0},{2,3},{3,2},{4,5},{5,4},{6,7},{7,6},{8,9},{9,8},{10,11... | collective-permute-start | bytes 196616 | tf_op jit(solution)/shard_map/ppermute | solution.py:184

commit v5 on v4

--- a/solution.py
+++ b/solution.py
@@ -44,16 +44,50 @@
     return result
 
 
+def signals_by_channel(inputs_ref, grad_ref, gate_ref, filter_ref):
+    gated = grad_ref[...].astype(jnp.float32) * gate_ref[...].astype(jnp.float32)
+    return [signal.T for signal in (gated, inputs_ref[...].astype(jnp.float32), filter_ref[...])]
+
+
+def hand_kernel(quarters, inputs_ref, grad_ref, gate_ref, filter_ref, out_ref):
+    first = lax.axis_index("core") == 0
+    run = filter_ref.shape[1] // (4 * quarters)
+    row = 0
+    for turned in signals_by_channel(inputs_ref, grad_ref, gate_ref, filter_ref):
+        for part in range(2):
+            for quarter in range(quarters):
+                start = (4 * quarter + part) * run
+                out_ref[row : row + run, :] = jnp.where(
+                    first,
+                    turned[start + 2 * run : start + 3 * run],
+                    turned[start : start + run],
+                )
+                row += run
+
+
 def pack_kernel(quarters, inputs_ref, grad_ref, gate_ref, filter_ref, out_ref):
-    gated = grad_ref[...].astype(jnp.float32) * gate_ref[...].astype(jnp.float32)
-    signals = (gated, inputs_ref[...].astype(jnp.float32), filter_ref[...])
+    core = lax.axis_index("core")
     run = filter_ref.shape[1] // (4 * quarters)
-    for index, signal in enumerate(signals):
-        turned = signal.T
-        for block in range(4 * quarters):
-            quarter, core, part = block // 4, block // 2 % 2, block % 2
-            row = 6 * (2 * run * quarter + core) + 2 * index + part
-            out_ref[pl.ds(row, run, stride=12), :] = turned[block * run : (block + 1) * run]
+    signals = signals_by_channel(inputs_ref, grad_ref, gate_ref, filter_ref)
+    for index, turned in enumerate(signals):
+        for part in range(2):
+            for quarter in range(quarters):
+                start = (4 * quarter + part) * run
+                row = 12 * run * quarter + 2 * index + part
+                out_ref[pl.ds(row + 6 * core, run, stride=12), :] = jnp.where(
+                    core == 0,
+                    turned[start : start + run],
+                    turned[start + 2 * run : start + 3 * run],
+                )
+
+
+def merge_kernel(handed_ref, packed_ref, out_ref):
+    core = lax.axis_index("core")
+    chips = handed_ref.shape[0] // 6
+    for row in range(6):
+        out_ref[pl.ds(row + 6 * (1 - core), chips, stride=12), :] = handed_ref[
+            row * chips : (row + 1) * chips, :
+        ]
 
 
 def spectra_kernel(signal_ref, cos_ref, sin_ref, *refs):
@@ -165,10 +199,20 @@
     quarters = lax.axis_size("rep")
     stride, channels = filter_param.shape
     f32 = jnp.float32
+    sources = (inputs[0], out_grad[0], out_gate[0], filter_param)
+    handed = pl.pallas_call(
+        functools.partial(hand_kernel, quarters), out_shape=pltpu.VMEM((members * 3, stride), f32)
+    )(*sources)
+    handed = lax.ppermute(handed, "core", [(0, 1), (1, 0)])
     packed = pl.pallas_call(
         functools.partial(pack_kernel, quarters), out_shape=pltpu.VMEM((members * 6, stride), f32)
-    )(inputs[0], out_grad[0], out_gate[0], filter_param)
-    spread = exchange(packed, ("chip", "core"))
+    )(*sources)
+    merged = pl.pallas_call(
+        merge_kernel,
+        out_shape=pltpu.VMEM((members * 6, stride), f32),
+        input_output_aliases={1: 0},
+    )(near(handed), near(packed))
+    spread = exchange(merged, "chip")
     constants = [near(jnp.asarray(table)) for table in tables(members, stride)]
     values = pl.pallas_call(spectra_kernel, out_shape=pltpu.VMEM((members * 4, stride), f32))(
         near(spread), *constants

time: 78.9 us -> 80.8 us (1.024)
  starting transfers between devices: 9.9 us -> 18.7 us
  blocking collectives: 60.1 us -> 52 us
  Pallas kernels: 4.67 us -> 5.83 us
    ppermute x0 -> x1, starting transfers between devices: none -> 8.79 us  [local(): handed = lax.ppermute(handed, 'core', [(0, 1), (1, 0)])]
    all_to_all x2, blocking collectives: 60.1 us -> 52 us  [exchange(): wide = lax.all_to_all(wide, axis, split_axis=0, concat_axis=0, tiled=True)]
    pallas_call x0 -> x2, Pallas kernels: none -> 1.19 us  [the longest x1 1.17 us: local(): pl.pallas_call(functools.partial(hand_kernel, quarters), out_shape=pltpu....]
  transfers between devices with their start and end apart: 2 -> 3, of which waited for: 2 -> 2; matrix products, arithmetic and copies ran while one was open for 0% -> 0% of each run, Pallas kernels for 1% -> 2%
where the time goes in v5:
time: 80.8 us; the launch traced here: 80.4 us
  blocking collectives  52 us (64%)
  starting transfers between devices  18.7 us (23%)
  Pallas kernels  5.83 us (7%)
  waiting for transfers between devices  3.01 us (4%)
  between operations  0.83 us (1%)
    all_to_all x2, blocking collectives, exchange(): wide = lax.all_to_all(wide, axis, split_axis=0, concat_axis=0, tiled=True)  52 us
    ppermute x1, starting transfers between devices, local(): handed = lax.ppermute(handed, 'core', [(0, 1), (1, 0)])  8.79 us
    all_to_all x1, starting transfers between devices, local(): lax.all_to_all(filter_picked, ('rep', 'core'), split_axis=0, concat_axis=...  7.92 us
    ppermute x1, starting transfers between devices, local(): other = lax.ppermute(input_picked, 'core', [(0, 1), (1, 0)])  2.04 us
    all_to_all x1, waiting for transfers between devices, local(): lax.all_to_all(filter_picked, ('rep', 'core'), split_axis=0, concat_axis=...  1.79 us
  transfers between devices with their start and end apart: 3, of which 2 were waited for; matrix products, arithmetic and copies ran while one was open for 0% of the time, Pallas kernels for 2%

profile of v5, /device:TPU:1, one launch (start us, length us, event | category | flops | bytes accessed | tf_op | source)
XLA Modules:
  0.0 80.4 jit_solution(15630082608861024701)
XLA Ops:
  0.6 1.2 %shard_map.158 = f32[384,128]{1,0:T(8,128)S(1)} custom-call(bf16[128,256]{1,0:T(8,128)(2,1)} %bitcast.25, bf16[128,256]{1,0:T(8,128)(2,1)} %bitcast.17, bf16[128,256]{1,0:T(8,128)(2,1)} %bitcast.20, f32[128,256]{1,0:T(8,128)} %filter_ref.3), custom_call_target="tpu_custom_call" | custom-call | tf_op jit(solution)/shard_map/pallas_call | solution.py:203
  1.8 8.8 %collective-permute-start = (f32[384,128]{1,0:T(8,128)S(1)}, f32[384,128]{1,0:T(8,128)S(1)}, u32[]{:S(2)}, u32[]{:S(2)}) collective-permute-start(f32[384,128]{1,0:T(8,128)S(1)} %shard_map.158), channel_id=1, source_target_pairs={{0,1},{1,0},{2,3},{3,2},{4,5},{5,4},{6,7},{7,6},{8,9},{9,8},{10,11... | collective-permute-start | bytes 589832 | tf_op jit(solution)/shard_map/ppermute | solution.py:206
  10.6 1.2 %shard_map.159.packed_ref = f32[768,128]{1,0:T(8,128)S(1)} custom-call(bf16[128,256]{1,0:T(8,128)(2,1)} %bitcast.26, bf16[128,256]{1,0:T(8,128)(2,1)} %bitcast.18, bf16[128,256]{1,0:T(8,128)(2,1)} %bitcast.21, f32[128,256]{1,0:T(8,128)} %filter_ref.3), custom_call_target="tpu_custom_call" | custom-call | tf_op jit(solution)/shard_map/pallas_call | solution.py:207
  11.8 0.0 collective-permute-done.handed_ref
  11.8 0.0 copy-start.10
  11.8 0.0 copy-start.11
  11.8 0.0 copy-start.2
  11.9 0.0 copy-start.3
  11.9 0.0 copy-start.4
  11.9 0.0 copy-start.5
  11.9 0.0 copy-start.6
  11.9 0.0 copy-start.7
  11.9 0.0 copy-start.8
  11.9 0.0 copy-start.9
  11.9 30.7 %all_to_all.21 = f32[64,1,1536]{2,1,0:T(1,128)S(1)} all-to-all(f32[64,1,1536]{2,1,0:T(1,128)S(1)} %bitcast.12), channel_id=1, replica_groups=mesh['rep'=4,'chip'=64,'core'=2] {'chip'}, dimensions={0} | all-to-all | bytes 786432 | tf_op jit(solution)/shard_map/all_to_all | solution.py:189
  42.6 0.0 copy-done.10
  42.6 0.0 copy-done.11
  42.6 0.0 copy-done.2
  42.6 0.0 copy-done.3
  42.6 0.0 copy-done.4
  42.6 0.0 copy-done.5
  42.7 0.0 copy-done.6
  42.7 0.0 copy-done.7
  42.7 0.0 copy-done.8
  42.7 0.0 copy-done.9
  42.7 1.4 %shard_map.161 = f32[512,128]{1,0:T(8,128)S(1)} custom-call(f32[768,128]{1,0:T(8,128)S(1)} %bitcast.15, f32[128,128]{1,0:T(8,128)S(1)} %copy-done.11, f32[128,128]{1,0:T(8,128)S(1)} %copy-done.10, bf16[256,128]{1,0:T(8,128)(2,1)S(1)} %copy-done.9, bf16[256,128]{1,0:T(8,128)(2,1)S(1)} %copy-done.8, bf16[256,256]{1,0:T(8,128)(2,1)S(1)} %copy-done.5, ...), custom_call_target="tpu_custom_call" | custom-call | tf_op jit(solution)/shard_map/pallas_call | solution.py:217
  44.1 21.3 %all_to_all.22 = f32[64,1,1024]{2,1,0:T(1,128)S(1)} all-to-all(f32[64,1,1024]{2,1,0:T(1,128)S(1)} %bitcast.16), channel_id=1, replica_groups=mesh['rep'=4,'chip'=64,'core'=2] {'chip'}, dimensions={0} | all-to-all | bytes 524288 | tf_op jit(solution)/shard_map/all_to_all | solution.py:189
  65.4 0.7 shard_map.162
  66.1 0.0 copy-start
  66.1 0.0 copy-start.1
  66.1 7.9 %all-to-all-start.2 = ((f32[8,32,128]{2,1,0:T(8,128)}), f32[8,32,128]{2,1,0:T(8,128)S(1)}, u32[]{:S(2)}, u32[]{:S(2)}) async-start(f32[8,32,128]{2,1,0:T(8,128)} %bitcast.9), calls=%async_computation.2 | async-start | bytes 262144 | tf_op jit(solution)/shard_map/all_to_all | solution.py:225
  74.0 0.0 copy-start.12
  74.0 2.0 %collective-permute-start.1 = (f32[128,128]{1,0:T(8,128)S(1)}, f32[128,128]{1,0:T(8,128)S(1)}, u32[]{:S(2)}, u32[]{:S(2)}) collective-permute-start(f32[128,128]{1,0:T(8,128)S(1)} %get-tuple-element.4), channel_id=1, source_target_pairs={{0,1},{1,0},{2,3},{3,2},{4,5},{5,4},{6,7},{7,6},{8,9},{9,8},{10,11... | collective-permute-start | bytes 196616 | tf_op jit(solution)/shard_map/ppermute | solution.py:228
  76.1 1.2 %collective-permute-done.1.other_ref = f32[128,128]{1,0:T(8,128)S(1)} collective-permute-done((f32[128,128]{1,0:T(8,128)S(1)}, f32[128,128]{1,0:T(8,128)S(1)}, u32[]{:S(2)}, u32[]{:S(2)}) %collective-permute-start.1) | collective-permute-done | bytes 65568 | tf_op jit(solution)/shard_map/ppermute | solution.py:228
  77.3 0.0 copy-done
  77.3 0.0 copy-done.1
  77.3 0.0 copy-done.12
  77.3 0.7 shard_map.163
  78.0 1.8 %all-to-all-done.2 = f32[8,32,128]{2,1,0:T(8,128)S(1)} async-done(((f32[8,32,128]{2,1,0:T(8,128)}), f32[8,32,128]{2,1,0:T(8,128)S(1)}, u32[]{:S(2)}, u32[]{:S(2)}) %all-to-all-start.2) | async-done | bytes 131104 | tf_op jit(solution)/shard_map/all_to_all | solution.py:225
  79.8 0.6 shard_map.164
  (1 shorter events, 0.0 us)
Async XLA Ops:
  1.8 10.0 %collective-permute-start = (f32[384,128]{1,0:T(8,128)S(1)}, f32[384,128]{1,0:T(8,128)S(1)}, u32[]{:S(2)}, u32[]{:S(2)}) collective-permute-start(f32[384,128]{1,0:T(8,128)S(1)} %shard_map.158), channel_id=1, source_target_pairs={{0,1},{1,0},{2,3},{3,2},{4,5},{5,4},{6,7},{7,6},{8,9},{9,8},{10,11... | collective-permute-start | bytes 589832 | tf_op jit(solution)/shard_map/ppermute | solution.py:206
  11.8 30.8 %copy-start.10 = (f32[128,128]{1,0:T(8,128)S(1)}, f32[128,128]{1,0:T(8,128)}, u32[]{:S(2)}) copy-start(f32[128,128]{1,0:T(8,128)} %constant.21.clone.sin_ref) | copy-start | bytes 196612
  11.8 30.8 %copy-start.11 = (f32[128,128]{1,0:T(8,128)S(1)}, f32[128,128]{1,0:T(8,128)}, u32[]{:S(2)}) copy-start(f32[128,128]{1,0:T(8,128)} %constant.20.clone.cos_ref) | copy-start | bytes 196612
  11.8 30.8 %copy-start.2 = (bf16[256,256]{1,0:T(8,128)(2,1)S(1)}, bf16[256,256]{1,0:T(8,128)(2,1)}, u32[]{:S(2)}) copy-start(bf16[256,256]{1,0:T(8,128)(2,1)} %constant.27.clone.refs_5_) | copy-start | bytes 393220
  11.9 30.8 %copy-start.3 = (bf16[256,256]{1,0:T(8,128)(2,1)S(1)}, bf16[256,256]{1,0:T(8,128)(2,1)}, u32[]{:S(2)}) copy-start(bf16[256,256]{1,0:T(8,128)(2,1)} %constant.26.clone.refs_4_) | copy-start | bytes 393220
  11.9 30.8 %copy-start.4 = (bf16[256,256]{1,0:T(8,128)(2,1)S(1)}, bf16[256,256]{1,0:T(8,128)(2,1)}, u32[]{:S(2)}) copy-start(bf16[256,256]{1,0:T(8,128)(2,1)} %constant.25.clone.refs_3_) | copy-start | bytes 393220
  11.9 30.8 %copy-start.5 = (bf16[256,256]{1,0:T(8,128)(2,1)S(1)}, bf16[256,256]{1,0:T(8,128)(2,1)}, u32[]{:S(2)}) copy-start(bf16[256,256]{1,0:T(8,128)(2,1)} %constant.24.clone.refs_2_) | copy-start | bytes 393220
  11.9 30.8 %copy-start.6 = (bf16[128,256]{1,0:T(8,128)(2,1)S(1)}, bf16[128,256]{1,0:T(8,128)(2,1)}, u32[]{:S(2)}) copy-start(bf16[128,256]{1,0:T(8,128)(2,1)} %constant.29.clone.refs_7_) | copy-start | bytes 196612
  11.9 30.8 %copy-start.7 = (bf16[128,256]{1,0:T(8,128)(2,1)S(1)}, bf16[128,256]{1,0:T(8,128)(2,1)}, u32[]{:S(2)}) copy-start(bf16[128,256]{1,0:T(8,128)(2,1)} %constant.28.clone.refs_6_) | copy-start | bytes 196612
  11.9 30.8 %copy-start.8 = (bf16[256,128]{1,0:T(8,128)(2,1)S(1)}, bf16[256,128]{1,0:T(8,128)(2,1)}, u32[]{:S(2)}) copy-start(bf16[256,128]{1,0:T(8,128)(2,1)} %constant.23.clone.refs_1_) | copy-start | bytes 196612
  11.9 30.8 %copy-start.9 = (bf16[256,128]{1,0:T(8,128)(2,1)S(1)}, bf16[256,128]{1,0:T(8,128)(2,1)}, u32[]{:S(2)}) copy-start(bf16[256,128]{1,0:T(8,128)(2,1)} %constant.22.clone.refs_0_) | copy-start | bytes 196612
  66.1 11.2 %copy-start = (bf16[1,128,256]{2,1,0:T(8,128)(2,1)S(1)}, bf16[1,128,256]{2,1,0:T(8,128)(2,1)}, u32[]{:S(2)}) copy-start(bf16[1,128,256]{2,1,0:T(8,128)(2,1)} %param.16) | copy-start | bytes 196612
  66.1 11.2 %copy-start.1 = (bf16[1,128,256]{2,1,0:T(8,128)(2,1)S(1)}, bf16[1,128,256]{2,1,0:T(8,128)(2,1)}, u32[]{:S(2)}) copy-start(bf16[1,128,256]{2,1,0:T(8,128)(2,1)} %param.17) | copy-start | bytes 196612
  66.1 13.7 %all-to-all-start.2 = ((f32[8,32,128]{2,1,0:T(8,128)}), f32[8,32,128]{2,1,0:T(8,128)S(1)}, u32[]{:S(2)}, u32[]{:S(2)}) async-start(f32[8,32,128]{2,1,0:T(8,128)} %bitcast.9), calls=%async_computation.2 | async-start | bytes 262144 | tf_op jit(solution)/shard_map/all_to_all | solution.py:225
  74.0 3.3 %copy-start.12 = (f32[256]{0:T(256)S(1)}, f32[256]{0:T(256)}, u32[]{:S(2)}) copy-start(f32[256]{0:T(256)} %param.19) | copy-start | bytes 3076
  74.0 3.3 %collective-permute-start.1 = (f32[128,128]{1,0:T(8,128)S(1)}, f32[128,128]{1,0:T(8,128)S(1)}, u32[]{:S(2)}, u32[]{:S(2)}) collective-permute-start(f32[128,128]{1,0:T(8,128)S(1)} %get-tuple-element.4), channel_id=1, source_target_pairs={{0,1},{1,0},{2,3},{3,2},{4,5},{5,4},{6,7},{7,6},{8,9},{9,8},{10,11... | collective-permute-start | bytes 196616 | tf_op jit(solution)/shard_map/ppermute | solution.py:228

commit v6 on v4

--- a/solution.py
+++ b/solution.py
@@ -28,7 +28,7 @@
 
 def tables(members, stride):
     padded = 2 * members * stride
-    t1 = np.arange(members)
+    t1 = np.arange(members).reshape(members // 2, 2).T.reshape(-1)
     t2 = np.arange(stride)
     odd = 2 * np.arange(members) + 1
     outer = 2.0 * np.pi / (4 * members) * (odd[:, None] * t1[None, :] % (4 * members))
@@ -38,7 +38,8 @@
     second = np.block([[np.cos(inner), -np.sin(inner)], [np.sin(inner), np.cos(inner)]])
     scale = 2.0 / padded / math.sqrt(members * stride)
     result = [np.asarray(np.cos(twist), np.float32), np.asarray(np.sin(twist), np.float32)]
-    for table in (first, second, second.T, first.T * scale):
+    last = first[:, np.argsort(t1)].T * scale
+    for table in (first, second, second.T, last):
         high = table.astype(jnp.bfloat16)
         result += [high, (table - high.astype(np.float64)).astype(jnp.bfloat16)]
     return result
@@ -52,8 +53,8 @@
         turned = signal.T
         for block in range(4 * quarters):
             quarter, core, part = block // 4, block // 2 % 2, block % 2
-            row = 6 * (2 * run * quarter + core) + 2 * index + part
-            out_ref[pl.ds(row, run, stride=12), :] = turned[block * run : (block + 1) * run]
+            row = 6 * run * (quarters * core + quarter) + 2 * index + part
+            out_ref[pl.ds(row, run, stride=6), :] = turned[block * run : (block + 1) * run]
 
 
 def spectra_kernel(signal_ref, cos_ref, sin_ref, *refs):
@@ -168,7 +169,7 @@
     packed = pl.pallas_call(
         functools.partial(pack_kernel, quarters), out_shape=pltpu.VMEM((members * 6, stride), f32)
     )(inputs[0], out_grad[0], out_gate[0], filter_param)
-    spread = exchange(packed, ("chip", "core"))
+    spread = exchange(packed, ("core", "chip"))
     constants = [near(jnp.asarray(table)) for table in tables(members, stride)]
     values = pl.pallas_call(spectra_kernel, out_shape=pltpu.VMEM((members * 4, stride), f32))(
         near(spread), *constants

time: 78.9 us -> 79.1 us (level)
  no operation moved by 1% of the time
where the time goes in v6:
time: 79.1 us; the launch traced here: 78.8 us
  blocking collectives  60.3 us (76%)
  starting transfers between devices  9.95 us (13%)
  Pallas kernels  4.66 us (6%)
  waiting for transfers between devices  3.01 us (4%)
    all_to_all x2, blocking collectives, exchange(): wide = lax.all_to_all(wide, axis, split_axis=0, concat_axis=0, tiled=True)  60.3 us
    all_to_all x1, starting transfers between devices, local(): lax.all_to_all(filter_picked, ('rep', 'core'), split_axis=0, concat_axis=...  7.91 us
    ppermute x1, starting transfers between devices, local(): other = lax.ppermute(input_picked, 'core', [(0, 1), (1, 0)])  2.04 us
    all_to_all x1, waiting for transfers between devices, local(): lax.all_to_all(filter_picked, ('rep', 'core'), split_axis=0, concat_axis=...  1.79 us
  transfers between devices with their start and end apart: 2, of which 2 were waited for; matrix products, arithmetic and copies ran while one was open for 0% of the time, Pallas kernels for 1%

profile of v6, /device:TPU:1, one launch (start us, length us, event | category | flops | bytes accessed | tf_op | source)
XLA Modules:
  0.0 78.8 jit_solution(17437697624733348783)
XLA Ops:
  0.6 0.0 copy-start.10
  0.6 0.0 copy-start.11
  0.7 1.2 %shard_map.158 = f32[768,128]{1,0:T(8,128)S(1)} custom-call(bf16[128,256]{1,0:T(8,128)(2,1)} %bitcast.23, bf16[128,256]{1,0:T(8,128)(2,1)} %bitcast.18, bf16[128,256]{1,0:T(8,128)(2,1)} %bitcast.20, f32[128,256]{1,0:T(8,128)} %filter_ref.1), custom_call_target="tpu_custom_call" | custom-call | tf_op jit(solution)/shard_map/pallas_call | solution.py:169
  1.9 0.0 copy-start.2
  1.9 0.0 copy-start.3
  1.9 0.0 copy-start.4
  1.9 0.0 copy-start.5
  1.9 0.0 copy-start.6
  1.9 0.0 copy-start.7
  1.9 0.0 copy-start.8
  1.9 0.0 copy-start.9
  2.0 41.2 %all_to_all.21 = f32[128,1,768]{2,1,0:T(1,128)S(1)} all-to-all(f32[128,1,768]{2,1,0:T(1,128)S(1)} %bitcast.15), channel_id=1, replica_groups=mesh['rep'=4,'chip'=64,'core'=2] {'core','chip'}, dimensions={0} | all-to-all | bytes 786432 | tf_op jit(solution)/shard_map/all_to_all | solution.py:156
  43.2 0.0 copy-done.10
  43.2 0.0 copy-done.11
  43.2 0.0 copy-done.2
  43.2 0.0 copy-done.3
  43.2 0.0 copy-done.4
  43.2 0.0 copy-done.5
  43.2 0.0 copy-done.6
  43.2 0.0 copy-done.7
  43.2 0.0 copy-done.8
  43.2 0.0 copy-done.9
  43.3 1.4 %shard_map.159 = f32[512,128]{1,0:T(8,128)S(1)} custom-call(f32[768,128]{1,0:T(8,128)S(1)} %bitcast.14, f32[128,128]{1,0:T(8,128)S(1)} %copy-done.11, f32[128,128]{1,0:T(8,128)S(1)} %copy-done.10, bf16[256,128]{1,0:T(8,128)(2,1)S(1)} %copy-done.9, bf16[256,128]{1,0:T(8,128)(2,1)S(1)} %copy-done.8, bf16[256,256]{1,0:T(8,128)(2,1)S(1)} %copy-done.5, ...), custom_call_target="tpu_custom_call" | custom-call | tf_op jit(solution)/shard_map/pallas_call | solution.py:174
  44.7 19.1 %all_to_all.22 = f32[64,1,1024]{2,1,0:T(1,128)S(1)} all-to-all(f32[64,1,1024]{2,1,0:T(1,128)S(1)} %bitcast.16), channel_id=1, replica_groups=mesh['rep'=4,'chip'=64,'core'=2] {'chip'}, dimensions={0} | all-to-all | bytes 524288 | tf_op jit(solution)/shard_map/all_to_all | solution.py:156
  63.7 0.7 shard_map.160
  64.4 0.0 copy-start
  64.4 0.0 copy-start.1
  64.4 7.9 %all-to-all-start.2 = ((f32[8,32,128]{2,1,0:T(8,128)}), f32[8,32,128]{2,1,0:T(8,128)S(1)}, u32[]{:S(2)}, u32[]{:S(2)}) async-start(f32[8,32,128]{2,1,0:T(8,128)} %bitcast.9), calls=%async_computation.2 | async-start | bytes 262144 | tf_op jit(solution)/shard_map/all_to_all | solution.py:182
  72.3 0.0 copy-start.12
  72.3 2.0 %collective-permute-start = (f32[128,128]{1,0:T(8,128)S(1)}, f32[128,128]{1,0:T(8,128)S(1)}, u32[]{:S(2)}, u32[]{:S(2)}) collective-permute-start(f32[128,128]{1,0:T(8,128)S(1)} %get-tuple-element.4), channel_id=1, source_target_pairs={{0,1},{1,0},{2,3},{3,2},{4,5},{5,4},{6,7},{7,6},{8,9},{9,8},{10,11... | collective-permute-start | bytes 196616 | tf_op jit(solution)/shard_map/ppermute | solution.py:185
  74.4 1.2 %collective-permute-done.other_ref = f32[128,128]{1,0:T(8,128)S(1)} collective-permute-done((f32[128,128]{1,0:T(8,128)S(1)}, f32[128,128]{1,0:T(8,128)S(1)}, u32[]{:S(2)}, u32[]{:S(2)}) %collective-permute-start) | collective-permute-done | bytes 65568 | tf_op jit(solution)/shard_map/ppermute | solution.py:185
  75.6 0.0 copy-done
  75.6 0.0 copy-done.1
  75.6 0.0 copy-done.12
  75.6 0.7 shard_map.161
  76.3 1.8 %all-to-all-done.2 = f32[8,32,128]{2,1,0:T(8,128)S(1)} async-done(((f32[8,32,128]{2,1,0:T(8,128)}), f32[8,32,128]{2,1,0:T(8,128)S(1)}, u32[]{:S(2)}, u32[]{:S(2)}) %all-to-all-start.2) | async-done | bytes 131104 | tf_op jit(solution)/shard_map/all_to_all | solution.py:182
  78.1 0.6 shard_map.162
Async XLA Ops:
  0.6 42.5 %copy-start.10 = (f32[128,128]{1,0:T(8,128)S(1)}, f32[128,128]{1,0:T(8,128)}, u32[]{:S(2)}) copy-start(f32[128,128]{1,0:T(8,128)} %constant.21.clone.sin_ref) | copy-start | bytes 196612
  0.6 42.5 %copy-start.11 = (f32[128,128]{1,0:T(8,128)S(1)}, f32[128,128]{1,0:T(8,128)}, u32[]{:S(2)}) copy-start(f32[128,128]{1,0:T(8,128)} %constant.20.clone.cos_ref) | copy-start | bytes 196612
  1.9 41.3 %copy-start.2 = (bf16[256,256]{1,0:T(8,128)(2,1)S(1)}, bf16[256,256]{1,0:T(8,128)(2,1)}, u32[]{:S(2)}) copy-start(bf16[256,256]{1,0:T(8,128)(2,1)} %constant.27.clone.refs_5_) | copy-start | bytes 393220
  1.9 41.3 %copy-start.3 = (bf16[256,256]{1,0:T(8,128)(2,1)S(1)}, bf16[256,256]{1,0:T(8,128)(2,1)}, u32[]{:S(2)}) copy-start(bf16[256,256]{1,0:T(8,128)(2,1)} %constant.26.clone.refs_4_) | copy-start | bytes 393220
  1.9 41.3 %copy-start.4 = (bf16[256,256]{1,0:T(8,128)(2,1)S(1)}, bf16[256,256]{1,0:T(8,128)(2,1)}, u32[]{:S(2)}) copy-start(bf16[256,256]{1,0:T(8,128)(2,1)} %constant.25.clone.refs_3_) | copy-start | bytes 393220
  1.9 41.3 %copy-start.5 = (bf16[256,256]{1,0:T(8,128)(2,1)S(1)}, bf16[256,256]{1,0:T(8,128)(2,1)}, u32[]{:S(2)}) copy-start(bf16[256,256]{1,0:T(8,128)(2,1)} %constant.24.clone.refs_2_) | copy-start | bytes 393220
  1.9 41.3 %copy-start.6 = (bf16[128,256]{1,0:T(8,128)(2,1)S(1)}, bf16[128,256]{1,0:T(8,128)(2,1)}, u32[]{:S(2)}) copy-start(bf16[128,256]{1,0:T(8,128)(2,1)} %constant.29.clone.refs_7_) | copy-start | bytes 196612
  1.9 41.3 %copy-start.7 = (bf16[128,256]{1,0:T(8,128)(2,1)S(1)}, bf16[128,256]{1,0:T(8,128)(2,1)}, u32[]{:S(2)}) copy-start(bf16[128,256]{1,0:T(8,128)(2,1)} %constant.28.clone.refs_6_) | copy-start | bytes 196612
  1.9 41.3 %copy-start.8 = (bf16[256,128]{1,0:T(8,128)(2,1)S(1)}, bf16[256,128]{1,0:T(8,128)(2,1)}, u32[]{:S(2)}) copy-start(bf16[256,128]{1,0:T(8,128)(2,1)} %constant.23.clone.refs_1_) | copy-start | bytes 196612
  1.9 41.3 %copy-start.9 = (bf16[256,128]{1,0:T(8,128)(2,1)S(1)}, bf16[256,128]{1,0:T(8,128)(2,1)}, u32[]{:S(2)}) copy-start(bf16[256,128]{1,0:T(8,128)(2,1)} %constant.22.clone.refs_0_) | copy-start | bytes 196612
  64.4 11.2 %copy-start = (bf16[1,128,256]{2,1,0:T(8,128)(2,1)S(1)}, bf16[1,128,256]{2,1,0:T(8,128)(2,1)}, u32[]{:S(2)}) copy-start(bf16[1,128,256]{2,1,0:T(8,128)(2,1)} %param.16) | copy-start | bytes 196612
  64.4 11.2 %copy-start.1 = (bf16[1,128,256]{2,1,0:T(8,128)(2,1)S(1)}, bf16[1,128,256]{2,1,0:T(8,128)(2,1)}, u32[]{:S(2)}) copy-start(bf16[1,128,256]{2,1,0:T(8,128)(2,1)} %param.17) | copy-start | bytes 196612
  64.4 13.7 %all-to-all-start.2 = ((f32[8,32,128]{2,1,0:T(8,128)}), f32[8,32,128]{2,1,0:T(8,128)S(1)}, u32[]{:S(2)}, u32[]{:S(2)}) async-start(f32[8,32,128]{2,1,0:T(8,128)} %bitcast.9), calls=%async_computation.2 | async-start | bytes 262144 | tf_op jit(solution)/shard_map/all_to_all | solution.py:182
  72.3 3.3 %copy-start.12 = (f32[256]{0:T(256)S(1)}, f32[256]{0:T(256)}, u32[]{:S(2)}) copy-start(f32[256]{0:T(256)} %param.19) | copy-start | bytes 3076
  72.3 3.3 %collective-permute-start = (f32[128,128]{1,0:T(8,128)S(1)}, f32[128,128]{1,0:T(8,128)S(1)}, u32[]{:S(2)}, u32[]{:S(2)}) collective-permute-start(f32[128,128]{1,0:T(8,128)S(1)} %get-tuple-element.4), channel_id=1, source_target_pairs={{0,1},{1,0},{2,3},{3,2},{4,5},{5,4},{6,7},{7,6},{8,9},{9,8},{10,11... | collective-permute-start | bytes 196616 | tf_op jit(solution)/shard_map/ppermute | solution.py:185

commit v7 on v3

v7 whole, which is shorter than its diff:
```python
import functools
import math

import jax
import jax.numpy as jnp
import numpy as np
from jax import lax
from jax.experimental import pallas as pl
from jax.experimental.pallas import tpu as pltpu
from jax.sharding import Mesh
from jax.sharding import PartitionSpec as P


def halves(values):
    high = values.astype(jnp.bfloat16)
    return high, (values - high.astype(jnp.float32)).astype(jnp.bfloat16)


def product(left, right):
    def dot(one, other):
        return jnp.dot(one, other, preferred_element_type=jnp.float32)

    total = dot(left[0], right[0])
    if right[1] is not None:
        total = total + dot(left[0], right[1])
    return total + dot(left[1], right[0])


def tables(members, stride):
    padded = 2 * members * stride
    t1 = np.arange(members)
    t2 = np.arange(stride)
    odd = 2 * np.arange(members) + 1
    outer = 2.0 * np.pi / (4 * members) * (odd[:, None] * t1[None, :] % (4 * members))
    twist = 2.0 * np.pi / (2 * padded) * (odd[:, None] * t2[None, :] % (2 * padded))
    inner = 2.0 * np.pi / stride * (t2[:, None] * t2[None, :] % stride)
    first = np.concatenate([np.cos(outer), -np.sin(outer)], axis=0)
    second = np.block([[np.cos(inner), -np.sin(inner)], [np.sin(inner), np.cos(inner)]])
    scale = 2.0 / padded / math.sqrt(members * stride)
    result = [np.asarray(np.cos(twist), np.float32), np.asarray(np.sin(twist), np.float32)]
    last = np.concatenate([first.T[0::2], first.T[1::2]], axis=0) * scale
    for table in (first, second, second.T, last):
        high = table.astype(jnp.bfloat16)
        result += [high, (table - high.astype(np.float64)).astype(jnp.bfloat16)]
    return result


def pack_kernel(inputs_ref, grad_ref, gate_ref, filter_ref, out_ref):
    gated = grad_ref[...].astype(jnp.float32) * gate_ref[...].astype(jnp.float32)
    signals = (gated, inputs_ref[...].astype(jnp.float32), filter_ref[...])
    chips = out_ref.shape[0] // 12
    for index, signal in enumerate(signals):
        turned = signal.T
        for quarter in range(4):
            row = 6 * (quarter // 2) + 2 * index + quarter % 2
            out_ref[pl.ds(row, chips, stride=12), :] = turned[
                quarter * chips : (quarter + 1) * chips
            ]


def spectra(signal_ref, first, second, cosine, sine):
    stride = signal_ref.shape[1]
    members = signal_ref.shape[0] // 6
    signals = [signal_ref[pl.ds(row, members, stride=6), :] for row in range(6)]
    partial = []
    for row in range(0, 6, 2):
        pair = jnp.concatenate(signals[row : row + 2], axis=1)
        sides = (pair.astype(jnp.bfloat16), None) if row == 2 else halves(pair)
        both = product(first, sides)
        partial += [both[:, :stride], both[:, stride:]]
    parts = []
    for value in partial:
        real, imag = value[:members], value[members:]
        turned = jnp.concatenate(
            [real * cosine + imag * sine, imag * cosine - real * sine], axis=1
        )
        parts.append(product(halves(turned), second))
    return parts


def correlated(one, other):
    stride = one.shape[1] // 2
    real, imag = one[:, :stride], one[:, stride:]
    other_real, other_imag = other[:, :stride], other[:, stride:]
    return jnp.concatenate(
        [real * other_real + imag * other_imag, imag * other_real - real * other_imag], axis=1
    )


def inverse(values, back, last, cosine, sine):
    columns = []
    for value in values:
        restored = product(halves(value), back)
        stride = restored.shape[1] // 2
        real, imag = restored[:, :stride], restored[:, stride:]
        columns.append(
            jnp.concatenate([real * cosine - imag * sine, imag * cosine + real * sine], axis=0)
        )
    return product(last, halves(jnp.concatenate(columns, axis=1)))


def pairs_of(refs):
    return [(refs[at][...], refs[at + 1][...]) for at in range(0, len(refs), 2)]


def filter_side_kernel(signal_ref, cos_ref, sin_ref, *refs):
    first, second, back, last = pairs_of(refs[:8])
    out_ref, product_ref = refs[8:]
    stride = signal_ref.shape[1]
    members = signal_ref.shape[0] // 6
    cosine, sine = cos_ref[...], sin_ref[...]
    parts = spectra(signal_ref, first, second, cosine, sine)
    values = inverse(
        [correlated(parts[0], parts[2]), correlated(parts[1], parts[3])], back, last, cosine, sine
    )
    for quarter in range(4):
        part = quarter % 2
        out_ref[quarter * members : (quarter + 1) * members, :] = values[
            :, part * stride : (part + 1) * stride
        ]
    for part in range(2):
        product_ref[part * members : (part + 1) * members, :] = correlated(
            parts[part], parts[4 + part]
        )


def input_side_kernel(product_ref, cos_ref, sin_ref, *refs):
    back, last = pairs_of(refs[:4])
    kept_ref, handed_ref = refs[4:]
    stride = cos_ref.shape[1]
    members = product_ref.shape[0] // 2
    chips = members // 2
    core = lax.axis_index("core")
    values = inverse(
        [product_ref[:members, :], product_ref[members:, :]],
        back,
        last,
        cos_ref[...],
        sin_ref[...],
    )
    for part in range(2):
        even = values[:chips, part * stride : (part + 1) * stride]
        odd = values[chips:, part * stride : (part + 1) * stride]
        rows = slice(part * chips, (part + 1) * chips)
        kept_ref[rows, :] = jnp.where(core == 0, even, odd)
        handed_ref[rows, :] = jnp.where(core == 0, odd, even)


def merge_kernel(kept_ref, handed_ref, pieces_ref, out_ref):
    first = lax.axis_index("core") == 0
    source = lax.axis_index("rep") // 2
    chips = out_ref.shape[0] // 5
    for part in range(2):
        mine = kept_ref[part * chips : (part + 1) * chips, :]
        other = handed_ref[part * chips : (part + 1) * chips, :]
        out_ref[pl.ds(part, chips, stride=5), :] = jnp.where(first, mine, other)
        out_ref[pl.ds(2 + part, chips, stride=5), :] = jnp.where(first, other, mine)
    total = None
    for member in range(4):
        start = pl.multiple_of((2 * member + source) * chips, chips)
        piece = pieces_ref[pl.ds(start, chips), :]
        total = piece if total is None else total + piece
    out_ref[pl.ds(4, chips, stride=5), :] = total


def last_kernel(returned_ref, grad_ref, gate_ref, skip_ref, input_ref, filter_ref):
    chips = returned_ref.shape[0] // 5
    filter_ref[...] = returned_ref[pl.ds(4, chips, stride=5), :]
    rows = [returned_ref[pl.ds(quarter, chips, stride=5), :] for quarter in range(4)]
    gated = grad_ref[...].astype(jnp.float32) * gate_ref[...].astype(jnp.float32)
    total = jnp.concatenate(rows, axis=0).T + gated * skip_ref[...]
    input_ref[...] = total.astype(jnp.bfloat16)


def exchange(values, axis):
    rows, columns = values.shape
    members = lax.axis_size(axis)
    wide = values.reshape(members, 1, rows // members * columns)
    wide = lax.all_to_all(wide, axis, split_axis=0, concat_axis=0, tiled=True)
    return wide.reshape(rows, columns)


def near(values):
    return pltpu.with_memory_space_constraint(values, pltpu.VMEM)


def local(inputs, out_grad, out_gate, filter_param, skip_gain):
    members = lax.axis_size(("chip", "core"))
    stride, channels = filter_param.shape
    f32 = jnp.float32
    packed = pl.pallas_call(pack_kernel, out_shape=pltpu.VMEM((members * 6, stride), f32))(
        inputs[0], out_grad[0], out_gate[0], filter_param
    )
    spread = exchange(packed, ("chip", "core"))
    constants = [near(jnp.asarray(table)) for table in tables(members, stride)]
    slots, products = pl.pallas_call(
        filter_side_kernel,
        out_shape=[
            pltpu.VMEM((members * 4, stride), f32),
            pltpu.VMEM((members * 2, 2 * stride), f32),
        ],
    )(near(spread), *constants)
    pieces = exchange(slots, ("rep", "core"))
    kept, handed = pl.pallas_call(
        input_side_kernel, out_shape=[pltpu.VMEM((members, stride), f32)] * 2
    )(near(products), *constants[:2], *constants[6:])
    handed = lax.ppermute(handed, "core", [(0, 1), (1, 0)])
    merged = pl.pallas_call(
        merge_kernel, out_shape=pltpu.VMEM((members // 2 * 5, stride), f32)
    )(near(kept), near(handed), near(pieces))
    returned = exchange(merged, "chip")
    input_part, filter_part = pl.pallas_call(
        last_kernel,
        out_shape=[
            jax.ShapeDtypeStruct((stride, channels), jnp.bfloat16),
            jax.ShapeDtypeStruct((channels // 4, stride), f32),
        ],
    )(near(returned), near(out_grad[0]), near(out_gate[0]), near(skip_gain[None, :]))
    return (input_part[None], filter_part.T)


def solution(mesh):
    seqs, members = mesh.devices.shape
    cores = Mesh(mesh.devices.reshape(seqs, members // 2, 2), ("rep", "chip", "core"))
    ctx = ("chip", "core")
    return jax.shard_map(
        local,
        mesh=cores,
        in_specs=(
            P("rep", ctx, None),
            P("rep", ctx, None),
            P("rep", ctx, None),
            P(ctx, None),
            P(),
        ),
        out_specs=(P("rep", ctx, None), P(ctx, "rep")),
        check_vma=False,
    )
```

time: 80.2 us -> 79.9 us (level); the launches traced: 78.8 us -> 79.4 us
  blocking collectives: 64.9 us -> 58.7 us
  starting transfers between devices: 4.4 us -> 8.51 us
  waiting for transfers between devices: 3.36 us -> 6.24 us
    all_to_all x2, blocking collectives: 64.9 us -> 58.7 us  [exchange(): wide = lax.all_to_all(wide, axis, split_axis=0, concat_axis=0, tiled=True)]
    all_to_all x1, starting transfers between devices: 4.4 us -> 6.59 us  [exchange(): wide = lax.all_to_all(wide, axis, split_axis=0, concat_axis=0, tiled=True)]
    ppermute x0 -> x1, starting transfers between devices: none -> 1.92 us  [local(): handed = lax.ppermute(handed, 'core', [(0, 1), (1, 0)])]
    all_to_all x1, waiting for transfers between devices: 3.36 us -> 5.02 us  [exchange(): wide = lax.all_to_all(wide, axis, split_axis=0, concat_axis=0, tiled=True)]
    ppermute x0 -> x1, waiting for transfers between devices: none -> 1.22 us  [local(): handed = lax.ppermute(handed, 'core', [(0, 1), (1, 0)])]
  transfers between devices with their start and end apart: 1 -> 2, of which waited for: 1 -> 2; matrix products, arithmetic and copies ran while one was open for 0% -> 0% of each run, Pallas kernels for 1% -> 1%
where the time goes in v7:
time: 79.9 us; the launch traced here: 79.4 us
  blocking collectives  58.7 us (73%)
  starting transfers between devices  8.51 us (11%)
  waiting for transfers between devices  6.24 us (8%)
  Pallas kernels  4.41 us (6%)
  between operations  0.81 us (1%)
    all_to_all x2, blocking collectives, exchange(): wide = lax.all_to_all(wide, axis, split_axis=0, concat_axis=0, tiled=True)  58.7 us
    all_to_all x1, starting transfers between devices, exchange(): wide = lax.all_to_all(wide, axis, split_axis=0, concat_axis=0, tiled=True)  6.59 us
    all_to_all x1, waiting for transfers between devices, exchange(): wide = lax.all_to_all(wide, axis, split_axis=0, concat_axis=0, tiled=True)  5.02 us
    pallas_call x1, Pallas kernels, local(): pl.pallas_call(filter_side_kernel, out_shape=[pltpu.VMEM((members * 4, st...  1.93 us
    ppermute x1, starting transfers between devices, local(): handed = lax.ppermute(handed, 'core', [(0, 1), (1, 0)])  1.92 us
  transfers between devices with their start and end apart: 2, of which 2 were waited for; matrix products, arithmetic and copies ran while one was open for 0% of the time, Pallas kernels for 1%

profile of v7, /device:TPU:1, one launch (start us, length us, event | category | flops | bytes accessed | tf_op | source)
XLA Modules:
  0.0 79.4 jit_solution(279335801937335392)
XLA Ops:
  0.6 0.0 copy-start.10
  0.6 0.0 copy-start.11
  0.7 1.2 %shard_map.158 = f32[768,128]{1,0:T(8,128)S(1)} custom-call(bf16[128,256]{1,0:T(8,128)(2,1)} %bitcast.22, bf16[128,256]{1,0:T(8,128)(2,1)} %bitcast.17, bf16[128,256]{1,0:T(8,128)(2,1)} %bitcast.19, f32[128,256]{1,0:T(8,128)} %filter_ref.1), custom_call_target="tpu_custom_call" | custom-call | tf_op jit(solution)/shard_map/pallas_call | solution.py:191
  1.9 0.0 copy-start
  1.9 0.0 copy-start.1
  1.9 0.0 copy-start.2
  1.9 0.0 copy-start.3
  1.9 0.0 copy-start.4
  1.9 0.0 copy-start.5
  1.9 0.0 copy-start.8
  1.9 0.0 copy-start.9
  2.0 40.8 %all_to_all.15 = f32[128,1,768]{2,1,0:T(1,128)S(1)} all-to-all(f32[128,1,768]{2,1,0:T(1,128)S(1)} %bitcast.13), channel_id=1, replica_groups=mesh['rep'=4,'chip'=64,'core'=2] {'chip','core'}, dimensions={0} | all-to-all | bytes 786432 | tf_op jit(solution)/shard_map/all_to_all | solution.py:179
  42.8 0.0 copy-done.10
  42.8 0.0 copy-done.11
  42.8 0.0 copy-done
  42.8 0.0 copy-done.1
  42.8 0.0 copy-done.2
  42.8 0.0 copy-done.3
  42.8 0.0 copy-done.4
  42.8 0.0 copy-done.5
  42.9 0.0 copy-done.8
  42.9 0.0 copy-done.9
  42.9 1.9 %shard_map.159 = (f32[512,128]{1,0:T(8,128)}, f32[256,256]{1,0:T(8,128)S(1)}) custom-call(f32[768,128]{1,0:T(8,128)S(1)} %bitcast.12, f32[128,128]{1,0:T(8,128)S(1)} %copy-done.5, f32[128,128]{1,0:T(8,128)S(1)} %copy-done.4, bf16[256,128]{1,0:T(8,128)(2,1)S(1)} %copy-done.11, bf16[256,128]{1,0:T(8,128)(2,1)S(1)} %copy-done.10, ...), custom_call_target="tpu_custom_call" | custom-call | tf_op jit(solution)/shard_map/pallas_call | solution.py:196
  44.8 6.6 %all-to-all-start.1 = ((f32[8,1,8192]{2,1,0:T(1,128)}), f32[8,1,8192]{2,1,0:T(1,128)S(1)}, u32[]{:S(2)}, u32[]{:S(2)}) async-start(f32[8,1,8192]{2,1,0:T(1,128)} %bitcast.5), calls=%async_computation.1 | async-start | bytes 524288 | tf_op jit(solution)/shard_map/all_to_all | solution.py:179
  51.4 0.5 shard_map.160
  51.9 1.9 %collective-permute-start = (f32[128,128]{1,0:T(8,128)S(1)}, f32[128,128]{1,0:T(8,128)S(1)}, u32[]{:S(2)}, u32[]{:S(2)}) collective-permute-start(f32[128,128]{1,0:T(8,128)S(1)} %get-tuple-element.10), channel_id=1, source_target_pairs={{0,1},{1,0},{2,3},{3,2},{4,5},{5,4},{6,7},{7,6},{8,9},{9,8},{10,11... | collective-permute-start | bytes 196616 | tf_op jit(solution)/shard_map/ppermute | solution.py:207
  53.9 1.2 %collective-permute-done.handed_ref = f32[128,128]{1,0:T(8,128)S(1)} collective-permute-done((f32[128,128]{1,0:T(8,128)S(1)}, f32[128,128]{1,0:T(8,128)S(1)}, u32[]{:S(2)}, u32[]{:S(2)}) %collective-permute-start) | collective-permute-done | bytes 65568 | tf_op jit(solution)/shard_map/ppermute | solution.py:207
  55.1 5.0 %all-to-all-done.1 = f32[8,1,8192]{2,1,0:T(1,128)S(1)} async-done(((f32[8,1,8192]{2,1,0:T(1,128)}), f32[8,1,8192]{2,1,0:T(1,128)S(1)}, u32[]{:S(2)}, u32[]{:S(2)}) %all-to-all-start.1) | async-done | bytes 262176 | tf_op jit(solution)/shard_map/all_to_all | solution.py:179
  60.1 0.0 copy-start.6
  60.1 0.0 copy-start.7
  60.1 17.8 %all_to_all.16 = f32[64,1,640]{2,1,0:T(1,128)S(1)} all-to-all(f32[64,1,640]{2,1,0:T(1,128)S(1)} %bitcast.16), channel_id=1, replica_groups=mesh['rep'=4,'chip'=64,'core'=2] {'chip'}, dimensions={0} | all-to-all | bytes 327680 | tf_op jit(solution)/shard_map/all_to_all | solution.py:179
  78.0 0.0 copy-start.12
  78.0 0.0 copy-done.6
  78.0 0.0 copy-done.7
  78.0 0.7 copy-done.12
  78.7 0.7 shard_map.162
  (1 shorter events, 0.0 us)
Async XLA Ops:
  0.6 42.2 %copy-start.10 = (bf16[256,128]{1,0:T(8,128)(2,1)S(1)}, bf16[256,128]{1,0:T(8,128)(2,1)}, u32[]{:S(2)}) copy-start(bf16[256,128]{1,0:T(8,128)(2,1)} %constant.23.clone.refs_1_) | copy-start | bytes 196612
  0.6 42.2 %copy-start.11 = (bf16[256,128]{1,0:T(8,128)(2,1)S(1)}, bf16[256,128]{1,0:T(8,128)(2,1)}, u32[]{:S(2)}) copy-start(bf16[256,128]{1,0:T(8,128)(2,1)} %constant.22.clone.refs_0_) | copy-start | bytes 196612
  1.9 40.9 %copy-start = (bf16[256,256]{1,0:T(8,128)(2,1)S(1)}, bf16[256,256]{1,0:T(8,128)(2,1)}, u32[]{:S(2)}) copy-start(bf16[256,256]{1,0:T(8,128)(2,1)} %constant.27.clone.refs_5_.refs_1_) | copy-start | bytes 393220
  1.9 40.9 %copy-start.1 = (bf16[256,256]{1,0:T(8,128)(2,1)S(1)}, bf16[256,256]{1,0:T(8,128)(2,1)}, u32[]{:S(2)}) copy-start(bf16[256,256]{1,0:T(8,128)(2,1)} %constant.26.clone.refs_4_.refs_0_) | copy-start | bytes 393220
  1.9 40.9 %copy-start.2 = (bf16[128,256]{1,0:T(8,128)(2,1)S(1)}, bf16[128,256]{1,0:T(8,128)(2,1)}, u32[]{:S(2)}) copy-start(bf16[128,256]{1,0:T(8,128)(2,1)} %constant.29.clone.refs_7_.refs_3_) | copy-start | bytes 196612
  1.9 40.9 %copy-start.3 = (bf16[128,256]{1,0:T(8,128)(2,1)S(1)}, bf16[128,256]{1,0:T(8,128)(2,1)}, u32[]{:S(2)}) copy-start(bf16[128,256]{1,0:T(8,128)(2,1)} %constant.28.clone.refs_6_.refs_2_) | copy-start | bytes 196612
  1.9 40.9 %copy-start.4 = (f32[128,128]{1,0:T(8,128)S(1)}, f32[128,128]{1,0:T(8,128)}, u32[]{:S(2)}) copy-start(f32[128,128]{1,0:T(8,128)} %constant.21.clone.sin_ref) | copy-start | bytes 196612
  1.9 40.9 %copy-start.5 = (f32[128,128]{1,0:T(8,128)S(1)}, f32[128,128]{1,0:T(8,128)}, u32[]{:S(2)}) copy-start(f32[128,128]{1,0:T(8,128)} %constant.20.clone.cos_ref) | copy-start | bytes 196612
  1.9 40.9 %copy-start.8 = (bf16[256,256]{1,0:T(8,128)(2,1)S(1)}, bf16[256,256]{1,0:T(8,128)(2,1)}, u32[]{:S(2)}) copy-start(bf16[256,256]{1,0:T(8,128)(2,1)} %constant.25.clone.refs_3_) | copy-start | bytes 393220
  1.9 40.9 %copy-start.9 = (bf16[256,256]{1,0:T(8,128)(2,1)S(1)}, bf16[256,256]{1,0:T(8,128)(2,1)}, u32[]{:S(2)}) copy-start(bf16[256,256]{1,0:T(8,128)(2,1)} %constant.24.clone.refs_2_) | copy-start | bytes 393220
  44.8 15.3 %all-to-all-start.1 = ((f32[8,1,8192]{2,1,0:T(1,128)}), f32[8,1,8192]{2,1,0:T(1,128)S(1)}, u32[]{:S(2)}, u32[]{:S(2)}) async-start(f32[8,1,8192]{2,1,0:T(1,128)} %bitcast.5), calls=%async_computation.1 | async-start | bytes 524288 | tf_op jit(solution)/shard_map/all_to_all | solution.py:179
  51.9 3.1 %collective-permute-start = (f32[128,128]{1,0:T(8,128)S(1)}, f32[128,128]{1,0:T(8,128)S(1)}, u32[]{:S(2)}, u32[]{:S(2)}) collective-permute-start(f32[128,128]{1,0:T(8,128)S(1)} %get-tuple-element.10), channel_id=1, source_target_pairs={{0,1},{1,0},{2,3},{3,2},{4,5},{5,4},{6,7},{7,6},{8,9},{9,8},{10,11... | collective-permute-start | bytes 196616 | tf_op jit(solution)/shard_map/ppermute | solution.py:207
  60.1 17.9 %copy-start.6 = (bf16[1,128,256]{2,1,0:T(8,128)(2,1)S(1)}, bf16[1,128,256]{2,1,0:T(8,128)(2,1)}, u32[]{:S(2)}) copy-start(bf16[1,128,256]{2,1,0:T(8,128)(2,1)} %param.16) | copy-start | bytes 196612
  60.1 17.8 %copy-start.7 = (bf16[1,128,256]{2,1,0:T(8,128)(2,1)S(1)}, bf16[1,128,256]{2,1,0:T(8,128)(2,1)}, u32[]{:S(2)}) copy-start(bf16[1,128,256]{2,1,0:T(8,128)(2,1)} %param.17) | copy-start | bytes 196612
  78.0 0.7 copy-start.12

commit v8 on v7

--- a/solution.py
+++ b/solution.py
@@ -45,8 +45,9 @@
     return result
 
 
-def pack_kernel(inputs_ref, grad_ref, gate_ref, filter_ref, out_ref):
+def pack_kernel(inputs_ref, grad_ref, gate_ref, filter_ref, skip_ref, out_ref, skipped_ref):
     gated = grad_ref[...].astype(jnp.float32) * gate_ref[...].astype(jnp.float32)
+    skipped_ref[...] = gated * skip_ref[...]
     signals = (gated, inputs_ref[...].astype(jnp.float32), filter_ref[...])
     chips = out_ref.shape[0] // 12
     for index, signal in enumerate(signals):
@@ -103,72 +104,57 @@
     return [(refs[at][...], refs[at + 1][...]) for at in range(0, len(refs), 2)]
 
 
-def filter_side_kernel(signal_ref, cos_ref, sin_ref, *refs):
+def spectra_kernel(signal_ref, cos_ref, sin_ref, *refs):
     first, second, back, last = pairs_of(refs[:8])
-    out_ref, product_ref = refs[8:]
+    kept_ref, handed_ref = refs[8:]
     stride = signal_ref.shape[1]
-    members = signal_ref.shape[0] // 6
+    chips = signal_ref.shape[0] // 12
+    even_core = lax.axis_index("core") == 0
     cosine, sine = cos_ref[...], sin_ref[...]
     parts = spectra(signal_ref, first, second, cosine, sine)
-    values = inverse(
-        [correlated(parts[0], parts[2]), correlated(parts[1], parts[3])], back, last, cosine, sine
-    )
-    for quarter in range(4):
-        part = quarter % 2
-        out_ref[quarter * members : (quarter + 1) * members, :] = values[
-            :, part * stride : (part + 1) * stride
-        ]
+    for index, other in enumerate((2, 4)):
+        products = [correlated(parts[part], parts[other + part]) for part in range(2)]
+        values = inverse(products, back, last, cosine, sine)
+        for part in range(2):
+            even = values[:chips, part * stride : (part + 1) * stride]
+            odd = values[chips:, part * stride : (part + 1) * stride]
+            rows = slice((2 * index + part) * chips, (2 * index + part + 1) * chips)
+            kept_ref[rows, :] = jnp.where(even_core, even, odd)
+            handed_ref[rows, :] = jnp.where(even_core, odd, even)
+
+
+def by_quarter(kept_ref, handed_ref, row, chips):
+    even_core = lax.axis_index("core") == 0
+    first, second = [], []
     for part in range(2):
-        product_ref[part * members : (part + 1) * members, :] = correlated(
-            parts[part], parts[4 + part]
-        )
-
-
-def input_side_kernel(product_ref, cos_ref, sin_ref, *refs):
-    back, last = pairs_of(refs[:4])
-    kept_ref, handed_ref = refs[4:]
-    stride = cos_ref.shape[1]
-    members = product_ref.shape[0] // 2
-    chips = members // 2
-    core = lax.axis_index("core")
-    values = inverse(
-        [product_ref[:members, :], product_ref[members:, :]],
-        back,
-        last,
-        cos_ref[...],
-        sin_ref[...],
-    )
-    for part in range(2):
-        even = values[:chips, part * stride : (part + 1) * stride]
-        odd = values[chips:, part * stride : (part + 1) * stride]
-        rows = slice(part * chips, (part + 1) * chips)
-        kept_ref[rows, :] = jnp.where(core == 0, even, odd)
-        handed_ref[rows, :] = jnp.where(core == 0, odd, even)
+        rows = slice(row + part * chips, row + (part + 1) * chips)
+        mine, other = kept_ref[rows, :], handed_ref[rows, :]
+        first.append(jnp.where(even_core, mine, other))
+        second.append(jnp.where(even_core, other, mine))
+    return first + second
+
+
+def slots_kernel(kept_ref, handed_ref, out_ref):
+    chips = out_ref.shape[0] // 4
+    for quarter, block in enumerate(by_quarter(kept_ref, handed_ref, 0, chips)):
+        out_ref[quarter * chips : (quarter + 1) * chips, :] = block
 
 
 def merge_kernel(kept_ref, handed_ref, pieces_ref, out_ref):
-    first = lax.axis_index("core") == 0
-    source = lax.axis_index("rep") // 2
     chips = out_ref.shape[0] // 5
-    for part in range(2):
-        mine = kept_ref[part * chips : (part + 1) * chips, :]
-        other = handed_ref[part * chips : (part + 1) * chips, :]
-        out_ref[pl.ds(part, chips, stride=5), :] = jnp.where(first, mine, other)
-        out_ref[pl.ds(2 + part, chips, stride=5), :] = jnp.where(first, other, mine)
-    total = None
-    for member in range(4):
-        start = pl.multiple_of((2 * member + source) * chips, chips)
-        piece = pieces_ref[pl.ds(start, chips), :]
-        total = piece if total is None else total + piece
+    for quarter, block in enumerate(by_quarter(kept_ref, handed_ref, 2 * chips, chips)):
+        out_ref[pl.ds(quarter, chips, stride=5), :] = block
+    total = pieces_ref[:chips, :]
+    for member in range(1, 4):
+        total = total + pieces_ref[member * chips : (member + 1) * chips, :]
     out_ref[pl.ds(4, chips, stride=5), :] = total
 
 
-def last_kernel(returned_ref, grad_ref, gate_ref, skip_ref, input_ref, filter_ref):
+def last_kernel(returned_ref, skipped_ref, input_ref, filter_ref):
     chips = returned_ref.shape[0] // 5
     filter_ref[...] = returned_ref[pl.ds(4, chips, stride=5), :]
     rows = [returned_ref[pl.ds(quarter, chips, stride=5), :] for quarter in range(4)]
-    gated = grad_ref[...].astype(jnp.float32) * gate_ref[...].astype(jnp.float32)
-    total = jnp.concatenate(rows, axis=0).T + gated * skip_ref[...]
+    total = jnp.concatenate(rows, axis=0).T + skipped_ref[...]
     input_ref[...] = total.astype(jnp.bfloat16)
 
 
@@ -188,26 +174,24 @@
     members = lax.axis_size(("chip", "core"))
     stride, channels = filter_param.shape
     f32 = jnp.float32
-    packed = pl.pallas_call(pack_kernel, out_shape=pltpu.VMEM((members * 6, stride), f32))(
-        inputs[0], out_grad[0], out_gate[0], filter_param
-    )
+    packed, skipped = pl.pallas_call(
+        pack_kernel,
+        out_shape=[pltpu.VMEM((members * 6, stride), f32), pltpu.VMEM((stride, channels), f32)],
+    )(inputs[0], out_grad[0], out_gate[0], filter_param, skip_gain[None, :])
     spread = exchange(packed, ("chip", "core"))
     constants = [near(jnp.asarray(table)) for table in tables(members, stride)]
-    slots, products = pl.pallas_call(
-        filter_side_kernel,
-        out_shape=[
-            pltpu.VMEM((members * 4, stride), f32),
-            pltpu.VMEM((members * 2, 2 * stride), f32),
-        ],
+    kept, handed = pl.pallas_call(
+        spectra_kernel, out_shape=[pltpu.VMEM((members * 2, stride), f32)] * 2
     )(near(spread), *constants)
-    pieces = exchange(slots, ("rep", "core"))
-    kept, handed = pl.pallas_call(
-        input_side_kernel, out_shape=[pltpu.VMEM((members, stride), f32)] * 2
-    )(near(products), *constants[:2], *constants[6:])
-    handed = lax.ppermute(handed, "core", [(0, 1), (1, 0)])
+    handed = near(lax.ppermute(handed, "core", [(0, 1), (1, 0)]))
+    kept = near(kept)
+    slots = pl.pallas_call(slots_kernel, out_shape=pltpu.VMEM((members * 2, stride), f32))(
+        kept, handed
+    )
+    pieces = exchange(slots, "rep")
     merged = pl.pallas_call(
         merge_kernel, out_shape=pltpu.VMEM((members // 2 * 5, stride), f32)
-    )(near(kept), near(handed), near(pieces))
+    )(kept, handed, near(pieces))
     returned = exchange(merged, "chip")
     input_part, filter_part = pl.pallas_call(
         last_kernel,
@@ -215,7 +199,7 @@
             jax.ShapeDtypeStruct((stride, channels), jnp.bfloat16),
             jax.ShapeDtypeStruct((channels // 4, stride), f32),
         ],
-    )(near(returned), near(out_grad[0]), near(out_gate[0]), near(skip_gain[None, :]))
+    )(near(returned), near(skipped))
     return (input_part[None], filter_part.T)
 
 

time: 79.9 us -> 78 us (0.976); the launches traced: 79.4 us -> 76.6 us
  blocking collectives: 58.7 us -> 67.4 us
  waiting for transfers between devices: 6.24 us -> 0.96 us
  starting transfers between devices: 8.51 us -> 3.96 us
  Pallas kernels: 4.41 us -> 3.49 us
    all_to_all x2 -> x3, blocking collectives: 58.7 us -> 67.4 us  [exchange(): wide = lax.all_to_all(wide, axis, split_axis=0, concat_axis=0, tiled=True)]
    all_to_all x1 -> x0, starting transfers between devices: 6.59 us -> none  [exchange(): wide = lax.all_to_all(wide, axis, split_axis=0, concat_axis=0, tiled=True)]
    all_to_all x1 -> x0, waiting for transfers between devices: 5.02 us -> none  [exchange(): wide = lax.all_to_all(wide, axis, split_axis=0, concat_axis=0, tiled=True)]
    ppermute x1, starting transfers between devices: 1.92 us -> 3.96 us  [local(): handed = near(lax.ppermute(handed, 'core', [(0, 1), (1, 0)]))]
    pallas_call x3, Pallas kernels: 3.66 us -> 2.74 us  [the longest x1 1.55 us: local(): pl.pallas_call(spectra_kernel, out_shape=[pltpu.VMEM((members * 2, stride...]
  transfers between devices with their start and end apart: 2 -> 1, of which waited for: 2 -> 1; matrix products, arithmetic and copies ran while one was open for 0% -> 0% of each run, Pallas kernels for 1% -> 0%
where the time goes in v8:
time: 78 us; the launch traced here: 76.6 us
  blocking collectives  67.4 us (86%)
  starting transfers between devices  3.96 us (5%)
  Pallas kernels  3.49 us (4%)
  waiting for transfers between devices  0.96 us (1%)
  between operations  0.8 us (1%)
    all_to_all x3, blocking collectives, exchange(): wide = lax.all_to_all(wide, axis, split_axis=0, concat_axis=0, tiled=True)  67.4 us
    ppermute x1, starting transfers between devices, local(): handed = near(lax.ppermute(handed, 'core', [(0, 1), (1, 0)]))  3.96 us
  transfers between devices with their start and end apart: 1, of which 1 were waited for; matrix products, arithmetic and copies ran while one was open for 0% of the time, Pallas kernels for 0%

profile of v8, /device:TPU:1, one launch (start us, length us, event | category | flops | bytes accessed | tf_op | source)
XLA Modules:
  0.0 76.6 jit_solution(14646749694629552122)
XLA Ops:
  0.6 0.0 copy-start.8
  0.6 0.0 copy-start.9
  0.7 1.2 %shard_map.158 = (f32[768,128]{1,0:T(8,128)S(1)}, f32[128,256]{1,0:T(8,128)S(1)}) custom-call(bf16[128,256]{1,0:T(8,128)(2,1)} %bitcast.18, bf16[128,256]{1,0:T(8,128)(2,1)} %bitcast.19, bf16[128,256]{1,0:T(8,128)(2,1)} %bitcast.20, f32[128,256]{1,0:T(8,128)} %filter_ref.1, f32[1,256]{1,0:T(1,128)} %bitcast.21), custom_call_target="tpu_custom_call" | custom-call | tf_op jit(solution)/shard_map/pallas_call | solution.py:177
  1.8 0.0 copy-start
  1.8 0.0 copy-start.1
  1.9 0.0 copy-start.2
  1.9 0.0 copy-start.3
  1.9 0.0 copy-start.4
  1.9 0.0 copy-start.5
  1.9 0.0 copy-start.6
  1.9 0.0 copy-start.7
  1.9 40.8 %all_to_all.15 = f32[128,1,768]{2,1,0:T(1,128)S(1)} all-to-all(f32[128,1,768]{2,1,0:T(1,128)S(1)} %bitcast.17), channel_id=1, replica_groups=mesh['rep'=4,'chip'=64,'core'=2] {'chip','core'}, dimensions={0} | all-to-all | bytes 786432 | tf_op jit(solution)/shard_map/all_to_all | solution.py:165
  42.8 0.0 copy-done.8
  42.8 0.0 copy-done.9
  42.8 0.0 copy-done
  42.8 0.0 copy-done.1
  42.8 0.0 copy-done.2
  42.8 0.0 copy-done.3
  42.8 0.0 copy-done.4
  42.8 0.0 copy-done.5
  42.8 0.0 copy-done.6
  42.8 0.0 copy-done.7
  42.8 1.6 %shard_map.159 = (f32[256,128]{1,0:T(8,128)S(1)}, f32[256,128]{1,0:T(8,128)S(1)}) custom-call(f32[768,128]{1,0:T(8,128)S(1)} %bitcast.12, f32[128,128]{1,0:T(8,128)S(1)} %copy-done.9, f32[128,128]{1,0:T(8,128)S(1)} %copy-done.8, bf16[256,128]{1,0:T(8,128)(2,1)S(1)} %copy-done.7, bf16[256,128]{1,0:T(8,128)(2,1)S(1)} %copy-done.6, ...), custom_call_target="tpu_custom_call" | custom-call | tf_op jit(solution)/shard_map/pallas_call | solution.py:183
  44.4 4.0 %collective-permute-start = (f32[256,128]{1,0:T(8,128)S(1)}, f32[256,128]{1,0:T(8,128)S(1)}, u32[]{:S(2)}, u32[]{:S(2)}) collective-permute-start(f32[256,128]{1,0:T(8,128)S(1)} %get-tuple-element.10), channel_id=1, source_target_pairs={{0,1},{1,0},{2,3},{3,2},{4,5},{5,4},{6,7},{7,6},{8,9},{9,8},{10,11... | collective-permute-start | bytes 393224 | tf_op jit(solution)/shard_map/ppermute | solution.py:186
  48.4 1.0 %collective-permute-done.handed_ref = f32[256,128]{1,0:T(8,128)S(1)} collective-permute-done((f32[256,128]{1,0:T(8,128)S(1)}, f32[256,128]{1,0:T(8,128)S(1)}, u32[]{:S(2)}, u32[]{:S(2)}) %collective-permute-start) | collective-permute-done | bytes 131104 | tf_op jit(solution)/shard_map/ppermute | solution.py:186
  49.3 8.8 %all_to_all.16 = f32[4,1,8192]{2,1,0:T(1,128)S(1)} all-to-all(f32[4,1,8192]{2,1,0:T(1,128)S(1)} %bitcast.16), channel_id=1, replica_groups=mesh['rep'=4,'chip'=64,'core'=2] {'rep'}, dimensions={0} | all-to-all | bytes 262144 | tf_op jit(solution)/shard_map/all_to_all | solution.py:165
  58.2 17.7 %all_to_all.17 = f32[64,1,640]{2,1,0:T(1,128)S(1)} all-to-all(f32[64,1,640]{2,1,0:T(1,128)S(1)} %bitcast.14), channel_id=1, replica_groups=mesh['rep'=4,'chip'=64,'core'=2] {'chip'}, dimensions={0} | all-to-all | bytes 327680 | tf_op jit(solution)/shard_map/all_to_all | solution.py:165
  75.9 0.7 shard_map.162
  (2 shorter events, 0.0 us)
Async XLA Ops:
  0.6 42.1 %copy-start.8 = (f32[128,128]{1,0:T(8,128)S(1)}, f32[128,128]{1,0:T(8,128)}, u32[]{:S(2)}) copy-start(f32[128,128]{1,0:T(8,128)} %constant.21.clone.sin_ref) | copy-start | bytes 196612
  0.6 42.1 %copy-start.9 = (f32[128,128]{1,0:T(8,128)S(1)}, f32[128,128]{1,0:T(8,128)}, u32[]{:S(2)}) copy-start(f32[128,128]{1,0:T(8,128)} %constant.20.clone.cos_ref) | copy-start | bytes 196612
  1.8 40.9 %copy-start = (bf16[256,256]{1,0:T(8,128)(2,1)S(1)}, bf16[256,256]{1,0:T(8,128)(2,1)}, u32[]{:S(2)}) copy-start(bf16[256,256]{1,0:T(8,128)(2,1)} %constant.27.clone.refs_5_) | copy-start | bytes 393220
  1.8 40.9 %copy-start.1 = (bf16[256,256]{1,0:T(8,128)(2,1)S(1)}, bf16[256,256]{1,0:T(8,128)(2,1)}, u32[]{:S(2)}) copy-start(bf16[256,256]{1,0:T(8,128)(2,1)} %constant.26.clone.refs_4_) | copy-start | bytes 393220
  1.9 40.9 %copy-start.2 = (bf16[256,256]{1,0:T(8,128)(2,1)S(1)}, bf16[256,256]{1,0:T(8,128)(2,1)}, u32[]{:S(2)}) copy-start(bf16[256,256]{1,0:T(8,128)(2,1)} %constant.25.clone.refs_3_) | copy-start | bytes 393220
  1.9 40.9 %copy-start.3 = (bf16[256,256]{1,0:T(8,128)(2,1)S(1)}, bf16[256,256]{1,0:T(8,128)(2,1)}, u32[]{:S(2)}) copy-start(bf16[256,256]{1,0:T(8,128)(2,1)} %constant.24.clone.refs_2_) | copy-start | bytes 393220
  1.9 40.9 %copy-start.4 = (bf16[128,256]{1,0:T(8,128)(2,1)S(1)}, bf16[128,256]{1,0:T(8,128)(2,1)}, u32[]{:S(2)}) copy-start(bf16[128,256]{1,0:T(8,128)(2,1)} %constant.29.clone.refs_7_) | copy-start | bytes 196612
  1.9 40.9 %copy-start.5 = (bf16[128,256]{1,0:T(8,128)(2,1)S(1)}, bf16[128,256]{1,0:T(8,128)(2,1)}, u32[]{:S(2)}) copy-start(bf16[128,256]{1,0:T(8,128)(2,1)} %constant.28.clone.refs_6_) | copy-start | bytes 196612
  1.9 40.9 %copy-start.6 = (bf16[256,128]{1,0:T(8,128)(2,1)S(1)}, bf16[256,128]{1,0:T(8,128)(2,1)}, u32[]{:S(2)}) copy-start(bf16[256,128]{1,0:T(8,128)(2,1)} %constant.23.clone.refs_1_) | copy-start | bytes 196612
  1.9 40.9 %copy-start.7 = (bf16[256,128]{1,0:T(8,128)(2,1)S(1)}, bf16[256,128]{1,0:T(8,128)(2,1)}, u32[]{:S(2)}) copy-start(bf16[256,128]{1,0:T(8,128)(2,1)} %constant.22.clone.refs_0_) | copy-start | bytes 196612
  44.4 4.9 %collective-permute-start = (f32[256,128]{1,0:T(8,128)S(1)}, f32[256,128]{1,0:T(8,128)S(1)}, u32[]{:S(2)}, u32[]{:S(2)}) collective-permute-start(f32[256,128]{1,0:T(8,128)S(1)} %get-tuple-element.10), channel_id=1, source_target_pairs={{0,1},{1,0},{2,3},{3,2},{4,5},{5,4},{6,7},{7,6},{8,9},{9,8},{10,11... | collective-permute-start | bytes 393224 | tf_op jit(solution)/shard_map/ppermute | solution.py:186

commit v9 on v8

--- a/solution.py
+++ b/solution.py
@@ -28,7 +28,7 @@
 
 def tables(members, stride):
     padded = 2 * members * stride
-    t1 = np.arange(members)
+    t1 = np.arange(members).reshape(members // 2, 2).T.reshape(-1)
     t2 = np.arange(stride)
     odd = 2 * np.arange(members) + 1
     outer = 2.0 * np.pi / (4 * members) * (odd[:, None] * t1[None, :] % (4 * members))
@@ -38,8 +38,7 @@
     second = np.block([[np.cos(inner), -np.sin(inner)], [np.sin(inner), np.cos(inner)]])
     scale = 2.0 / padded / math.sqrt(members * stride)
     result = [np.asarray(np.cos(twist), np.float32), np.asarray(np.sin(twist), np.float32)]
-    last = np.concatenate([first.T[0::2], first.T[1::2]], axis=0) * scale
-    for table in (first, second, second.T, last):
+    for table in (first, second, second.T, first.T * scale):
         high = table.astype(jnp.bfloat16)
         result += [high, (table - high.astype(np.float64)).astype(jnp.bfloat16)]
     return result
@@ -53,8 +52,8 @@
     for index, signal in enumerate(signals):
         turned = signal.T
         for quarter in range(4):
-            row = 6 * (quarter // 2) + 2 * index + quarter % 2
-            out_ref[pl.ds(row, chips, stride=12), :] = turned[
+            row = 6 * chips * (quarter // 2) + 2 * index + quarter % 2
+            out_ref[pl.ds(row, chips, stride=6), :] = turned[
                 quarter * chips : (quarter + 1) * chips
             ]
 
@@ -178,7 +177,7 @@
         pack_kernel,
         out_shape=[pltpu.VMEM((members * 6, stride), f32), pltpu.VMEM((stride, channels), f32)],
     )(inputs[0], out_grad[0], out_gate[0], filter_param, skip_gain[None, :])
-    spread = exchange(packed, ("chip", "core"))
+    spread = exchange(packed, ("core", "chip"))
     constants = [near(jnp.asarray(table)) for table in tables(members, stride)]
     kept, handed = pl.pallas_call(
         spectra_kernel, out_shape=[pltpu.VMEM((members * 2, stride), f32)] * 2

time: 78 us -> 77.7 us (level)
  starting transfers between devices: 3.96 us -> 2.72 us
  blocking collectives: 67.4 us -> 68.3 us
    ppermute x1, starting transfers between devices: 3.96 us -> 2.72 us  [local(): handed = near(lax.ppermute(handed, 'core', [(0, 1), (1, 0)]))]
    all_to_all x3, blocking collectives: 67.4 us -> 68.3 us  [exchange(): wide = lax.all_to_all(wide, axis, split_axis=0, concat_axis=0, tiled=True)]
where the time goes in v9:
time: 77.7 us; the launch traced here: 76.3 us
  blocking collectives  68.3 us (88%)
  Pallas kernels  3.49 us (4%)
  starting transfers between devices  2.72 us (4%)
  waiting for transfers between devices  0.96 us (1%)
  between operations  0.8 us (1%)
    all_to_all x3, blocking collectives, exchange(): wide = lax.all_to_all(wide, axis, split_axis=0, concat_axis=0, tiled=True)  68.3 us
    ppermute x1, starting transfers between devices, local(): handed = near(lax.ppermute(handed, 'core', [(0, 1), (1, 0)]))  2.72 us
  transfers between devices with their start and end apart: 1, of which 1 were waited for; matrix products, arithmetic and copies ran while one was open for 0% of the time, Pallas kernels for 0%

profile of v9, /device:TPU:1, one launch (start us, length us, event | category | flops | bytes accessed | tf_op | source)
XLA Modules:
  0.0 76.3 jit_solution(73364706421431070)
XLA Ops:
  0.6 0.0 copy-start.8
  0.6 0.0 copy-start.9
  0.7 1.2 %shard_map.158 = (f32[768,128]{1,0:T(8,128)S(1)}, f32[128,256]{1,0:T(8,128)S(1)}) custom-call(bf16[128,256]{1,0:T(8,128)(2,1)} %bitcast.18, bf16[128,256]{1,0:T(8,128)(2,1)} %bitcast.19, bf16[128,256]{1,0:T(8,128)(2,1)} %bitcast.20, f32[128,256]{1,0:T(8,128)} %filter_ref.1, f32[1,256]{1,0:T(1,128)} %bitcast.21), custom_call_target="tpu_custom_call" | custom-call | tf_op jit(solution)/shard_map/pallas_call | solution.py:176
  1.8 0.0 copy-start
  1.8 0.0 copy-start.1
  1.9 0.0 copy-start.2
  1.9 0.0 copy-start.3
  1.9 0.0 copy-start.4
  1.9 0.0 copy-start.5
  1.9 0.0 copy-start.6
  1.9 0.0 copy-start.7
  1.9 41.2 %all_to_all.15 = f32[128,1,768]{2,1,0:T(1,128)S(1)} all-to-all(f32[128,1,768]{2,1,0:T(1,128)S(1)} %bitcast.17), channel_id=1, replica_groups=mesh['rep'=4,'chip'=64,'core'=2] {'core','chip'}, dimensions={0} | all-to-all | bytes 786432 | tf_op jit(solution)/shard_map/all_to_all | solution.py:164
  43.1 0.0 copy-done.8
  43.1 0.0 copy-done.9
  43.1 0.0 copy-done
  43.2 0.0 copy-done.1
  43.2 0.0 copy-done.2
  43.2 0.0 copy-done.3
  43.2 0.0 copy-done.4
  43.2 0.0 copy-done.5
  43.2 0.0 copy-done.6
  43.2 0.0 copy-done.7
  43.2 1.6 %shard_map.159 = (f32[256,128]{1,0:T(8,128)S(1)}, f32[256,128]{1,0:T(8,128)S(1)}) custom-call(f32[768,128]{1,0:T(8,128)S(1)} %bitcast.12, f32[128,128]{1,0:T(8,128)S(1)} %copy-done.9, f32[128,128]{1,0:T(8,128)S(1)} %copy-done.8, bf16[256,128]{1,0:T(8,128)(2,1)S(1)} %copy-done.7, bf16[256,128]{1,0:T(8,128)(2,1)S(1)} %copy-done.6, ...), custom_call_target="tpu_custom_call" | custom-call | tf_op jit(solution)/shard_map/pallas_call | solution.py:182
  44.8 2.7 %collective-permute-start = (f32[256,128]{1,0:T(8,128)S(1)}, f32[256,128]{1,0:T(8,128)S(1)}, u32[]{:S(2)}, u32[]{:S(2)}) collective-permute-start(f32[256,128]{1,0:T(8,128)S(1)} %get-tuple-element.10), channel_id=1, source_target_pairs={{0,1},{1,0},{2,3},{3,2},{4,5},{5,4},{6,7},{7,6},{8,9},{9,8},{10,11... | collective-permute-start | bytes 393224 | tf_op jit(solution)/shard_map/ppermute | solution.py:185
  47.5 1.0 %collective-permute-done.handed_ref = f32[256,128]{1,0:T(8,128)S(1)} collective-permute-done((f32[256,128]{1,0:T(8,128)S(1)}, f32[256,128]{1,0:T(8,128)S(1)}, u32[]{:S(2)}, u32[]{:S(2)}) %collective-permute-start) | collective-permute-done | bytes 131104 | tf_op jit(solution)/shard_map/ppermute | solution.py:185
  48.5 8.9 %all_to_all.16 = f32[4,1,8192]{2,1,0:T(1,128)S(1)} all-to-all(f32[4,1,8192]{2,1,0:T(1,128)S(1)} %bitcast.16), channel_id=1, replica_groups=mesh['rep'=4,'chip'=64,'core'=2] {'rep'}, dimensions={0} | all-to-all | bytes 262144 | tf_op jit(solution)/shard_map/all_to_all | solution.py:164
  57.4 18.2 %all_to_all.17 = f32[64,1,640]{2,1,0:T(1,128)S(1)} all-to-all(f32[64,1,640]{2,1,0:T(1,128)S(1)} %bitcast.14), channel_id=1, replica_groups=mesh['rep'=4,'chip'=64,'core'=2] {'chip'}, dimensions={0} | all-to-all | bytes 327680 | tf_op jit(solution)/shard_map/all_to_all | solution.py:164
  75.6 0.7 shard_map.162
  (2 shorter events, 0.0 us)
Async XLA Ops:
  0.6 42.5 %copy-start.8 = (f32[128,128]{1,0:T(8,128)S(1)}, f32[128,128]{1,0:T(8,128)}, u32[]{:S(2)}) copy-start(f32[128,128]{1,0:T(8,128)} %constant.21.clone.sin_ref) | copy-start | bytes 196612
  0.6 42.5 %copy-start.9 = (f32[128,128]{1,0:T(8,128)S(1)}, f32[128,128]{1,0:T(8,128)}, u32[]{:S(2)}) copy-start(f32[128,128]{1,0:T(8,128)} %constant.20.clone.cos_ref) | copy-start | bytes 196612
  1.8 41.3 %copy-start = (bf16[256,256]{1,0:T(8,128)(2,1)S(1)}, bf16[256,256]{1,0:T(8,128)(2,1)}, u32[]{:S(2)}) copy-start(bf16[256,256]{1,0:T(8,128)(2,1)} %constant.27.clone.refs_5_) | copy-start | bytes 393220
  1.8 41.3 %copy-start.1 = (bf16[256,256]{1,0:T(8,128)(2,1)S(1)}, bf16[256,256]{1,0:T(8,128)(2,1)}, u32[]{:S(2)}) copy-start(bf16[256,256]{1,0:T(8,128)(2,1)} %constant.26.clone.refs_4_) | copy-start | bytes 393220
  1.9 41.3 %copy-start.2 = (bf16[256,256]{1,0:T(8,128)(2,1)S(1)}, bf16[256,256]{1,0:T(8,128)(2,1)}, u32[]{:S(2)}) copy-start(bf16[256,256]{1,0:T(8,128)(2,1)} %constant.25.clone.refs_3_) | copy-start | bytes 393220
  1.9 41.3 %copy-start.3 = (bf16[256,256]{1,0:T(8,128)(2,1)S(1)}, bf16[256,256]{1,0:T(8,128)(2,1)}, u32[]{:S(2)}) copy-start(bf16[256,256]{1,0:T(8,128)(2,1)} %constant.24.clone.refs_2_) | copy-start | bytes 393220
  1.9 41.3 %copy-start.4 = (bf16[128,256]{1,0:T(8,128)(2,1)S(1)}, bf16[128,256]{1,0:T(8,128)(2,1)}, u32[]{:S(2)}) copy-start(bf16[128,256]{1,0:T(8,128)(2,1)} %constant.29.clone.refs_7_) | copy-start | bytes 196612
  1.9 41.3 %copy-start.5 = (bf16[128,256]{1,0:T(8,128)(2,1)S(1)}, bf16[128,256]{1,0:T(8,128)(2,1)}, u32[]{:S(2)}) copy-start(bf16[128,256]{1,0:T(8,128)(2,1)} %constant.28.clone.refs_6_) | copy-start | bytes 196612
  1.9 41.3 %copy-start.6 = (bf16[256,128]{1,0:T(8,128)(2,1)S(1)}, bf16[256,128]{1,0:T(8,128)(2,1)}, u32[]{:S(2)}) copy-start(bf16[256,128]{1,0:T(8,128)(2,1)} %constant.23.clone.refs_1_) | copy-start | bytes 196612
  1.9 41.3 %copy-start.7 = (bf16[256,128]{1,0:T(8,128)(2,1)S(1)}, bf16[256,128]{1,0:T(8,128)(2,1)}, u32[]{:S(2)}) copy-start(bf16[256,128]{1,0:T(8,128)(2,1)} %constant.22.clone.refs_0_) | copy-start | bytes 196612
  44.8 3.7 %collective-permute-start = (f32[256,128]{1,0:T(8,128)S(1)}, f32[256,128]{1,0:T(8,128)S(1)}, u32[]{:S(2)}, u32[]{:S(2)}) collective-permute-start(f32[256,128]{1,0:T(8,128)S(1)} %get-tuple-element.10), channel_id=1, source_target_pairs={{0,1},{1,0},{2,3},{3,2},{4,5},{5,4},{6,7},{7,6},{8,9},{9,8},{10,11... | collective-permute-start | bytes 393224 | tf_op jit(solution)/shard_map/ppermute | solution.py:185

commit v10 on v8

--- a/solution.py
+++ b/solution.py
@@ -16,14 +16,22 @@
     return high, (values - high.astype(jnp.float32)).astype(jnp.bfloat16)
 
 
-def product(left, right):
-    def dot(one, other):
-        return jnp.dot(one, other, preferred_element_type=jnp.float32)
-
-    total = dot(left[0], right[0])
-    if right[1] is not None:
-        total = total + dot(left[0], right[1])
-    return total + dot(left[1], right[0])
+def dot(left, right):
+    return jnp.dot(left, right, preferred_element_type=jnp.float32)
+
+
+def values_by_table(values, table):
+    rows = values.shape[0]
+    high, low = halves(values)
+    both = dot(jnp.concatenate([high, low], axis=0), table[0])
+    return both[:rows] + both[rows:] + dot(high, table[1])
+
+
+def table_by_values(table, high, low):
+    rows = table[0].shape[0]
+    both = dot(jnp.concatenate(table, axis=0), high)
+    total = both[:rows] + both[rows:]
+    return total if low is None else total + dot(table[0], low)
 
 
 def tables(members, stride):
@@ -63,19 +71,19 @@
     stride = signal_ref.shape[1]
     members = signal_ref.shape[0] // 6
     signals = [signal_ref[pl.ds(row, members, stride=6), :] for row in range(6)]
-    partial = []
+    parts = []
     for row in range(0, 6, 2):
         pair = jnp.concatenate(signals[row : row + 2], axis=1)
         sides = (pair.astype(jnp.bfloat16), None) if row == 2 else halves(pair)
-        both = product(first, sides)
-        partial += [both[:, :stride], both[:, stride:]]
-    parts = []
-    for value in partial:
-        real, imag = value[:members], value[members:]
-        turned = jnp.concatenate(
-            [real * cosine + imag * sine, imag * cosine - real * sine], axis=1
-        )
-        parts.append(product(halves(turned), second))
+        both = table_by_values(first, *sides)
+        turned = []
+        for value in (both[:, :stride], both[:, stride:]):
+            real, imag = value[:members], value[members:]
+            turned.append(
+                jnp.concatenate([real * cosine + imag * sine, imag * cosine - real * sine], axis=1)
+            )
+        spectrum = values_by_table(jnp.concatenate(turned, axis=0), second)
+        parts += [spectrum[:members], spectrum[members:]]
     return parts
 
 
@@ -89,15 +97,16 @@
 
 
 def inverse(values, back, last, cosine, sine):
+    members, stride = cosine.shape
+    restored = values_by_table(jnp.concatenate(values, axis=0), back)
     columns = []
-    for value in values:
-        restored = product(halves(value), back)
-        stride = restored.shape[1] // 2
-        real, imag = restored[:, :stride], restored[:, stride:]
+    for start in (0, members):
+        real = restored[start : start + members, :stride]
+        imag = restored[start : start + members, stride:]
         columns.append(
             jnp.concatenate([real * cosine - imag * sine, imag * cosine + real * sine], axis=0)
         )
-    return product(last, halves(jnp.concatenate(columns, axis=1)))
+    return table_by_values(last, *halves(jnp.concatenate(columns, axis=1)))
 
 
 def pairs_of(refs):

time: 78 us -> 78.3 us (level)
  no operation moved by 1% of the time
where the time goes in v10:
time: 78.3 us; the launch traced here: 77 us
  blocking collectives  67.4 us (86%)
  starting transfers between devices  3.95 us (5%)
  Pallas kernels  3.8 us (5%)
  waiting for transfers between devices  0.96 us (1%)
  between operations  0.8 us (1%)
    all_to_all x3, blocking collectives, exchange(): wide = lax.all_to_all(wide, axis, split_axis=0, concat_axis=0, tiled=True)  67.4 us
    ppermute x1, starting transfers between devices, local(): handed = near(lax.ppermute(handed, 'core', [(0, 1), (1, 0)]))  3.95 us
    pallas_call x1, Pallas kernels, local(): pl.pallas_call(spectra_kernel, out_shape=[pltpu.VMEM((members * 2, stride...  1.87 us
  transfers between devices with their start and end apart: 1, of which 1 were waited for; matrix products, arithmetic and copies ran while one was open for 0% of the time, Pallas kernels for 0%

profile of v10, /device:TPU:1, one launch (start us, length us, event | category | flops | bytes accessed | tf_op | source)
XLA Modules:
  0.0 77.0 jit_solution(11073373154895246301)
XLA Ops:
  0.6 0.0 copy-start.8
  0.6 0.0 copy-start.9
  0.7 1.2 %shard_map.158 = (f32[768,128]{1,0:T(8,128)S(1)}, f32[128,256]{1,0:T(8,128)S(1)}) custom-call(bf16[128,256]{1,0:T(8,128)(2,1)} %bitcast.18, bf16[128,256]{1,0:T(8,128)(2,1)} %bitcast.19, bf16[128,256]{1,0:T(8,128)(2,1)} %bitcast.20, f32[128,256]{1,0:T(8,128)} %filter_ref.1, f32[1,256]{1,0:T(1,128)} %bitcast.21), custom_call_target="tpu_custom_call" | custom-call | tf_op jit(solution)/shard_map/pallas_call | solution.py:186
  1.8 0.0 copy-start
  1.8 0.0 copy-start.1
  1.9 0.0 copy-start.2
  1.9 0.0 copy-start.3
  1.9 0.0 copy-start.4
  1.9 0.0 copy-start.5
  1.9 0.0 copy-start.6
  1.9 0.0 copy-start.7
  1.9 40.8 %all_to_all.15 = f32[128,1,768]{2,1,0:T(1,128)S(1)} all-to-all(f32[128,1,768]{2,1,0:T(1,128)S(1)} %bitcast.17), channel_id=1, replica_groups=mesh['rep'=4,'chip'=64,'core'=2] {'chip','core'}, dimensions={0} | all-to-all | bytes 786432 | tf_op jit(solution)/shard_map/all_to_all | solution.py:174
  42.8 0.0 copy-done.8
  42.8 0.0 copy-done.9
  42.8 0.0 copy-done
  42.8 0.0 copy-done.1
  42.8 0.0 copy-done.2
  42.8 0.0 copy-done.3
  42.8 0.0 copy-done.4
  42.8 0.0 copy-done.5
  42.8 0.0 copy-done.6
  42.8 0.0 copy-done.7
  42.8 1.9 %shard_map.159 = (f32[256,128]{1,0:T(8,128)S(1)}, f32[256,128]{1,0:T(8,128)S(1)}) custom-call(f32[768,128]{1,0:T(8,128)S(1)} %bitcast.12, f32[128,128]{1,0:T(8,128)S(1)} %copy-done.9, f32[128,128]{1,0:T(8,128)S(1)} %copy-done.8, bf16[256,128]{1,0:T(8,128)(2,1)S(1)} %copy-done.7, bf16[256,128]{1,0:T(8,128)(2,1)S(1)} %copy-done.6, ...), custom_call_target="tpu_custom_call" | custom-call | tf_op jit(solution)/shard_map/pallas_call | solution.py:192
  44.7 3.9 %collective-permute-start = (f32[256,128]{1,0:T(8,128)S(1)}, f32[256,128]{1,0:T(8,128)S(1)}, u32[]{:S(2)}, u32[]{:S(2)}) collective-permute-start(f32[256,128]{1,0:T(8,128)S(1)} %get-tuple-element.10), channel_id=1, source_target_pairs={{0,1},{1,0},{2,3},{3,2},{4,5},{5,4},{6,7},{7,6},{8,9},{9,8},{10,11... | collective-permute-start | bytes 393224 | tf_op jit(solution)/shard_map/ppermute | solution.py:195
  48.7 1.0 %collective-permute-done.handed_ref = f32[256,128]{1,0:T(8,128)S(1)} collective-permute-done((f32[256,128]{1,0:T(8,128)S(1)}, f32[256,128]{1,0:T(8,128)S(1)}, u32[]{:S(2)}, u32[]{:S(2)}) %collective-permute-start) | collective-permute-done | bytes 131104 | tf_op jit(solution)/shard_map/ppermute | solution.py:195
  49.7 8.9 %all_to_all.16 = f32[4,1,8192]{2,1,0:T(1,128)S(1)} all-to-all(f32[4,1,8192]{2,1,0:T(1,128)S(1)} %bitcast.16), channel_id=1, replica_groups=mesh['rep'=4,'chip'=64,'core'=2] {'rep'}, dimensions={0} | all-to-all | bytes 262144 | tf_op jit(solution)/shard_map/all_to_all | solution.py:174
  58.5 17.7 %all_to_all.17 = f32[64,1,640]{2,1,0:T(1,128)S(1)} all-to-all(f32[64,1,640]{2,1,0:T(1,128)S(1)} %bitcast.14), channel_id=1, replica_groups=mesh['rep'=4,'chip'=64,'core'=2] {'chip'}, dimensions={0} | all-to-all | bytes 327680 | tf_op jit(solution)/shard_map/all_to_all | solution.py:174
  76.2 0.7 shard_map.162
  (2 shorter events, 0.0 us)
Async XLA Ops:
  0.6 42.1 %copy-start.8 = (f32[128,128]{1,0:T(8,128)S(1)}, f32[128,128]{1,0:T(8,128)}, u32[]{:S(2)}) copy-start(f32[128,128]{1,0:T(8,128)} %constant.21.clone.sin_ref) | copy-start | bytes 196612
  0.6 42.1 %copy-start.9 = (f32[128,128]{1,0:T(8,128)S(1)}, f32[128,128]{1,0:T(8,128)}, u32[]{:S(2)}) copy-start(f32[128,128]{1,0:T(8,128)} %constant.20.clone.cos_ref) | copy-start | bytes 196612
  1.8 40.9 %copy-start = (bf16[256,256]{1,0:T(8,128)(2,1)S(1)}, bf16[256,256]{1,0:T(8,128)(2,1)}, u32[]{:S(2)}) copy-start(bf16[256,256]{1,0:T(8,128)(2,1)} %constant.27.clone.refs_5_) | copy-start | bytes 393220
  1.8 40.9 %copy-start.1 = (bf16[256,256]{1,0:T(8,128)(2,1)S(1)}, bf16[256,256]{1,0:T(8,128)(2,1)}, u32[]{:S(2)}) copy-start(bf16[256,256]{1,0:T(8,128)(2,1)} %constant.26.clone.refs_4_) | copy-start | bytes 393220
  1.9 40.9 %copy-start.2 = (bf16[256,256]{1,0:T(8,128)(2,1)S(1)}, bf16[256,256]{1,0:T(8,128)(2,1)}, u32[]{:S(2)}) copy-start(bf16[256,256]{1,0:T(8,128)(2,1)} %constant.25.clone.refs_3_) | copy-start | bytes 393220
  1.9 40.9 %copy-start.3 = (bf16[256,256]{1,0:T(8,128)(2,1)S(1)}, bf16[256,256]{1,0:T(8,128)(2,1)}, u32[]{:S(2)}) copy-start(bf16[256,256]{1,0:T(8,128)(2,1)} %constant.24.clone.refs_2_) | copy-start | bytes 393220
  1.9 40.9 %copy-start.4 = (bf16[128,256]{1,0:T(8,128)(2,1)S(1)}, bf16[128,256]{1,0:T(8,128)(2,1)}, u32[]{:S(2)}) copy-start(bf16[128,256]{1,0:T(8,128)(2,1)} %constant.29.clone.refs_7_) | copy-start | bytes 196612
  1.9 40.9 %copy-start.5 = (bf16[128,256]{1,0:T(8,128)(2,1)S(1)}, bf16[128,256]{1,0:T(8,128)(2,1)}, u32[]{:S(2)}) copy-start(bf16[128,256]{1,0:T(8,128)(2,1)} %constant.28.clone.refs_6_) | copy-start | bytes 196612
  1.9 40.9 %copy-start.6 = (bf16[256,128]{1,0:T(8,128)(2,1)S(1)}, bf16[256,128]{1,0:T(8,128)(2,1)}, u32[]{:S(2)}) copy-start(bf16[256,128]{1,0:T(8,128)(2,1)} %constant.23.clone.refs_1_) | copy-start | bytes 196612
  1.9 40.9 %copy-start.7 = (bf16[256,128]{1,0:T(8,128)(2,1)S(1)}, bf16[256,128]{1,0:T(8,128)(2,1)}, u32[]{:S(2)}) copy-start(bf16[256,128]{1,0:T(8,128)(2,1)} %constant.22.clone.refs_0_) | copy-start | bytes 196612
  44.7 4.9 %collective-permute-start = (f32[256,128]{1,0:T(8,128)S(1)}, f32[256,128]{1,0:T(8,128)S(1)}, u32[]{:S(2)}, u32[]{:S(2)}) collective-permute-start(f32[256,128]{1,0:T(8,128)S(1)} %get-tuple-element.10), channel_id=1, source_target_pairs={{0,1},{1,0},{2,3},{3,2},{4,5},{5,4},{6,7},{7,6},{8,9},{9,8},{10,11... | collective-permute-start | bytes 393224 | tf_op jit(solution)/shard_map/ppermute | solution.py:195

commit v11 on v8

--- a/solution.py
+++ b/solution.py
@@ -112,15 +112,18 @@
     even_core = lax.axis_index("core") == 0
     cosine, sine = cos_ref[...], sin_ref[...]
     parts = spectra(signal_ref, first, second, cosine, sine)
+    last = [
+        jnp.where(even_core, half, jnp.concatenate([half[chips:], half[:chips]], axis=0))
+        for half in last
+    ]
     for index, other in enumerate((2, 4)):
         products = [correlated(parts[part], parts[other + part]) for part in range(2)]
         values = inverse(products, back, last, cosine, sine)
         for part in range(2):
-            even = values[:chips, part * stride : (part + 1) * stride]
-            odd = values[chips:, part * stride : (part + 1) * stride]
+            columns = slice(part * stride, (part + 1) * stride)
             rows = slice((2 * index + part) * chips, (2 * index + part + 1) * chips)
-            kept_ref[rows, :] = jnp.where(even_core, even, odd)
-            handed_ref[rows, :] = jnp.where(even_core, odd, even)
+            kept_ref[rows, :] = values[:chips, columns]
+            handed_ref[rows, :] = values[chips:, columns]
 
 
 def by_quarter(kept_ref, handed_ref, row, chips):

time: 78 us -> 78 us (level)
  no operation moved by 1% of the time
where the time goes in v11:
time: 78 us; the launch traced here: 76.6 us
  blocking collectives  67.4 us (86%)
  starting transfers between devices  3.95 us (5%)
  Pallas kernels  3.49 us (4%)
  waiting for transfers between devices  0.96 us (1%)
  between operations  0.8 us (1%)
    all_to_all x3, blocking collectives, exchange(): wide = lax.all_to_all(wide, axis, split_axis=0, concat_axis=0, tiled=True)  67.4 us
    ppermute x1, starting transfers between devices, local(): handed = near(lax.ppermute(handed, 'core', [(0, 1), (1, 0)]))  3.95 us
  transfers between devices with their start and end apart: 1, of which 1 were waited for; matrix products, arithmetic and copies ran while one was open for 0% of the time, Pallas kernels for 0%

profile of v11, /device:TPU:1, one launch (start us, length us, event | category | flops | bytes accessed | tf_op | source)
XLA Modules:
  0.0 76.6 jit_solution(13543052394445666123)
XLA Ops:
  0.6 0.0 copy-start.8
  0.6 0.0 copy-start.9
  0.7 1.2 %shard_map.158 = (f32[768,128]{1,0:T(8,128)S(1)}, f32[128,256]{1,0:T(8,128)S(1)}) custom-call(bf16[128,256]{1,0:T(8,128)(2,1)} %bitcast.18, bf16[128,256]{1,0:T(8,128)(2,1)} %bitcast.19, bf16[128,256]{1,0:T(8,128)(2,1)} %bitcast.20, f32[128,256]{1,0:T(8,128)} %filter_ref.1, f32[1,256]{1,0:T(1,128)} %bitcast.21), custom_call_target="tpu_custom_call" | custom-call | tf_op jit(solution)/shard_map/pallas_call | solution.py:180
  1.8 0.0 copy-start
  1.8 0.0 copy-start.1
  1.9 0.0 copy-start.2
  1.9 0.0 copy-start.3
  1.9 0.0 copy-start.4
  1.9 0.0 copy-start.5
  1.9 0.0 copy-start.6
  1.9 0.0 copy-start.7
  1.9 40.8 %all_to_all.15 = f32[128,1,768]{2,1,0:T(1,128)S(1)} all-to-all(f32[128,1,768]{2,1,0:T(1,128)S(1)} %bitcast.17), channel_id=1, replica_groups=mesh['rep'=4,'chip'=64,'core'=2] {'chip','core'}, dimensions={0} | all-to-all | bytes 786432 | tf_op jit(solution)/shard_map/all_to_all | solution.py:168
  42.8 0.0 copy-done.8
  42.8 0.0 copy-done.9
  42.8 0.0 copy-done
  42.8 0.0 copy-done.1
  42.8 0.0 copy-done.2
  42.8 0.0 copy-done.3
  42.8 0.0 copy-done.4
  42.8 0.0 copy-done.5
  42.8 0.0 copy-done.6
  42.8 0.0 copy-done.7
  42.8 1.6 %shard_map.159 = (f32[256,128]{1,0:T(8,128)S(1)}, f32[256,128]{1,0:T(8,128)S(1)}) custom-call(f32[768,128]{1,0:T(8,128)S(1)} %bitcast.12, f32[128,128]{1,0:T(8,128)S(1)} %copy-done.9, f32[128,128]{1,0:T(8,128)S(1)} %copy-done.8, bf16[256,128]{1,0:T(8,128)(2,1)S(1)} %copy-done.7, bf16[256,128]{1,0:T(8,128)(2,1)S(1)} %copy-done.6, ...), custom_call_target="tpu_custom_call" | custom-call | tf_op jit(solution)/shard_map/pallas_call | solution.py:186
  44.4 4.0 %collective-permute-start = (f32[256,128]{1,0:T(8,128)S(1)}, f32[256,128]{1,0:T(8,128)S(1)}, u32[]{:S(2)}, u32[]{:S(2)}) collective-permute-start(f32[256,128]{1,0:T(8,128)S(1)} %get-tuple-element.10), channel_id=1, source_target_pairs={{0,1},{1,0},{2,3},{3,2},{4,5},{5,4},{6,7},{7,6},{8,9},{9,8},{10,11... | collective-permute-start | bytes 393224 | tf_op jit(solution)/shard_map/ppermute | solution.py:189
  48.4 1.0 %collective-permute-done.handed_ref = f32[256,128]{1,0:T(8,128)S(1)} collective-permute-done((f32[256,128]{1,0:T(8,128)S(1)}, f32[256,128]{1,0:T(8,128)S(1)}, u32[]{:S(2)}, u32[]{:S(2)}) %collective-permute-start) | collective-permute-done | bytes 131104 | tf_op jit(solution)/shard_map/ppermute | solution.py:189
  49.3 8.8 %all_to_all.16 = f32[4,1,8192]{2,1,0:T(1,128)S(1)} all-to-all(f32[4,1,8192]{2,1,0:T(1,128)S(1)} %bitcast.16), channel_id=1, replica_groups=mesh['rep'=4,'chip'=64,'core'=2] {'rep'}, dimensions={0} | all-to-all | bytes 262144 | tf_op jit(solution)/shard_map/all_to_all | solution.py:168
  58.2 17.7 %all_to_all.17 = f32[64,1,640]{2,1,0:T(1,128)S(1)} all-to-all(f32[64,1,640]{2,1,0:T(1,128)S(1)} %bitcast.14), channel_id=1, replica_groups=mesh['rep'=4,'chip'=64,'core'=2] {'chip'}, dimensions={0} | all-to-all | bytes 327680 | tf_op jit(solution)/shard_map/all_to_all | solution.py:168
  75.9 0.7 shard_map.162
  (2 shorter events, 0.0 us)
Async XLA Ops:
  0.6 42.1 %copy-start.8 = (f32[128,128]{1,0:T(8,128)S(1)}, f32[128,128]{1,0:T(8,128)}, u32[]{:S(2)}) copy-start(f32[128,128]{1,0:T(8,128)} %constant.21.clone.sin_ref) | copy-start | bytes 196612
  0.6 42.1 %copy-start.9 = (f32[128,128]{1,0:T(8,128)S(1)}, f32[128,128]{1,0:T(8,128)}, u32[]{:S(2)}) copy-start(f32[128,128]{1,0:T(8,128)} %constant.20.clone.cos_ref) | copy-start | bytes 196612
  1.8 40.9 %copy-start = (bf16[256,256]{1,0:T(8,128)(2,1)S(1)}, bf16[256,256]{1,0:T(8,128)(2,1)}, u32[]{:S(2)}) copy-start(bf16[256,256]{1,0:T(8,128)(2,1)} %constant.27.clone.refs_5_) | copy-start | bytes 393220
  1.8 40.9 %copy-start.1 = (bf16[256,256]{1,0:T(8,128)(2,1)S(1)}, bf16[256,256]{1,0:T(8,128)(2,1)}, u32[]{:S(2)}) copy-start(bf16[256,256]{1,0:T(8,128)(2,1)} %constant.26.clone.refs_4_) | copy-start | bytes 393220
  1.9 40.9 %copy-start.2 = (bf16[256,256]{1,0:T(8,128)(2,1)S(1)}, bf16[256,256]{1,0:T(8,128)(2,1)}, u32[]{:S(2)}) copy-start(bf16[256,256]{1,0:T(8,128)(2,1)} %constant.25.clone.refs_3_) | copy-start | bytes 393220
  1.9 40.9 %copy-start.3 = (bf16[256,256]{1,0:T(8,128)(2,1)S(1)}, bf16[256,256]{1,0:T(8,128)(2,1)}, u32[]{:S(2)}) copy-start(bf16[256,256]{1,0:T(8,128)(2,1)} %constant.24.clone.refs_2_) | copy-start | bytes 393220
  1.9 40.9 %copy-start.4 = (bf16[128,256]{1,0:T(8,128)(2,1)S(1)}, bf16[128,256]{1,0:T(8,128)(2,1)}, u32[]{:S(2)}) copy-start(bf16[128,256]{1,0:T(8,128)(2,1)} %constant.29.clone.refs_7_) | copy-start | bytes 196612
  1.9 40.9 %copy-start.5 = (bf16[128,256]{1,0:T(8,128)(2,1)S(1)}, bf16[128,256]{1,0:T(8,128)(2,1)}, u32[]{:S(2)}) copy-start(bf16[128,256]{1,0:T(8,128)(2,1)} %constant.28.clone.refs_6_) | copy-start | bytes 196612
  1.9 40.9 %copy-start.6 = (bf16[256,128]{1,0:T(8,128)(2,1)S(1)}, bf16[256,128]{1,0:T(8,128)(2,1)}, u32[]{:S(2)}) copy-start(bf16[256,128]{1,0:T(8,128)(2,1)} %constant.23.clone.refs_1_) | copy-start | bytes 196612
  1.9 40.9 %copy-start.7 = (bf16[256,128]{1,0:T(8,128)(2,1)S(1)}, bf16[256,128]{1,0:T(8,128)(2,1)}, u32[]{:S(2)}) copy-start(bf16[256,128]{1,0:T(8,128)(2,1)} %constant.22.clone.refs_0_) | copy-start | bytes 196612
  44.4 4.9 %collective-permute-start = (f32[256,128]{1,0:T(8,128)S(1)}, f32[256,128]{1,0:T(8,128)S(1)}, u32[]{:S(2)}, u32[]{:S(2)}) collective-permute-start(f32[256,128]{1,0:T(8,128)S(1)} %get-tuple-element.10), channel_id=1, source_target_pairs={{0,1},{1,0},{2,3},{3,2},{4,5},{5,4},{6,7},{7,6},{8,9},{9,8},{10,11... | collective-permute-start | bytes 393224 | tf_op jit(solution)/shard_map/ppermute | solution.py:189

commit v12 on v8

--- a/solution.py
+++ b/solution.py
@@ -188,7 +188,7 @@
     slots = pl.pallas_call(slots_kernel, out_shape=pltpu.VMEM((members * 2, stride), f32))(
         kept, handed
     )
-    pieces = exchange(slots, "rep")
+    pieces = lax.all_to_all(slots, "rep", split_axis=0, concat_axis=0, tiled=True)
     merged = pl.pallas_call(
         merge_kernel, out_shape=pltpu.VMEM((members // 2 * 5, stride), f32)
     )(kept, handed, near(pieces))

time: 78 us -> 78 us (level)
    all_to_all x3 -> x2, blocking collectives: 67.4 us -> 58.5 us  [exchange(): wide = lax.all_to_all(wide, axis, split_axis=0, concat_axis=0, tiled=True)]
    all_to_all x0 -> x1, blocking collectives: none -> 8.84 us  [local(): lax.all_to_all(slots, 'rep', split_axis=0, concat_axis=0, tiled=True)]
where the time goes in v12:
time: 78 us; the launch traced here: 76.6 us
  blocking collectives  67.4 us (86%)
  starting transfers between devices  3.96 us (5%)
  Pallas kernels  3.49 us (4%)
  waiting for transfers between devices  0.96 us (1%)
  between operations  0.8 us (1%)
    all_to_all x2, blocking collectives, exchange(): wide = lax.all_to_all(wide, axis, split_axis=0, concat_axis=0, tiled=True)  58.5 us
    all_to_all x1, blocking collectives, local(): lax.all_to_all(slots, 'rep', split_axis=0, concat_axis=0, tiled=True)  8.84 us
    ppermute x1, starting transfers between devices, local(): handed = near(lax.ppermute(handed, 'core', [(0, 1), (1, 0)]))  3.96 us
  transfers between devices with their start and end apart: 1, of which 1 were waited for; matrix products, arithmetic and copies ran while one was open for 0% of the time, Pallas kernels for 0%

profile of v12, /device:TPU:1, one launch (start us, length us, event | category | flops | bytes accessed | tf_op | source)
XLA Modules:
  0.0 76.6 jit_solution(14646749694629552122)
XLA Ops:
  0.6 0.0 copy-start.8
  0.6 0.0 copy-start.9
  0.7 1.2 %shard_map.158 = (f32[768,128]{1,0:T(8,128)S(1)}, f32[128,256]{1,0:T(8,128)S(1)}) custom-call(bf16[128,256]{1,0:T(8,128)(2,1)} %bitcast.18, bf16[128,256]{1,0:T(8,128)(2,1)} %bitcast.19, bf16[128,256]{1,0:T(8,128)(2,1)} %bitcast.20, f32[128,256]{1,0:T(8,128)} %filter_ref.1, f32[1,256]{1,0:T(1,128)} %bitcast.21), custom_call_target="tpu_custom_call" | custom-call | tf_op jit(solution)/shard_map/pallas_call | solution.py:177
  1.8 0.0 copy-start
  1.8 0.0 copy-start.1
  1.9 0.0 copy-start.2
  1.9 0.0 copy-start.3
  1.9 0.0 copy-start.4
  1.9 0.0 copy-start.5
  1.9 0.0 copy-start.6
  1.9 0.0 copy-start.7
  1.9 40.8 %all_to_all.21 = f32[128,1,768]{2,1,0:T(1,128)S(1)} all-to-all(f32[128,1,768]{2,1,0:T(1,128)S(1)} %bitcast.17), channel_id=1, replica_groups=mesh['rep'=4,'chip'=64,'core'=2] {'chip','core'}, dimensions={0} | all-to-all | bytes 786432 | tf_op jit(solution)/shard_map/all_to_all | solution.py:165
  42.8 0.0 copy-done.8
  42.8 0.0 copy-done.9
  42.8 0.0 copy-done
  42.8 0.0 copy-done.1
  42.8 0.0 copy-done.2
  42.8 0.0 copy-done.3
  42.8 0.0 copy-done.4
  42.8 0.0 copy-done.5
  42.8 0.0 copy-done.6
  42.8 0.0 copy-done.7
  42.8 1.6 %shard_map.159 = (f32[256,128]{1,0:T(8,128)S(1)}, f32[256,128]{1,0:T(8,128)S(1)}) custom-call(f32[768,128]{1,0:T(8,128)S(1)} %bitcast.12, f32[128,128]{1,0:T(8,128)S(1)} %copy-done.9, f32[128,128]{1,0:T(8,128)S(1)} %copy-done.8, bf16[256,128]{1,0:T(8,128)(2,1)S(1)} %copy-done.7, bf16[256,128]{1,0:T(8,128)(2,1)S(1)} %copy-done.6, ...), custom_call_target="tpu_custom_call" | custom-call | tf_op jit(solution)/shard_map/pallas_call | solution.py:183
  44.4 4.0 %collective-permute-start = (f32[256,128]{1,0:T(8,128)S(1)}, f32[256,128]{1,0:T(8,128)S(1)}, u32[]{:S(2)}, u32[]{:S(2)}) collective-permute-start(f32[256,128]{1,0:T(8,128)S(1)} %get-tuple-element.10), channel_id=1, source_target_pairs={{0,1},{1,0},{2,3},{3,2},{4,5},{5,4},{6,7},{7,6},{8,9},{9,8},{10,11... | collective-permute-start | bytes 393224 | tf_op jit(solution)/shard_map/ppermute | solution.py:186
  48.4 1.0 %collective-permute-done.handed_ref = f32[256,128]{1,0:T(8,128)S(1)} collective-permute-done((f32[256,128]{1,0:T(8,128)S(1)}, f32[256,128]{1,0:T(8,128)S(1)}, u32[]{:S(2)}, u32[]{:S(2)}) %collective-permute-start) | collective-permute-done | bytes 131104 | tf_op jit(solution)/shard_map/ppermute | solution.py:186
  49.3 8.8 %all_to_all.22 = f32[4,64,128]{2,1,0:T(8,128)S(1)} all-to-all(f32[4,64,128]{2,1,0:T(8,128)S(1)} %bitcast.16), channel_id=1, replica_groups=mesh['rep'=4,'chip'=64,'core'=2] {'rep'}, dimensions={0} | all-to-all | bytes 262144 | tf_op jit(solution)/shard_map/all_to_all | solution.py:191
  58.2 17.7 %all_to_all.23 = f32[64,1,640]{2,1,0:T(1,128)S(1)} all-to-all(f32[64,1,640]{2,1,0:T(1,128)S(1)} %bitcast.14), channel_id=1, replica_groups=mesh['rep'=4,'chip'=64,'core'=2] {'chip'}, dimensions={0} | all-to-all | bytes 327680 | tf_op jit(solution)/shard_map/all_to_all | solution.py:165
  75.9 0.7 shard_map.162
  (2 shorter events, 0.0 us)
Async XLA Ops:
  0.6 42.1 %copy-start.8 = (f32[128,128]{1,0:T(8,128)S(1)}, f32[128,128]{1,0:T(8,128)}, u32[]{:S(2)}) copy-start(f32[128,128]{1,0:T(8,128)} %constant.21.clone.sin_ref) | copy-start | bytes 196612
  0.6 42.1 %copy-start.9 = (f32[128,128]{1,0:T(8,128)S(1)}, f32[128,128]{1,0:T(8,128)}, u32[]{:S(2)}) copy-start(f32[128,128]{1,0:T(8,128)} %constant.20.clone.cos_ref) | copy-start | bytes 196612
  1.8 40.9 %copy-start = (bf16[256,256]{1,0:T(8,128)(2,1)S(1)}, bf16[256,256]{1,0:T(8,128)(2,1)}, u32[]{:S(2)}) copy-start(bf16[256,256]{1,0:T(8,128)(2,1)} %constant.27.clone.refs_5_) | copy-start | bytes 393220
  1.8 40.9 %copy-start.1 = (bf16[256,256]{1,0:T(8,128)(2,1)S(1)}, bf16[256,256]{1,0:T(8,128)(2,1)}, u32[]{:S(2)}) copy-start(bf16[256,256]{1,0:T(8,128)(2,1)} %constant.26.clone.refs_4_) | copy-start | bytes 393220
  1.9 40.9 %copy-start.2 = (bf16[256,256]{1,0:T(8,128)(2,1)S(1)}, bf16[256,256]{1,0:T(8,128)(2,1)}, u32[]{:S(2)}) copy-start(bf16[256,256]{1,0:T(8,128)(2,1)} %constant.25.clone.refs_3_) | copy-start | bytes 393220
  1.9 40.9 %copy-start.3 = (bf16[256,256]{1,0:T(8,128)(2,1)S(1)}, bf16[256,256]{1,0:T(8,128)(2,1)}, u32[]{:S(2)}) copy-start(bf16[256,256]{1,0:T(8,128)(2,1)} %constant.24.clone.refs_2_) | copy-start | bytes 393220
  1.9 40.9 %copy-start.4 = (bf16[128,256]{1,0:T(8,128)(2,1)S(1)}, bf16[128,256]{1,0:T(8,128)(2,1)}, u32[]{:S(2)}) copy-start(bf16[128,256]{1,0:T(8,128)(2,1)} %constant.29.clone.refs_7_) | copy-start | bytes 196612
  1.9 40.9 %copy-start.5 = (bf16[128,256]{1,0:T(8,128)(2,1)S(1)}, bf16[128,256]{1,0:T(8,128)(2,1)}, u32[]{:S(2)}) copy-start(bf16[128,256]{1,0:T(8,128)(2,1)} %constant.28.clone.refs_6_) | copy-start | bytes 196612
  1.9 40.9 %copy-start.6 = (bf16[256,128]{1,0:T(8,128)(2,1)S(1)}, bf16[256,128]{1,0:T(8,128)(2,1)}, u32[]{:S(2)}) copy-start(bf16[256,128]{1,0:T(8,128)(2,1)} %constant.23.clone.refs_1_) | copy-start | bytes 196612
  1.9 40.9 %copy-start.7 = (bf16[256,128]{1,0:T(8,128)(2,1)S(1)}, bf16[256,128]{1,0:T(8,128)(2,1)}, u32[]{:S(2)}) copy-start(bf16[256,128]{1,0:T(8,128)(2,1)} %constant.22.clone.refs_0_) | copy-start | bytes 196612
  44.4 4.9 %collective-permute-start = (f32[256,128]{1,0:T(8,128)S(1)}, f32[256,128]{1,0:T(8,128)S(1)}, u32[]{:S(2)}, u32[]{:S(2)}) collective-permute-start(f32[256,128]{1,0:T(8,128)S(1)} %get-tuple-element.10), channel_id=1, source_target_pairs={{0,1},{1,0},{2,3},{3,2},{4,5},{5,4},{6,7},{7,6},{8,9},{9,8},{10,11... | collective-permute-start | bytes 393224 | tf_op jit(solution)/shard_map/ppermute | solution.py:186

commit v13 on v8

--- a/solution.py
+++ b/solution.py
@@ -37,11 +37,12 @@
     first = np.concatenate([np.cos(outer), -np.sin(outer)], axis=0)
     second = np.block([[np.cos(inner), -np.sin(inner)], [np.sin(inner), np.cos(inner)]])
     scale = 2.0 / padded / math.sqrt(members * stride)
-    result = [np.asarray(np.cos(twist), np.float32), np.asarray(np.sin(twist), np.float32)]
+    result = [np.concatenate([np.cos(twist), np.sin(twist)], axis=0).astype(np.float32)]
     last = np.concatenate([first.T[0::2], first.T[1::2]], axis=0) * scale
     for table in (first, second, second.T, last):
         high = table.astype(jnp.bfloat16)
-        result += [high, (table - high.astype(np.float64)).astype(jnp.bfloat16)]
+        low = (table - high.astype(np.float64)).astype(jnp.bfloat16)
+        result.append(np.concatenate([high, low], axis=0))
     return result
 
 
@@ -100,17 +101,18 @@
     return product(last, halves(jnp.concatenate(columns, axis=1)))
 
 
-def pairs_of(refs):
-    return [(refs[at][...], refs[at + 1][...]) for at in range(0, len(refs), 2)]
-
-
-def spectra_kernel(signal_ref, cos_ref, sin_ref, *refs):
-    first, second, back, last = pairs_of(refs[:8])
-    kept_ref, handed_ref = refs[8:]
+def pair_of(ref):
+    rows = ref.shape[0] // 2
+    return ref[:rows, :], ref[rows:, :]
+
+
+def spectra_kernel(signal_ref, twist_ref, *refs):
+    first, second, back, last = [pair_of(ref) for ref in refs[:4]]
+    kept_ref, handed_ref = refs[4:]
     stride = signal_ref.shape[1]
     chips = signal_ref.shape[0] // 12
     even_core = lax.axis_index("core") == 0
-    cosine, sine = cos_ref[...], sin_ref[...]
+    cosine, sine = pair_of(twist_ref)
     parts = spectra(signal_ref, first, second, cosine, sine)
     for index, other in enumerate((2, 4)):
         products = [correlated(parts[part], parts[other + part]) for part in range(2)]

time: 78 us -> 77.9 us (level)
  no operation moved by 1% of the time
where the time goes in v13:
time: 77.9 us; the launch traced here: 76.5 us
  blocking collectives  67.4 us (87%)
  starting transfers between devices  3.95 us (5%)
  Pallas kernels  3.49 us (4%)
  waiting for transfers between devices  0.96 us (1%)
    all_to_all x3, blocking collectives, exchange(): wide = lax.all_to_all(wide, axis, split_axis=0, concat_axis=0, tiled=True)  67.4 us
    ppermute x1, starting transfers between devices, local(): handed = near(lax.ppermute(handed, 'core', [(0, 1), (1, 0)]))  3.95 us
  transfers between devices with their start and end apart: 1, of which 1 were waited for; matrix products, arithmetic and copies ran while one was open for 0% of the time, Pallas kernels for 0%

profile of v13, /device:TPU:1, one launch (start us, length us, event | category | flops | bytes accessed | tf_op | source)
XLA Modules:
  0.0 76.5 jit_solution(17571231199547212512)
XLA Ops:
  0.6 0.0 copy-start.4
  0.6 1.2 %shard_map.113 = (f32[768,128]{1,0:T(8,128)S(1)}, f32[128,256]{1,0:T(8,128)S(1)}) custom-call(bf16[128,256]{1,0:T(8,128)(2,1)} %bitcast.18, bf16[128,256]{1,0:T(8,128)(2,1)} %bitcast.19, bf16[128,256]{1,0:T(8,128)(2,1)} %bitcast.20, f32[128,256]{1,0:T(8,128)} %filter_ref.1, f32[1,256]{1,0:T(1,128)} %bitcast.21), custom_call_target="tpu_custom_call" | custom-call | tf_op jit(solution)/shard_map/pallas_call | solution.py:179
  1.8 0.0 copy-start
  1.8 0.0 copy-start.1
  1.8 0.0 copy-start.2
  1.9 0.0 copy-start.3
  1.9 40.8 %all_to_all.15 = f32[128,1,768]{2,1,0:T(1,128)S(1)} all-to-all(f32[128,1,768]{2,1,0:T(1,128)S(1)} %bitcast.17), channel_id=1, replica_groups=mesh['rep'=4,'chip'=64,'core'=2] {'chip','core'}, dimensions={0} | all-to-all | bytes 786432 | tf_op jit(solution)/shard_map/all_to_all | solution.py:167
  42.7 0.0 copy-done.4
  42.7 0.0 copy-done
  42.7 0.0 copy-done.1
  42.7 0.0 copy-done.2
  42.7 0.0 copy-done.3
  42.7 1.6 %shard_map.114 = (f32[256,128]{1,0:T(8,128)S(1)}, f32[256,128]{1,0:T(8,128)S(1)}) custom-call(f32[768,128]{1,0:T(8,128)S(1)} %bitcast.12, f32[256,128]{1,0:T(8,128)S(1)} %copy-done.4, bf16[512,128]{1,0:T(8,128)(2,1)S(1)} %copy-done.3, bf16[512,256]{1,0:T(8,128)(2,1)S(1)} %copy-done.1, bf16[512,256]{1,0:T(8,128)(2,1)S(1)} %copy-done, ...), custom_call_target="tpu_custom_call" | custom-call | tf_op jit(solution)/shard_map/pallas_call | solution.py:185
  44.3 3.9 %collective-permute-start = (f32[256,128]{1,0:T(8,128)S(1)}, f32[256,128]{1,0:T(8,128)S(1)}, u32[]{:S(2)}, u32[]{:S(2)}) collective-permute-start(f32[256,128]{1,0:T(8,128)S(1)} %get-tuple-element.10), channel_id=1, source_target_pairs={{0,1},{1,0},{2,3},{3,2},{4,5},{5,4},{6,7},{7,6},{8,9},{9,8},{10,11... | collective-permute-start | bytes 393224 | tf_op jit(solution)/shard_map/ppermute | solution.py:188
  48.2 1.0 %collective-permute-done.handed_ref = f32[256,128]{1,0:T(8,128)S(1)} collective-permute-done((f32[256,128]{1,0:T(8,128)S(1)}, f32[256,128]{1,0:T(8,128)S(1)}, u32[]{:S(2)}, u32[]{:S(2)}) %collective-permute-start) | collective-permute-done | bytes 131104 | tf_op jit(solution)/shard_map/ppermute | solution.py:188
  49.2 8.9 %all_to_all.16 = f32[4,1,8192]{2,1,0:T(1,128)S(1)} all-to-all(f32[4,1,8192]{2,1,0:T(1,128)S(1)} %bitcast.16), channel_id=1, replica_groups=mesh['rep'=4,'chip'=64,'core'=2] {'rep'}, dimensions={0} | all-to-all | bytes 262144 | tf_op jit(solution)/shard_map/all_to_all | solution.py:167
  58.1 17.7 %all_to_all.17 = f32[64,1,640]{2,1,0:T(1,128)S(1)} all-to-all(f32[64,1,640]{2,1,0:T(1,128)S(1)} %bitcast.14), channel_id=1, replica_groups=mesh['rep'=4,'chip'=64,'core'=2] {'chip'}, dimensions={0} | all-to-all | bytes 327680 | tf_op jit(solution)/shard_map/all_to_all | solution.py:167
  75.8 0.7 shard_map.117
  (2 shorter events, 0.0 us)
Async XLA Ops:
  0.6 42.1 %copy-start.4 = (f32[256,128]{1,0:T(8,128)S(1)}, f32[256,128]{1,0:T(8,128)}, u32[]{:S(2)}) copy-start(f32[256,128]{1,0:T(8,128)} %constant.10.clone.twist_ref) | copy-start | bytes 393220
  1.8 40.9 %copy-start = (bf16[512,256]{1,0:T(8,128)(2,1)S(1)}, bf16[512,256]{1,0:T(8,128)(2,1)}, u32[]{:S(2)}) copy-start(bf16[512,256]{1,0:T(8,128)(2,1)} %constant.13.clone.refs_2_) | copy-start | bytes 786436
  1.8 40.9 %copy-start.1 = (bf16[512,256]{1,0:T(8,128)(2,1)S(1)}, bf16[512,256]{1,0:T(8,128)(2,1)}, u32[]{:S(2)}) copy-start(bf16[512,256]{1,0:T(8,128)(2,1)} %constant.12.clone.refs_1_) | copy-start | bytes 786436
  1.8 40.9 %copy-start.2 = (bf16[256,256]{1,0:T(8,128)(2,1)S(1)}, bf16[256,256]{1,0:T(8,128)(2,1)}, u32[]{:S(2)}) copy-start(bf16[256,256]{1,0:T(8,128)(2,1)} %constant.14.clone.refs_3_) | copy-start | bytes 393220
  1.9 40.9 %copy-start.3 = (bf16[512,128]{1,0:T(8,128)(2,1)S(1)}, bf16[512,128]{1,0:T(8,128)(2,1)}, u32[]{:S(2)}) copy-start(bf16[512,128]{1,0:T(8,128)(2,1)} %constant.11.clone.refs_0_) | copy-start | bytes 393220
  44.3 4.9 %collective-permute-start = (f32[256,128]{1,0:T(8,128)S(1)}, f32[256,128]{1,0:T(8,128)S(1)}, u32[]{:S(2)}, u32[]{:S(2)}) collective-permute-start(f32[256,128]{1,0:T(8,128)S(1)} %get-tuple-element.10), channel_id=1, source_target_pairs={{0,1},{1,0},{2,3},{3,2},{4,5},{5,4},{6,7},{7,6},{8,9},{9,8},{10,11... | collective-permute-start | bytes 393224 | tf_op jit(solution)/shard_map/ppermute | solution.py:188

commit v14 on v13

--- a/solution.py
+++ b/solution.py
@@ -114,15 +114,18 @@
     even_core = lax.axis_index("core") == 0
     cosine, sine = pair_of(twist_ref)
     parts = spectra(signal_ref, first, second, cosine, sine)
+    last = [
+        jnp.where(even_core, half, jnp.concatenate([half[chips:], half[:chips]], axis=0))
+        for half in last
+    ]
     for index, other in enumerate((2, 4)):
         products = [correlated(parts[part], parts[other + part]) for part in range(2)]
         values = inverse(products, back, last, cosine, sine)
         for part in range(2):
-            even = values[:chips, part * stride : (part + 1) * stride]
-            odd = values[chips:, part * stride : (part + 1) * stride]
+            columns = slice(part * stride, (part + 1) * stride)
             rows = slice((2 * index + part) * chips, (2 * index + part + 1) * chips)
-            kept_ref[rows, :] = jnp.where(even_core, even, odd)
-            handed_ref[rows, :] = jnp.where(even_core, odd, even)
+            kept_ref[rows, :] = values[:chips, columns]
+            handed_ref[rows, :] = values[chips:, columns]
 
 
 def by_quarter(kept_ref, handed_ref, row, chips):

time: 77.9 us -> 77.9 us (level)
  no operation moved by 1% of the time
where the time goes in v14:
time: 77.9 us; the launch traced here: 76.5 us
  blocking collectives  67.4 us (87%)
  starting transfers between devices  3.95 us (5%)
  Pallas kernels  3.48 us (4%)
  waiting for transfers between devices  0.96 us (1%)
    all_to_all x3, blocking collectives, exchange(): wide = lax.all_to_all(wide, axis, split_axis=0, concat_axis=0, tiled=True)  67.4 us
    ppermute x1, starting transfers between devices, local(): handed = near(lax.ppermute(handed, 'core', [(0, 1), (1, 0)]))  3.95 us
  transfers between devices with their start and end apart: 1, of which 1 were waited for; matrix products, arithmetic and copies ran while one was open for 0% of the time, Pallas kernels for 0%

profile of v14, /device:TPU:1, one launch (start us, length us, event | category | flops | bytes accessed | tf_op | source)
XLA Modules:
  0.0 76.5 jit_solution(12361029884015876531)
XLA Ops:
  0.6 0.0 copy-start.4
  0.6 1.2 %shard_map.113 = (f32[768,128]{1,0:T(8,128)S(1)}, f32[128,256]{1,0:T(8,128)S(1)}) custom-call(bf16[128,256]{1,0:T(8,128)(2,1)} %bitcast.18, bf16[128,256]{1,0:T(8,128)(2,1)} %bitcast.19, bf16[128,256]{1,0:T(8,128)(2,1)} %bitcast.20, f32[128,256]{1,0:T(8,128)} %filter_ref.1, f32[1,256]{1,0:T(1,128)} %bitcast.21), custom_call_target="tpu_custom_call" | custom-call | tf_op jit(solution)/shard_map/pallas_call | solution.py:182
  1.8 0.0 copy-start
  1.8 0.0 copy-start.1
  1.8 0.0 copy-start.2
  1.9 0.0 copy-start.3
  1.9 40.8 %all_to_all.15 = f32[128,1,768]{2,1,0:T(1,128)S(1)} all-to-all(f32[128,1,768]{2,1,0:T(1,128)S(1)} %bitcast.17), channel_id=1, replica_groups=mesh['rep'=4,'chip'=64,'core'=2] {'chip','core'}, dimensions={0} | all-to-all | bytes 786432 | tf_op jit(solution)/shard_map/all_to_all | solution.py:170
  42.7 0.0 copy-done.4
  42.7 0.0 copy-done
  42.7 0.0 copy-done.1
  42.7 0.0 copy-done.2
  42.7 0.0 copy-done.3
  42.7 1.5 %shard_map.114 = (f32[256,128]{1,0:T(8,128)S(1)}, f32[256,128]{1,0:T(8,128)S(1)}) custom-call(f32[768,128]{1,0:T(8,128)S(1)} %bitcast.12, f32[256,128]{1,0:T(8,128)S(1)} %copy-done.4, bf16[512,128]{1,0:T(8,128)(2,1)S(1)} %copy-done.3, bf16[512,256]{1,0:T(8,128)(2,1)S(1)} %copy-done.1, bf16[512,256]{1,0:T(8,128)(2,1)S(1)} %copy-done, ...), custom_call_target="tpu_custom_call" | custom-call | tf_op jit(solution)/shard_map/pallas_call | solution.py:188
  44.3 3.9 %collective-permute-start = (f32[256,128]{1,0:T(8,128)S(1)}, f32[256,128]{1,0:T(8,128)S(1)}, u32[]{:S(2)}, u32[]{:S(2)}) collective-permute-start(f32[256,128]{1,0:T(8,128)S(1)} %get-tuple-element.10), channel_id=1, source_target_pairs={{0,1},{1,0},{2,3},{3,2},{4,5},{5,4},{6,7},{7,6},{8,9},{9,8},{10,11... | collective-permute-start | bytes 393224 | tf_op jit(solution)/shard_map/ppermute | solution.py:191
  48.2 1.0 %collective-permute-done.handed_ref = f32[256,128]{1,0:T(8,128)S(1)} collective-permute-done((f32[256,128]{1,0:T(8,128)S(1)}, f32[256,128]{1,0:T(8,128)S(1)}, u32[]{:S(2)}, u32[]{:S(2)}) %collective-permute-start) | collective-permute-done | bytes 131104 | tf_op jit(solution)/shard_map/ppermute | solution.py:191
  49.2 8.9 %all_to_all.16 = f32[4,1,8192]{2,1,0:T(1,128)S(1)} all-to-all(f32[4,1,8192]{2,1,0:T(1,128)S(1)} %bitcast.16), channel_id=1, replica_groups=mesh['rep'=4,'chip'=64,'core'=2] {'rep'}, dimensions={0} | all-to-all | bytes 262144 | tf_op jit(solution)/shard_map/all_to_all | solution.py:170
  58.1 17.7 %all_to_all.17 = f32[64,1,640]{2,1,0:T(1,128)S(1)} all-to-all(f32[64,1,640]{2,1,0:T(1,128)S(1)} %bitcast.14), channel_id=1, replica_groups=mesh['rep'=4,'chip'=64,'core'=2] {'chip'}, dimensions={0} | all-to-all | bytes 327680 | tf_op jit(solution)/shard_map/all_to_all | solution.py:170
  75.8 0.7 shard_map.117
  (2 shorter events, 0.0 us)
Async XLA Ops:
  0.6 42.1 %copy-start.4 = (f32[256,128]{1,0:T(8,128)S(1)}, f32[256,128]{1,0:T(8,128)}, u32[]{:S(2)}) copy-start(f32[256,128]{1,0:T(8,128)} %constant.10.clone.twist_ref) | copy-start | bytes 393220
  1.8 40.9 %copy-start = (bf16[512,256]{1,0:T(8,128)(2,1)S(1)}, bf16[512,256]{1,0:T(8,128)(2,1)}, u32[]{:S(2)}) copy-start(bf16[512,256]{1,0:T(8,128)(2,1)} %constant.13.clone.refs_2_) | copy-start | bytes 786436
  1.8 40.9 %copy-start.1 = (bf16[512,256]{1,0:T(8,128)(2,1)S(1)}, bf16[512,256]{1,0:T(8,128)(2,1)}, u32[]{:S(2)}) copy-start(bf16[512,256]{1,0:T(8,128)(2,1)} %constant.12.clone.refs_1_) | copy-start | bytes 786436
  1.8 40.9 %copy-start.2 = (bf16[256,256]{1,0:T(8,128)(2,1)S(1)}, bf16[256,256]{1,0:T(8,128)(2,1)}, u32[]{:S(2)}) copy-start(bf16[256,256]{1,0:T(8,128)(2,1)} %constant.14.clone.refs_3_) | copy-start | bytes 393220
  1.9 40.9 %copy-start.3 = (bf16[512,128]{1,0:T(8,128)(2,1)S(1)}, bf16[512,128]{1,0:T(8,128)(2,1)}, u32[]{:S(2)}) copy-start(bf16[512,128]{1,0:T(8,128)(2,1)} %constant.11.clone.refs_0_) | copy-start | bytes 393220
  44.3 4.9 %collective-permute-start = (f32[256,128]{1,0:T(8,128)S(1)}, f32[256,128]{1,0:T(8,128)S(1)}, u32[]{:S(2)}, u32[]{:S(2)}) collective-permute-start(f32[256,128]{1,0:T(8,128)S(1)} %get-tuple-element.10), channel_id=1, source_target_pairs={{0,1},{1,0},{2,3},{3,2},{4,5},{5,4},{6,7},{7,6},{8,9},{9,8},{10,11... | collective-permute-start | bytes 393224 | tf_op jit(solution)/shard_map/ppermute | solution.py:191
